TPU v7x, 256 devices: a whole 4x4x8 slice. The times are simulated.
256 devices in a mesh: pipe: 4 (over y_hi, core), expert: 16 (over z, y_lo), dp: 4 (over x).
Axes of the slice: x: 4, y: 4 (y_hi: 2, y_lo: 2; y = y_hi * 2 + y_lo), z: 8, core: 2. Of those that a mesh axis runs over, the one named last changes fastest.
Arguments:
- x_fwd: bfloat16 [4, 2048, 3584], P('pipe', 'expert'), may hold values from -6 to 6
- ids_fwd: int32 [4, 2048, 2], P('pipe', 'expert'), may hold values from 0 to 15, all different within a row; in each aligned block of 128 rows (0 to 127, 128 to 255, ..., all dimensions but the last counted through in order) at most 24 rows name the same one
- gates_fwd: float32 [4, 2048, 2], P('pipe', 'expert'), may hold values from 0.1 to 0.6
- x_bwd: bfloat16 [4, 2048, 3584], P('pipe', 'expert'), may hold values from -6 to 6
- ids_bwd: int32 [4, 2048, 2], P('pipe', 'expert'), may hold values from 0 to 15, all different within a row; in each aligned block of 128 rows (0 to 127, 128 to 255, ..., all dimensions but the last counted through in order) at most 24 rows name the same one
- gates_bwd: float32 [4, 2048, 2], P('pipe', 'expert'), may hold values from 0.1 to 0.6
- grad_in: bfloat16 [4, 2048, 3584], P('pipe', 'expert', 'dp'), may hold values from -6 to 6
- w_gate: bfloat16 [4, 16, 3584, 2048], P('pipe', 'expert', None, 'dp'), may hold values from -0.09375 to 0.09375
- w_up: bfloat16 [4, 16, 3584, 2048], P('pipe', 'expert', None, 'dp'), may hold values from -0.09375 to 0.09375
- w_down: bfloat16 [4, 16, 2048, 3584], P('pipe', 'expert', 'dp'), may hold values from -0.125 to 0.125
Outputs:
- sent_forward: bfloat16 [4, 2048, 3584], P('pipe', 'expert', 'dp')
- sent_backward: bfloat16 [4, 2048, 3584], P('pipe', 'expert', 'dp')
Inputs may be any that keep to these rules, and one draw needn't show every extreme that they name: `ids_fwd`: each row names 2 different experts. Within the rows of one index of expert at one section (aligned blocks of 128 rows) no expert is named by more than 24 rows, a bound that some block reaches. `ids_bwd`: same law as ids_fwd.
All inputs are finite; a program needn't handle non-finite values.
Results may differ from a plain program's by a relative error of at most 0.0075.
Values may be sent and summed in bfloat16 or wider, within the bound.
No kernel may reach another device: no remote copies, remote signals or barrier semaphores. Data moves between devices by JAX's collectives and lax.ppermute only.
A program may use at most 128 MiB of HBM per device.

v0:
```python
import jax
import jax.numpy as jnp
from jax import lax
from jax.sharding import PartitionSpec as P


def shifted(array, axis, by):
    count = lax.axis_size(axis)
    return lax.ppermute(array, axis, [(i, (i + by) % count) for i in range(count)])


def route_slots(route_ids, experts, capacity):
    flat_ids = route_ids.reshape(-1)
    onehot = (flat_ids[:, None] == jnp.arange(experts, dtype=jnp.int32)[None, :]).astype(jnp.int32)
    position = jnp.sum((jnp.cumsum(onehot, axis=0) - 1) * onehot, axis=1)
    target = flat_ids * capacity + position
    owner = (
        jnp.full((experts * capacity,), -1, jnp.int32)
        .at[target]
        .set(jnp.arange(flat_ids.shape[0], dtype=jnp.int32))
    )
    return (target, owner)


def pack_rows(source, owner, topk, experts, capacity):
    picked = jnp.take(source, jnp.maximum(owner, 0) // topk, axis=0)
    filled = jnp.where((owner >= 0)[:, None], picked, jnp.zeros_like(picked))
    return filled.reshape(experts, capacity, source.shape[1])


def local(x_fwd, ids_fwd, gates_fwd, x_bwd, ids_bwd, gates_bwd, grad_in, w_gate, w_up, w_down):
    experts = lax.axis_size("expert")
    groups = lax.axis_size("dp")
    dp_rank = lax.axis_index("dp")
    rows_dev = x_fwd.shape[1]
    topk = ids_fwd.shape[2]
    capacity = rows_dev * topk * 3 // (2 * experts)
    feature_width = x_fwd.shape[2]
    quarter = feature_width // groups
    gate_mat = w_gate[0, 0]
    up_mat = w_up[0, 0]
    down_mat = w_down[0, 0]
    fwd_rows = x_fwd[0]
    fwd_target, fwd_owner = route_slots(ids_fwd[0], experts, capacity)
    fwd_own = lax.dynamic_slice_in_dim(fwd_rows, dp_rank * quarter, quarter, 1)
    fwd_send = pack_rows(fwd_rows, fwd_owner, topk, experts, capacity)
    received = lax.all_to_all(fwd_send, "expert", split_axis=0, concat_axis=0, tiled=True)
    items = received.shape[1]
    flat_rows = received.reshape(-1, feature_width)
    gate_pre = jnp.dot(flat_rows, gate_mat, preferred_element_type=jnp.float32)
    up_pre = jnp.dot(flat_rows, up_mat, preferred_element_type=jnp.float32)
    hidden = (jax.nn.silu(gate_pre) * up_pre).astype(jnp.bfloat16)
    partial_out = jnp.dot(hidden, down_mat, preferred_element_type=jnp.float32)
    summed = lax.psum_scatter(
        partial_out.astype(jnp.bfloat16), "dp", scatter_dimension=1, tiled=True
    )
    fwd_back = lax.all_to_all(
        summed.reshape(experts, items, quarter), "expert", split_axis=0, concat_axis=0, tiled=True
    )
    fwd_copies = jnp.take(fwd_back.reshape(-1, quarter), fwd_target, axis=0).astype(jnp.float32)
    fwd_copies = fwd_copies.reshape(rows_dev, topk, quarter) * gates_fwd[0][:, :, None]
    layer_out = (fwd_own.astype(jnp.float32) + jnp.sum(fwd_copies, axis=1)).astype(jnp.bfloat16)
    bwd_rows = x_bwd[0]
    grad_own = grad_in[0]
    bwd_target, bwd_owner = route_slots(ids_bwd[0], experts, capacity)
    gate_flat = gates_bwd[0].reshape(-1)
    owner_gate = jnp.where(bwd_owner >= 0, jnp.take(gate_flat, jnp.maximum(bwd_owner, 0)), 0.0)
    grad_rows = lax.all_gather(grad_own, "dp", axis=1, tiled=True)
    bwd_send = pack_rows(bwd_rows, bwd_owner, topk, experts, capacity)
    grad_packed = pack_rows(grad_rows, bwd_owner, topk, experts, capacity)
    scaled_send = (
        grad_packed.astype(jnp.float32) * owner_gate.reshape(experts, capacity, 1)
    ).astype(jnp.bfloat16)
    inputs_in = lax.all_to_all(bwd_send, "expert", split_axis=0, concat_axis=0, tiled=True)
    scaled_in = lax.all_to_all(scaled_send, "expert", split_axis=0, concat_axis=0, tiled=True)
    items = inputs_in.shape[1]
    flat_rows = inputs_in.reshape(-1, feature_width)
    flat_scaled = scaled_in.reshape(-1, feature_width)
    gate_pre = jnp.dot(flat_rows, gate_mat, preferred_element_type=jnp.float32)
    up_pre = jnp.dot(flat_rows, up_mat, preferred_element_type=jnp.float32)
    squash = jax.nn.sigmoid(gate_pre)
    back_hidden = jnp.dot(flat_scaled, down_mat.T, preferred_element_type=jnp.float32)
    d_gate = (back_hidden * up_pre * squash * (1.0 + gate_pre * (1.0 - squash))).astype(
        jnp.bfloat16
    )
    d_up = (back_hidden * gate_pre * squash).astype(jnp.bfloat16)
    partial_grad = jnp.dot(d_gate, gate_mat.T, preferred_element_type=jnp.float32)
    partial_grad = partial_grad + jnp.dot(d_up, up_mat.T, preferred_element_type=jnp.float32)
    summed = lax.psum_scatter(
        partial_grad.astype(jnp.bfloat16), "dp", scatter_dimension=1, tiled=True
    )
    bwd_back = lax.all_to_all(
        summed.reshape(experts, items, quarter), "expert", split_axis=0, concat_axis=0, tiled=True
    )
    bwd_copies = jnp.take(bwd_back.reshape(-1, quarter), bwd_target, axis=0).astype(jnp.float32)
    bwd_copies = bwd_copies.reshape(rows_dev, topk, quarter)
    layer_grad = (grad_own.astype(jnp.float32) + jnp.sum(bwd_copies, axis=1)).astype(jnp.bfloat16)
    sent_forward = shifted(layer_out[None], "pipe", 1)
    sent_backward = shifted(layer_grad[None], "pipe", -1)
    return (sent_forward, sent_backward)


def solution(mesh):
    in_specs = (
        P("pipe", "expert", None),
        P("pipe", "expert", None),
        P("pipe", "expert", None),
        P("pipe", "expert", None),
        P("pipe", "expert", None),
        P("pipe", "expert", None),
        P("pipe", "expert", "dp"),
        P("pipe", "expert", None, "dp"),
        P("pipe", "expert", None, "dp"),
        P("pipe", "expert", "dp", None),
    )
    out_specs = (P("pipe", "expert", "dp"), P("pipe", "expert", "dp"))
    return jax.shard_map(local, mesh=mesh, in_specs=in_specs, out_specs=out_specs, check_vma=False)
```

profile of v0, /device:TPU:1, one launch (start us, length us, event | category | flops | bytes accessed | tf_op | source)
XLA Modules:
  0.0 352.8 jit_solution(13127115962614669711)
XLA Ops:
  7.2 0.9 copy.28
  8.4 0.7 broadcast_multiply_fusion
  9.1 0.6 reduce-window.16
  10.2 1.4 scatter_custom_fusion.1
  11.7 0.8 copy.32
  12.6 2.8 gather_fusion
  15.4 13.6 %all-gather = bf16[1,128,3584]{2,1,0:T(8,128)(2,1)S(1)} all-gather(bf16[1,128,896]{2,1,0:T(8,128)(2,1)S(1)} %copy-done.4), channel_id=2, replica_groups=mesh['pipe'=4,'expert'=16,'dp'=4] {'dp'}, dimensions={2}, use_global_device_ids=true | all-gather | bytes 1146880 | tf_op jit(solution)/shard_map/all_gather | solution.py:68
  29.1 3.9 %gather_fusion.3 = bf16[384,3584]{1,0:T(8,128)(2,1)} fusion(bf16[128,3584]{1,0:T(8,128)(2,1)S(1)} %bitcast.102, s32[1024]{0:T(1024)S(1)} %pad_clamp_fusion.2), kind=kCustom, calls=%fused_computation.2.clone | custom fusion | bytes 5506560 | tf_op jit(solution)/shard_map/jit(_take)/gather | solution.py:26
  32.9 3.9 %gather_fusion.4 = bf16[384,3584]{1,0:T(8,128)(2,1)} fusion(bf16[128,3584]{1,0:T(8,128)(2,1)S(1)} %bitcast.101, s32[1024]{0:T(1024)S(1)} %pad_clamp_fusion.2), kind=kCustom, calls=%fused_computation.3.clone | custom fusion | bytes 5506560 | tf_op jit(solution)/shard_map/jit(_take)/gather | solution.py:26
  36.9 4.1 %select_select_fusion = (bf16[384,3584]{1,0:T(8,128)(2,1)}, bf16[384,3584]{1,0:T(8,128)(2,1)S(1)}) fusion(bf16[384,3584]{1,0:T(8,128)(2,1)} %gather_fusion.4, pred[384]{0:T(512)(128)(4,1)S(1)} %get-tuple-element.8, pred[384]{0:T(512)(128)(4,1)S(1)} %get-tuple-element.7, bf16[384,3584]{1,0:T(8,128)(2,1)} %gather_fusion.3), kind=kLoop, calls=%fused_computation.27 | loop fusion | flops 5505024 | bytes 11010816 | tf_op jit(solution)/shard_map/jit(_where)/select_n | solution.py:27
  41.0 0.8 fusion.1
  41.8 71.6 %all_to_all.25 = bf16[16,24,3584]{2,1,0:T(8,128)(2,1)} all-to-all(bf16[16,24,3584]{2,1,0:T(8,128)(2,1)S(1)} %fusion.1), channel_id=1, replica_groups=mesh['pipe'=4,'expert'=16,'dp'=4] {'expert'}, dimensions={0} | all-to-all | bytes 5505024 | tf_op jit(solution)/shard_map/all_to_all | solution.py:75
  113.3 4.6 %all-to-all-start.3 = ((bf16[16,24,3584]{2,1,0:T(8,128)(2,1)}), bf16[16,24,3584]{2,1,0:T(8,128)(2,1)}, u32[]{:S(2)}, u32[]{:S(2)}) async-start(bf16[16,24,3584]{2,1,0:T(8,128)(2,1)} %bitcast.106), calls=%async_computation.3 | async-start | bytes 5505024 | tf_op jit(solution)/shard_map/all_to_all | solution.py:74
  118.4 0.6 reduce-window.14
  119.0 0.2 slice_reduce_fusion.1
  119.6 1.4 scatter_custom_fusion
  121.0 3.9 %gather_fusion.1 = bf16[384,3584]{1,0:T(8,128)(2,1)} fusion(bf16[128,3584]{1,0:T(8,128)(2,1)S(1)} %bitcast.103, s32[1024]{0:T(1024)S(1)} %pad_clamp_fusion.4), kind=kCustom, calls=%fused_computation.clone | custom fusion | bytes 5506560 | tf_op jit(solution)/shard_map/jit(_take)/gather | solution.py:26
  125.0 4.0 %select_select_fusion.2 = bf16[384,3584]{1,0:T(8,128)(2,1)} fusion(bf16[384,3584]{1,0:T(8,128)(2,1)} %gather_fusion.1, pred[384]{0:T(512)(128)(4,1)S(1)} %get-tuple-element.12, pred[384]{0:T(512)(128)(4,1)S(1)} %get-tuple-element.14), kind=kLoop, calls=%fused_computation.29 | loop fusion | flops 2752512 | bytes 5505792 | tf_op jit(solution)/shard_map/jit(_where)/select_n | solution.py:27
  128.9 3.6 %fusion.2 = f32[384,512]{1,0:T(8,128)S(1)} fusion(bf16[384,3584]{1,0:T(8,128)(2,1)S(1)} %bitcast.111, bf16[1,1,512,3584]{3,2,1,0:T(8,128)(2,1)} %param.23), kind=kOutput, calls=%fused_computation.13 | convolution fusion | flops 1409286144 | bytes 7208960 | tf_op jit(solution)/shard_map/dot_general | solution.py:82
  132.6 47.2 %all-to-all-done.3 = bf16[16,24,3584]{2,1,0:T(8,128)(2,1)} async-done(((bf16[16,24,3584]{2,1,0:T(8,128)(2,1)}), bf16[16,24,3584]{2,1,0:T(8,128)(2,1)}, u32[]{:S(2)}, u32[]{:S(2)}) %all-to-all-start.3) | async-done | bytes 2752544 | tf_op jit(solution)/shard_map/all_to_all | solution.py:74
  179.8 5.7 %all-to-all-start = ((bf16[16,24,3584]{2,1,0:T(8,128)(2,1)}), bf16[16,24,3584]{2,1,0:T(8,128)(2,1)}, u32[]{:S(2)}, u32[]{:S(2)}) async-start(bf16[16,24,3584]{2,1,0:T(8,128)(2,1)} %bitcast.107), calls=%async_computation | async-start | bytes 5505024 | tf_op jit(solution)/shard_map/all_to_all | solution.py:47
  185.5 0.2 reduce-scatter.9.cloned.1.call-start
  185.8 4.4 %fusion.12 = f32[384,512]{1,0:T(8,128)S(1)} fusion(bf16[384,3584]{1,0:T(8,128)(2,1)} %bitcast.21, bf16[1,1,3584,512]{3,2,1,0:T(8,128)(2,1)} %param.21), kind=kOutput, calls=%fused_computation.23 | convolution fusion | flops 1409286144 | bytes 7208960 | tf_op jit(solution)/shard_map/dot_general | solution.py:79
  190.2 9.5 %fusion.10 = f32[384,3584]{1,0:T(8,128)} fusion(bf16[1,1,3584,512]{3,2,1,0:T(8,128)(2,1)} %param.21, f32[384,512]{1,0:T(8,128)S(1)} %fusion.2, bf16[384,3584]{1,0:T(8,128)(2,1)} %bitcast.21, bf16[1,1,3584,512]{3,2,1,0:T(8,128)(2,1)} %param.22, f32[384,512]{1,0:T(8,128)S(1)} %fusion.12), kind=kOutput, calls=%fused_computation.21 | convolution fusion | flops 2820538368 | bytes 17170432 | tf_op jit(solution)/shard_map/dot_general | solution.py:87
  199.8 6.9 %fusion = bf16[384,3584]{1,0:T(8,128)(2,1)} fusion(f32[384,3584]{1,0:T(8,128)} %fusion.10, bf16[1,1,3584,512]{3,2,1,0:T(8,128)(2,1)} %param.22, f32[384,512]{1,0:T(8,128)S(1)} %fusion.2, f32[384,512]{1,0:T(8,128)S(1)} %fusion.12), kind=kOutput, calls=%fused_computation.9 | convolution fusion | flops 1413218304 | bytes 13500416 | tf_op jit(solution)/shard_map/dot_general | solution.py:88
  206.7 4.5 %copy.35 = bf16[384,3584]{0,1:T(8,128)(2,1)} copy(bf16[384,3584]{1,0:T(8,128)(2,1)} %fusion) | data formatting | bytes 5505024
  211.3 37.0 %all-to-all-done = bf16[16,24,3584]{2,1,0:T(8,128)(2,1)} async-done(((bf16[16,24,3584]{2,1,0:T(8,128)(2,1)}), bf16[16,24,3584]{2,1,0:T(8,128)(2,1)}, u32[]{:S(2)}, u32[]{:S(2)}) %all-to-all-start) | async-done | bytes 2752544 | tf_op jit(solution)/shard_map/all_to_all | solution.py:47
  248.3 4.5 %fusion.14 = f32[384,512]{1,0:T(8,128)S(1)} fusion(bf16[384,3584]{1,0:T(8,128)(2,1)} %bitcast.5, bf16[1,1,3584,512]{3,2,1,0:T(8,128)(2,1)} %param.21), kind=kOutput, calls=%fused_computation.25 | convolution fusion | flops 1409286144 | bytes 7208960 | tf_op jit(solution)/shard_map/dot_general | solution.py:50
  252.8 8.7 %convolution_convert_fusion = bf16[384,3584]{1,0:T(8,128)(2,1)} fusion(bf16[1,1,512,3584]{3,2,1,0:T(8,128)(2,1)} %param.23, bf16[384,3584]{1,0:T(8,128)(2,1)} %bitcast.5, bf16[1,1,3584,512]{3,2,1,0:T(8,128)(2,1)} %param.22, f32[384,512]{1,0:T(8,128)S(1)} %fusion.14), kind=kOutput, calls=%fused_computation.10 | convolution fusion | flops 2821128192 | bytes 13631488 | tf_op jit(solution)/shard_map/dot_general | solution.py:53
  261.5 4.5 %copy.33 = bf16[384,3584]{0,1:T(8,128)(2,1)} copy(bf16[384,3584]{1,0:T(8,128)(2,1)} %convolution_convert_fusion) | data formatting | bytes 5505024
  266.1 2.2 copy.36
  268.3 5.5 %all-to-all-start.4 = ((bf16[16,24,896]{2,1,0:T(8,128)(2,1)}), bf16[16,24,896]{2,1,0:T(8,128)(2,1)S(1)}, u32[]{:S(2)}, u32[]{:S(2)}) async-start(bf16[16,24,896]{2,1,0:T(8,128)(2,1)} %bitcast.22), calls=%async_computation.4 | async-start | bytes 1376256 | tf_op jit(solution)/shard_map/all_to_all | solution.py:92
  273.8 28.3 %reduce-scatter.7.cloned.1.call-done = bf16[896,384]{1,0:T(8,128)(2,1)} async-done(((bf16[3584,384]{1,0:T(8,128)(2,1)}), bf16[896,384]{1,0:T(8,128)(2,1)}) %reduce-scatter.7.cloned.1.call-update) | async-done | bytes 688144
  302.1 2.2 copy.34
  304.3 7.8 %all-to-all-start.1 = ((bf16[16,24,896]{2,1,0:T(8,128)(2,1)}), bf16[16,24,896]{2,1,0:T(8,128)(2,1)S(1)}, u32[]{:S(2)}, u32[]{:S(2)}) async-start(bf16[16,24,896]{2,1,0:T(8,128)(2,1)} %bitcast.9), calls=%async_computation.1 | async-start | bytes 1376256 | tf_op jit(solution)/shard_map/all_to_all | solution.py:57
  312.3 1.2 gather_fusion.5
  313.6 1.5 reshape.182
  315.1 2.3 reduce_sum.50
  317.4 0.7 fusion.41
  318.1 0.9 collective-permute-start.1
  319.0 12.0 %all-to-all-done.1 = bf16[16,24,896]{2,1,0:T(8,128)(2,1)S(1)} async-done(((bf16[16,24,896]{2,1,0:T(8,128)(2,1)}), bf16[16,24,896]{2,1,0:T(8,128)(2,1)S(1)}, u32[]{:S(2)}, u32[]{:S(2)}) %all-to-all-start.1) | async-done | bytes 688160 | tf_op jit(solution)/shard_map/all_to_all | solution.py:57
  331.0 1.2 gather_fusion.2
  332.3 1.5 reshape.179
  333.8 2.4 multiply_reduce_fusion
  336.2 5.4 %collective-permute-start = (bf16[1,128,896]{2,1,0:T(8,128)(2,1)S(1)}, bf16[1,128,896]{2,1,0:T(8,128)(2,1)S(1)}, u32[]{:S(2)}, u32[]{:S(2)}) collective-permute-start(bf16[1,128,896]{2,1,0:T(8,128)(2,1)S(1)} %fusion.42), channel_id=1, source_target_pairs={{0,64},{64,128},{128,192},{192,0},{1,65},{65,129},{129,193},{193,1... | collective-permute-start | bytes 688136 | tf_op jit(solution)/shard_map/ppermute | solution.py:9
  341.6 3.0 collective-permute-done
  344.6 0.7 copy.43
  345.2 0.7 copy.44
  (60 shorter events, 2.5 us)
Async XLA Ops:
  7.2 25.8 %copy-start = (bf16[1,128,3584]{2,1,0:T(8,128)(2,1)S(1)}, bf16[1,128,3584]{2,1,0:T(8,128)(2,1)}, u32[]{:S(2)}) copy-start(bf16[1,128,3584]{2,1,0:T(8,128)(2,1)} %param.17) | copy-start | bytes 2752516
  7.2 8.3 %copy-start.4 = (bf16[1,128,896]{2,1,0:T(8,128)(2,1)S(1)}, bf16[1,128,896]{2,1,0:T(8,128)(2,1)}, u32[]{:S(2)}) copy-start(bf16[1,128,896]{2,1,0:T(8,128)(2,1)} %param.20) | copy-start | bytes 688132
  113.3 4.6 %copy-start.5 = (s32[1,128,2]{1,2,0:T(2,128)S(1)}, s32[1,128,2]{1,2,0:T(2,128)}, u32[]{:S(2)}) copy-start(s32[1,128,2]{1,2,0:T(2,128)} %param.15) | copy-start | bytes 3076
  113.3 7.7 %copy-start.2 = (bf16[1,128,3584]{2,1,0:T(8,128)(2,1)S(1)}, bf16[1,128,3584]{2,1,0:T(8,128)(2,1)}, u32[]{:S(2)}) copy-start(bf16[1,128,3584]{2,1,0:T(8,128)(2,1)} %param.14) | copy-start | bytes 2752516
  113.3 66.5 %all-to-all-start.3 = ((bf16[16,24,3584]{2,1,0:T(8,128)(2,1)}), bf16[16,24,3584]{2,1,0:T(8,128)(2,1)}, u32[]{:S(2)}, u32[]{:S(2)}) async-start(bf16[16,24,3584]{2,1,0:T(8,128)(2,1)} %bitcast.106), calls=%async_computation.3 | async-start | bytes 5505024 | tf_op jit(solution)/shard_map/all_to_all | solution.py:74
  125.0 4.0 %copy-start.3 = (bf16[16,24,3584]{2,1,0:T(8,128)(2,1)S(1)}, bf16[16,24,3584]{2,1,0:T(8,128)(2,1)}, u32[]{:S(2)}) copy-start(bf16[16,24,3584]{2,1,0:T(8,128)(2,1)} %all_to_all.25) | copy-start | bytes 8257540
  179.8 68.5 %all-to-all-start = ((bf16[16,24,3584]{2,1,0:T(8,128)(2,1)}), bf16[16,24,3584]{2,1,0:T(8,128)(2,1)}, u32[]{:S(2)}, u32[]{:S(2)}) async-start(bf16[16,24,3584]{2,1,0:T(8,128)(2,1)} %bitcast.107), calls=%async_computation | async-start | bytes 5505024 | tf_op jit(solution)/shard_map/all_to_all | solution.py:47
  185.5 80.5 %reduce-scatter.9.cloned.1.call-start = ((), (), s32[]{:S(2)}) async-start(), calls=%async_computation.8 | async-start | bytes 3440640
  211.2 90.8 %reduce-scatter.7.cloned.1.call-start = ((), (), s32[]{:S(2)}) async-start(), calls=%async_computation.7 | async-start | bytes 3440640
  266.1 46.0 %copy-start.6 = (f32[1,128,2]{1,2,0:T(2,128)S(1)}, f32[1,128,2]{1,2,0:T(2,128)}, u32[]{:S(2)}) copy-start(f32[1,128,2]{1,2,0:T(2,128)} %param.16) | copy-start | bytes 3076
  268.3 36.0 %all-to-all-start.4 = ((bf16[16,24,896]{2,1,0:T(8,128)(2,1)}), bf16[16,24,896]{2,1,0:T(8,128)(2,1)S(1)}, u32[]{:S(2)}, u32[]{:S(2)}) async-start(bf16[16,24,896]{2,1,0:T(8,128)(2,1)} %bitcast.22), calls=%async_computation.4 | async-start | bytes 1376256 | tf_op jit(solution)/shard_map/all_to_all | solution.py:92
  304.3 26.6 %all-to-all-start.1 = ((bf16[16,24,896]{2,1,0:T(8,128)(2,1)}), bf16[16,24,896]{2,1,0:T(8,128)(2,1)S(1)}, u32[]{:S(2)}, u32[]{:S(2)}) async-start(bf16[16,24,896]{2,1,0:T(8,128)(2,1)} %bitcast.9), calls=%async_computation.1 | async-start | bytes 1376256 | tf_op jit(solution)/shard_map/all_to_all | solution.py:57
  318.1 23.5 %collective-permute-start.1 = (bf16[1,128,896]{2,1,0:T(8,128)(2,1)}, bf16[1,128,896]{2,1,0:T(8,128)(2,1)S(1)}, u32[]{:S(2)}, u32[]{:S(2)}) collective-permute-start(bf16[1,128,896]{2,1,0:T(8,128)(2,1)} %fusion.41), channel_id=1, source_target_pairs={{0,192},{64,0},{128,64},{192,128},{1,193},{65,1},{129,65},{193,129... | collective-permute-start | bytes 688136 | tf_op jit(solution)/shard_map/ppermute | solution.py:9
  332.2 13.8 %copy-start.1 = (bf16[1,128,3584]{2,1,0:T(8,128)(2,1)S(1)}, bf16[1,128,3584]{2,1,0:T(8,128)(2,1)}, u32[]{:S(2)}) copy-start(bf16[1,128,3584]{2,1,0:T(8,128)(2,1)} %param.17) | copy-start | bytes 2752516
  336.2 8.4 %collective-permute-start = (bf16[1,128,896]{2,1,0:T(8,128)(2,1)S(1)}, bf16[1,128,896]{2,1,0:T(8,128)(2,1)S(1)}, u32[]{:S(2)}, u32[]{:S(2)}) collective-permute-start(bf16[1,128,896]{2,1,0:T(8,128)(2,1)S(1)} %fusion.42), channel_id=1, source_target_pairs={{0,64},{64,128},{128,192},{192,0},{1,65},{65,129},{129,193},{193,1... | collective-permute-start | bytes 688136 | tf_op jit(solution)/shard_map/ppermute | solution.py:9
Sparse Core Ops, SparseCore 0:
  211.4 38.9 reduce-scatter.8
  266.2 35.8 reduce-scatter.6
where the time goes:
time: 354 us; the launch traced here: 353 us
  waiting for transfers between devices  128 us (36%)
  blocking collectives  85.2 us (24%)
  local copies, waits for them, and re-layouts  41 us (12%)
  matrix products  37.8 us (11%)
  starting transfers between devices  30.1 us (9%)
  other arithmetic  16.7 us (5%)
  between operations  14.4 us (4%)
    all_to_all x1, blocking collectives, local(): lax.all_to_all(scaled_send, 'expert', split_axis=0, concat_axis=0, tiled=...  71.6 us
    all_to_all x1, waiting for transfers between devices, local(): lax.all_to_all(bwd_send, 'expert', split_axis=0, concat_axis=0, tiled=True)  47.2 us
    all_to_all x1, waiting for transfers between devices, local(): lax.all_to_all(fwd_send, 'expert', split_axis=0, concat_axis=0, tiled=True)  37 us
    unnamed x4, waiting for transfers between devices  28.3 us
    unnamed x23, local copies, waits for them, and re-layouts  16.7 us
    all_gather x1, blocking collectives, local(): grad_rows = lax.all_gather(grad_own, 'dp', axis=1, tiled=True)  13.6 us
    all_to_all x2, starting transfers between devices, local(): lax.all_to_all(summed.reshape(experts, items, quarter), 'expert', split_a...  13.2 us
    all_to_all x2, waiting for transfers between devices, local(): lax.all_to_all(summed.reshape(experts, items, quarter), 'expert', split_a...  12 us
  transfers between devices with their start and end apart: 8, of which 5 were waited for; matrix products, arithmetic and copies ran while one was open for 21% of the time, Pallas kernels for 0%

commit v1 on v0

v1 whole, which is shorter than its diff:
```python
import functools

import jax
import jax.numpy as jnp
from jax import lax
from jax.experimental import pallas as pl
from jax.experimental.pallas import tpu as pltpu
from jax.sharding import PartitionSpec as P

F32 = jnp.float32
BF16 = jnp.bfloat16
MIB = 1024 * 1024


def shifted(array, axis, by):
    count = lax.axis_size(axis)
    return lax.ppermute(array, axis, [(i, (i + by) % count) for i in range(count)])


def dot(a, b):
    return jnp.dot(a, b, preferred_element_type=F32)


def dot_nt(a, b):
    return lax.dot_general(a, b, (((1,), (1,)), ((), ())), preferred_element_type=F32)


def params(mib):
    return pltpu.CompilerParams(vmem_limit_bytes=mib * MIB)


def cost(flops, nbytes):
    return pl.CostEstimate(flops=int(flops), bytes_accessed=int(nbytes), transcendentals=0)


def whole(shape):
    return pl.BlockSpec(shape, lambda *_: (0,) * len(shape))


def targets(ids, experts, capacity):
    topk, rows = ids.shape
    expert_of = lax.broadcasted_iota(jnp.int32, (experts, rows), 0)
    earlier = (
        lax.broadcasted_iota(jnp.int32, (rows, rows), 0)
        < lax.broadcasted_iota(jnp.int32, (rows, rows), 1)
    ).astype(BF16)
    before = jnp.zeros((experts, 1), F32)
    found = []
    for k in range(topk):
        named = (expert_of == ids[k : k + 1]).astype(F32)
        place = dot(named.astype(BF16), earlier) + before
        place = jnp.sum(named * place, axis=0, keepdims=True)
        found.append(ids[k : k + 1] * capacity + place.astype(jnp.int32))
        before = before + jnp.sum(named, axis=1, keepdims=True)
    return found


def as_column(row):
    rows = row.shape[1]
    same = lax.broadcasted_iota(jnp.int32, (rows, rows), 0) == lax.broadcasted_iota(
        jnp.int32, (rows, rows), 1
    )
    return jnp.sum(jnp.where(same, row, jnp.zeros_like(row)), axis=1, keepdims=True)


def slot_hits(ids, experts, capacity):
    rows = ids.shape[1]
    slot = lax.broadcasted_iota(jnp.int32, (experts * capacity, rows), 0)
    return [slot == t for t in targets(ids, experts, capacity)]


def one_hot(hit):
    return jnp.where(hit, 1.0, 0.0).astype(BF16)


def pack_kernel(experts, capacity, rank_ref, ids_ref, source_ref, out_ref):
    hits = slot_hits(ids_ref[...], experts, capacity)
    chosen = one_hot(functools.reduce(jnp.logical_or, hits))
    out_ref[...] = dot(chosen, source_ref[...]).astype(BF16)


def pack_scaled_kernel(experts, capacity, ids_ref, gates_ref, source_ref, out_ref):
    hits = slot_hits(ids_ref[...], experts, capacity)
    chosen = one_hot(functools.reduce(jnp.logical_or, hits))
    gate = sum(
        jnp.sum(jnp.where(hit, gates_ref[k : k + 1], 0.0), axis=1, keepdims=True)
        for k, hit in enumerate(hits)
    )
    out_ref[...] = (gate * dot(chosen, source_ref[...])).astype(BF16)


def pack(rank, ids, source, experts, capacity, quarter):
    rows = source.shape[0]
    slots = experts * capacity
    return pl.pallas_call(
        functools.partial(pack_kernel, experts, capacity),
        grid_spec=pltpu.PrefetchScalarGridSpec(
            num_scalar_prefetch=1,
            grid=(1,),
            in_specs=[
                whole(ids.shape),
                pl.BlockSpec((rows, quarter), lambda i, order: (0, order[0])),
            ],
            out_specs=whole((slots, quarter)),
        ),
        out_shape=jax.ShapeDtypeStruct((slots, quarter), BF16),
        compiler_params=params(24),
        cost_estimate=cost(2 * slots * rows * quarter, 4 * slots * quarter),
    )(rank, ids, source)


def pack_scaled(ids, gates, source, experts, capacity):
    rows, quarter = source.shape
    slots = experts * capacity
    return pl.pallas_call(
        functools.partial(pack_scaled_kernel, experts, capacity),
        out_shape=jax.ShapeDtypeStruct((slots, quarter), BF16),
        compiler_params=params(24),
        cost_estimate=cost(2 * slots * rows * quarter, 4 * slots * quarter),
    )(ids, gates, source)


def token_hits(ids, experts, capacity):
    rows = ids.shape[1]
    slot = lax.broadcasted_iota(jnp.int32, (rows, experts * capacity), 1)
    return [slot == as_column(t) for t in targets(ids, experts, capacity)]


def combine_gated_kernel(experts, capacity, rank_ref, ids_ref, gates_ref, own_ref, back_ref, out_ref):
    total = own_ref[...].astype(F32)
    for k, hit in enumerate(token_hits(ids_ref[...], experts, capacity)):
        total += as_column(gates_ref[k : k + 1]) * dot(one_hot(hit), back_ref[...])
    out_ref[...] = total.astype(BF16)


def combine_kernel(experts, capacity, ids_ref, own_ref, back_ref, out_ref):
    hits = token_hits(ids_ref[...], experts, capacity)
    chosen = one_hot(functools.reduce(jnp.logical_or, hits))
    total = own_ref[...].astype(F32) + dot(chosen, back_ref[...])
    out_ref[...] = total.astype(BF16)


def combine_gated(rank, ids, gates, own, back, experts, capacity):
    rows = ids.shape[1]
    slots, quarter = back.shape
    return pl.pallas_call(
        functools.partial(combine_gated_kernel, experts, capacity),
        grid_spec=pltpu.PrefetchScalarGridSpec(
            num_scalar_prefetch=1,
            grid=(1,),
            in_specs=[
                whole(ids.shape),
                whole(gates.shape),
                pl.BlockSpec((rows, quarter), lambda i, order: (0, order[0])),
                whole(back.shape),
            ],
            out_specs=whole((rows, quarter)),
        ),
        out_shape=jax.ShapeDtypeStruct((rows, quarter), BF16),
        compiler_params=params(24),
        cost_estimate=cost(4 * slots * rows * quarter, 4 * slots * quarter),
    )(rank, ids, gates, own, back)


def combine(ids, own, back, experts, capacity):
    rows = ids.shape[1]
    slots, quarter = back.shape
    return pl.pallas_call(
        functools.partial(combine_kernel, experts, capacity),
        out_shape=jax.ShapeDtypeStruct((rows, quarter), BF16),
        compiler_params=params(24),
        cost_estimate=cost(2 * slots * rows * quarter, 4 * slots * quarter),
    )(ids, own, back)


def gather_quarters(block):
    half = block.shape[0] // 2
    left = shifted(block, "dp", 1)
    right = shifted(block, "dp", -1)
    far_top = shifted(left[:half], "dp", 1)
    far_bottom = shifted(right[half:], "dp", -1)
    return (block, left, right, far_top, far_bottom)


def pick(step, refs, far_ref):
    own, left, right, far_top, far_bottom = refs
    half = far_top.shape[0]

    @pl.when(step == 0)
    def _():
        far_ref[...] = own[...]

    @pl.when(step == 1)
    def _():
        far_ref[...] = left[...]

    @pl.when(step == 2)
    def _():
        far_ref[...] = right[...]

    @pl.when(step == 3)
    def _():
        far_ref[:half] = far_top[...]
        far_ref[half:] = far_bottom[...]

    return far_ref[...]


def forward_hidden_kernel(order_ref, *refs):
    xs = refs[:5]
    gate_ref, up_ref, down_ref, hidden_ref, far_out_ref, rows_ref, gate_acc, up_acc = refs[5:]
    step = pl.program_id(0)
    rows = pick(step, xs, rows_ref)
    gate_part = dot(rows, gate_ref[...])
    up_part = dot(rows, up_ref[...])

    @pl.when(step == 0)
    def _():
        gate_acc[...] = gate_part
        up_acc[...] = up_part

    @pl.when(step > 0)
    def _():
        gate_acc[...] += gate_part
        up_acc[...] += up_part

    @pl.when(step == pl.num_programs(0) - 1)
    def _():
        gate_pre = gate_acc[...]
        hidden = (gate_pre * jax.nn.sigmoid(gate_pre) * up_acc[...]).astype(BF16)
        hidden_ref[...] = hidden
        far_out_ref[...] = dot(hidden, down_ref[...]).astype(BF16)


def quarter_specs(blocks):
    return [
        pl.BlockSpec(b.shape, lambda i, order: (0, 0), pipeline_mode=pl.Buffered(1)) for b in blocks
    ]


def forward_hidden(order, xs, gate_mat, up_mat, down_mat):
    slots, quarter = xs[0].shape
    width = gate_mat.shape[1]
    groups = gate_mat.shape[0] // quarter
    weight = pl.BlockSpec((quarter, width), lambda i, order: (order[i], 0))
    return pl.pallas_call(
        forward_hidden_kernel,
        grid_spec=pltpu.PrefetchScalarGridSpec(
            num_scalar_prefetch=1,
            grid=(groups,),
            in_specs=quarter_specs(xs)
            + [weight, weight, pl.BlockSpec((width, quarter), lambda i, order: (0, order[3]))],
            out_specs=[whole((slots, width)), whole((slots, quarter))],
            scratch_shapes=[
                pltpu.VMEM((slots, quarter), BF16),
                pltpu.VMEM((slots, width), F32),
                pltpu.VMEM((slots, width), F32),
            ],
        ),
        out_shape=[
            jax.ShapeDtypeStruct((slots, width), BF16),
            jax.ShapeDtypeStruct((slots, quarter), BF16),
        ],
        compiler_params=params(40),
        cost_estimate=cost(
            2 * slots * width * quarter * (2 * groups + 1), 2 * quarter * width * (2 * groups + 1)
        ),
    )(order, *xs, gate_mat, up_mat, down_mat)


def forward_rest_kernel(order_ref, hidden_ref, down_ref, *out_refs):
    step = pl.program_id(0)
    part = dot(hidden_ref[...], down_ref[...]).astype(BF16)
    for number, out_ref in enumerate(out_refs):

        @pl.when(step == number)
        def _():
            out_ref[...] = part


def forward_rest(order, hidden, down_mat, quarter):
    slots, width = hidden.shape
    return pl.pallas_call(
        forward_rest_kernel,
        grid_spec=pltpu.PrefetchScalarGridSpec(
            num_scalar_prefetch=1,
            grid=(3,),
            in_specs=[
                whole((slots, width)),
                pl.BlockSpec((width, quarter), lambda i, order: (0, order[(i + 1) % 3])),
            ],
            out_specs=[whole((slots, quarter))] * 3,
        ),
        out_shape=[jax.ShapeDtypeStruct((slots, quarter), BF16)] * 3,
        compiler_params=params(40),
        cost_estimate=cost(6 * slots * width * quarter, 6 * quarter * (width + slots)),
    )(order, hidden, down_mat)


def backward_hidden_kernel(order_ref, *refs):
    ss, xs = refs[:5], refs[5:10]
    (
        gate_ref,
        up_ref,
        down_ref,
        far_gate_ref,
        far_up_ref,
        d_gate_ref,
        d_up_ref,
        far_out_ref,
        rows_ref,
        gate_acc,
        up_acc,
        back_acc,
    ) = refs[10:]
    step = pl.program_id(0)
    rows = pick(step, xs, rows_ref)
    gate_part = dot(rows, gate_ref[...])
    up_part = dot(rows, up_ref[...])
    scaled = pick(step, ss, rows_ref)
    back_part = dot_nt(scaled, down_ref[...])

    @pl.when(step == 0)
    def _():
        gate_acc[...] = gate_part
        up_acc[...] = up_part
        back_acc[...] = back_part

    @pl.when(step > 0)
    def _():
        gate_acc[...] += gate_part
        up_acc[...] += up_part
        back_acc[...] += back_part

    @pl.when(step == pl.num_programs(0) - 1)
    def _():
        gate_pre = gate_acc[...]
        squash = jax.nn.sigmoid(gate_pre)
        turned = back_acc[...] * squash
        d_gate = (turned * up_acc[...] * (1.0 + gate_pre * (1.0 - squash))).astype(BF16)
        d_up = (turned * gate_pre).astype(BF16)
        d_gate_ref[...] = d_gate
        d_up_ref[...] = d_up
        far = dot_nt(d_gate, far_gate_ref[...]) + dot_nt(d_up, far_up_ref[...])
        far_out_ref[...] = far.astype(BF16)


def backward_hidden(order, ss, xs, gate_mat, up_mat, down_mat):
    slots, quarter = xs[0].shape
    width = gate_mat.shape[1]
    groups = gate_mat.shape[0] // quarter
    weight = pl.BlockSpec((quarter, width), lambda i, order: (order[i], 0))
    far = pl.BlockSpec((quarter, width), lambda i, order: (order[3], 0))
    return pl.pallas_call(
        backward_hidden_kernel,
        grid_spec=pltpu.PrefetchScalarGridSpec(
            num_scalar_prefetch=1,
            grid=(groups,),
            in_specs=quarter_specs(ss)
            + quarter_specs(xs)
            + [
                weight,
                weight,
                pl.BlockSpec((width, quarter), lambda i, order: (0, order[i])),
                far,
                far,
            ],
            out_specs=[whole((slots, width)), whole((slots, width)), whole((slots, quarter))],
            scratch_shapes=[pltpu.VMEM((slots, quarter), BF16)]
            + [pltpu.VMEM((slots, width), F32)] * 3,
        ),
        out_shape=[
            jax.ShapeDtypeStruct((slots, width), BF16),
            jax.ShapeDtypeStruct((slots, width), BF16),
            jax.ShapeDtypeStruct((slots, quarter), BF16),
        ],
        compiler_params=params(48),
        cost_estimate=cost(
            2 * slots * width * quarter * (3 * groups + 2), 2 * quarter * width * (3 * groups + 2)
        ),
    )(order, *ss, *xs, gate_mat, up_mat, down_mat, gate_mat, up_mat)


def backward_rest_kernel(order_ref, d_gate_ref, d_up_ref, gate_ref, up_ref, *out_refs):
    step = pl.program_id(0)
    part = dot_nt(d_gate_ref[...], gate_ref[...]) + dot_nt(d_up_ref[...], up_ref[...])
    part = part.astype(BF16)
    for number, out_ref in enumerate(out_refs):

        @pl.when(step == number)
        def _():
            out_ref[...] = part


def backward_rest(order, d_gate, d_up, gate_mat, up_mat, quarter):
    slots, width = d_gate.shape
    weight = pl.BlockSpec((quarter, width), lambda i, order: (order[(i + 1) % 3], 0))
    return pl.pallas_call(
        backward_rest_kernel,
        grid_spec=pltpu.PrefetchScalarGridSpec(
            num_scalar_prefetch=1,
            grid=(3,),
            in_specs=[whole((slots, width)), whole((slots, width)), weight, weight],
            out_specs=[whole((slots, quarter))] * 3,
        ),
        out_shape=[jax.ShapeDtypeStruct((slots, quarter), BF16)] * 3,
        compiler_params=params(40),
        cost_estimate=cost(12 * slots * width * quarter, 6 * quarter * (2 * width + slots)),
    )(order, d_gate, d_up, gate_mat, up_mat)


def relay_add_kernel(left_ref, right_ref, top_ref, bottom_ref, left_out, right_out):
    half = top_ref.shape[0]
    left_out[:half] = (left_ref[:half].astype(F32) + top_ref[...].astype(F32)).astype(BF16)
    left_out[half:] = left_ref[half:]
    right_out[:half] = right_ref[:half]
    right_out[half:] = (right_ref[half:].astype(F32) + bottom_ref[...].astype(F32)).astype(BF16)


def relay_add(left, right, top, bottom):
    shape = jax.ShapeDtypeStruct(left.shape, BF16)
    return pl.pallas_call(
        relay_add_kernel,
        out_shape=[shape, shape],
        compiler_params=params(24),
        cost_estimate=cost(left.size, 10 * left.size),
    )(left, right, top, bottom)


def sum_kernel(a_ref, b_ref, c_ref, out_ref):
    total = a_ref[...].astype(F32) + b_ref[...].astype(F32) + c_ref[...].astype(F32)
    out_ref[...] = total.astype(BF16)


def summed(a, b, c):
    return pl.pallas_call(
        sum_kernel,
        out_shape=jax.ShapeDtypeStruct(a.shape, BF16),
        compiler_params=params(24),
        cost_estimate=cost(3 * a.size, 8 * a.size),
    )(a, b, c)


def far_halves(far):
    half = far.shape[0] // 2
    return shifted(far[:half], "dp", -1), shifted(far[half:], "dp", 1)


def scatter_sums(left, right, own, top, bottom):
    to_left, to_right = relay_add(left, right, top, bottom)
    return summed(own, shifted(to_left, "dp", -1), shifted(to_right, "dp", 1))


def exchange(rows, experts):
    slots, width = rows.shape
    blocks = rows.reshape(experts, slots // experts, width)
    return lax.all_to_all(blocks, "expert", split_axis=0, concat_axis=0, tiled=True).reshape(
        slots, width
    )


def local(x_fwd, ids_fwd, gates_fwd, x_bwd, ids_bwd, gates_bwd, grad_in, w_gate, w_up, w_down):
    experts = lax.axis_size("expert")
    groups = lax.axis_size("dp")
    dp_rank = lax.axis_index("dp")
    rows_dev = x_fwd.shape[1]
    topk = ids_fwd.shape[2]
    capacity = rows_dev * topk * 3 // (2 * experts)
    quarter = x_fwd.shape[2] // groups
    order = (dp_rank + jnp.array([0, groups - 1, 1, 2], jnp.int32)) % groups
    gate_mat = w_gate[0, 0]
    up_mat = w_up[0, 0]
    down_mat = w_down[0, 0]
    fwd_ids, fwd_gates = ids_fwd[0].T, gates_fwd[0].T
    bwd_ids, bwd_gates = ids_bwd[0].T, gates_bwd[0].T

    scaled = pack_scaled(bwd_ids, bwd_gates, grad_in[0], experts, capacity)
    scaled = exchange(scaled, experts)
    bwd_rows = exchange(pack(order, bwd_ids, x_bwd[0], experts, capacity, quarter), experts)
    fwd_rows = exchange(pack(order, fwd_ids, x_fwd[0], experts, capacity, quarter), experts)

    ss = gather_quarters(scaled)
    xs = gather_quarters(bwd_rows)
    fs = gather_quarters(fwd_rows)

    d_gate, d_up, far = backward_hidden(order, ss, xs, gate_mat, up_mat, down_mat)
    top, bottom = far_halves(far)
    left, right, own = backward_rest(order, d_gate, d_up, gate_mat, up_mat, quarter)
    bwd_sum = scatter_sums(left, right, own, top, bottom)
    bwd_back = exchange(bwd_sum, experts)

    hidden, far = forward_hidden(order, fs, gate_mat, up_mat, down_mat)
    top, bottom = far_halves(far)
    left, right, own = forward_rest(order, hidden, down_mat, quarter)
    fwd_sum = scatter_sums(left, right, own, top, bottom)
    fwd_back = exchange(fwd_sum, experts)

    layer_grad = combine(bwd_ids, grad_in[0], bwd_back, experts, capacity)
    sent_backward = shifted(layer_grad[None], "pipe", -1)
    layer_out = combine_gated(order, fwd_ids, fwd_gates, x_fwd[0], fwd_back, experts, capacity)
    sent_forward = shifted(layer_out[None], "pipe", 1)
    return (sent_forward, sent_backward)


def solution(mesh):
    in_specs = (
        P("pipe", "expert", None),
        P("pipe", "expert", None),
        P("pipe", "expert", None),
        P("pipe", "expert", None),
        P("pipe", "expert", None),
        P("pipe", "expert", None),
        P("pipe", "expert", "dp"),
        P("pipe", "expert", None, "dp"),
        P("pipe", "expert", None, "dp"),
        P("pipe", "expert", "dp", None),
    )
    out_specs = (P("pipe", "expert", "dp"), P("pipe", "expert", "dp"))
    return jax.shard_map(local, mesh=mesh, in_specs=in_specs, out_specs=out_specs, check_vma=False)
```

time: 354 us -> 226 us (0.64)
  blocking collectives: 85.2 us -> 0 us
  starting transfers between devices: 30.1 us -> 82.3 us
  waiting for transfers between devices: 128 us -> 81.3 us
  matrix products: 37.8 us -> 0 us
  Pallas kernels: 0 us -> 37.5 us
  local copies, waits for them, and re-layouts: 41 us -> 22.4 us
  other arithmetic: 16.7 us -> 0.75 us
  between operations: 14.4 us -> 0.93 us
    all_to_all x1 -> x0, blocking collectives: 71.6 us -> none  [local(): lax.all_to_all(scaled_send, 'expert', split_axis=0, concat_axis=0, tiled=...]
    all_to_all x4 -> x5, waiting for transfers between devices: 96.3 us -> 34.9 us  [exchange(): lax.all_to_all(blocks, 'expert', split_axis=0, concat_axis=0, tiled=True)]
    ppermute x2 -> x22, waiting for transfers between devices: 2.97 us -> 46.5 us  [shifted(): lax.ppermute(array, axis, [(i, (i + by) % count) for i in range(count)])]
    ppermute x2 -> x22, starting transfers between devices: 6.29 us -> 45.1 us  [shifted(): lax.ppermute(array, axis, [(i, (i + by) % count) for i in range(count)])]
    dot_general x6 -> x0, matrix products: 37.8 us -> none  [the longest x1 9.54 us: local(): jnp.dot(d_gate, gate_mat.T, preferred_element_type=jnp.float32)]
    pallas_call x0 -> x13, Pallas kernels: none -> 37.5 us  [the longest x1 12.8 us: backward_hidden(): pl.pallas_call(backward_hidden_kernel, grid_spec=pltpu.PrefetchScalarGrid...]
    unnamed x4 -> x0, waiting for transfers between devices: 28.3 us -> none
    gather x6 -> x0, local copies, waits for them, and re-layouts: 16.9 us -> none  [the longest x3 11.7 us: pack_rows(): picked = jnp.take(source, jnp.maximum(owner, 0) // topk, axis=0)]
  transfers between devices with their start and end apart: 8 -> 27, of which waited for: 5 -> 15; matrix products, arithmetic and copies ran while one was open for 21% -> 3% of each run, Pallas kernels for 0% -> 16%
where the time goes in v1:
time: 226 us; the launch traced here: 225 us
  starting transfers between devices  82.3 us (36%)
  waiting for transfers between devices  81.3 us (36%)
  Pallas kernels  37.5 us (17%)
  local copies, waits for them, and re-layouts  22.4 us (10%)
    ppermute x22, waiting for transfers between devices, shifted(): lax.ppermute(array, axis, [(i, (i + by) % count) for i in range(count)])  46.5 us
    ppermute x22, starting transfers between devices, shifted(): lax.ppermute(array, axis, [(i, (i + by) % count) for i in range(count)])  45.1 us
    all_to_all x5, starting transfers between devices, exchange(): lax.all_to_all(blocks, 'expert', split_axis=0, concat_axis=0, tiled=True)  37.2 us
    all_to_all x5, waiting for transfers between devices, exchange(): lax.all_to_all(blocks, 'expert', split_axis=0, concat_axis=0, tiled=True)  34.9 us
    unnamed x40, local copies, waits for them, and re-layouts  15.8 us
    pallas_call x1, Pallas kernels, backward_hidden(): pl.pallas_call(backward_hidden_kernel, grid_spec=pltpu.PrefetchScalarGrid...  12.8 us
    pallas_call x1, Pallas kernels, forward_hidden(): pl.pallas_call(forward_hidden_kernel, grid_spec=pltpu.PrefetchScalarGridS...  7.49 us
  transfers between devices with their start and end apart: 27, of which 15 were waited for; matrix products, arithmetic and copies ran while one was open for 3% of the time, Pallas kernels for 16%

profile of v1, /device:TPU:1, one launch (start us, length us, event | category | flops | bytes accessed | tf_op | source)
XLA Modules:
  0.0 225.3 jit_solution(4977280570299892362)
XLA Ops:
  1.4 1.2 copy-done.8
  3.3 1.9 shard_map.129
  5.1 10.1 %all-to-all-start.3 = ((bf16[16,24,896]{2,1,0:T(8,128)(2,1)}), bf16[16,24,896]{2,1,0:T(8,128)(2,1)S(1)}, u32[]{:S(2)}, u32[]{:S(2)}) async-start(bf16[16,24,896]{2,1,0:T(8,128)(2,1)} %bitcast.23), calls=%async_computation.3 | async-start | bytes 1376256 | tf_op jit(solution)/shard_map/all_to_all | solution.py:457
  17.5 1.4 shard_map.128
  18.9 15.1 %all-to-all-done.3 = bf16[16,24,896]{2,1,0:T(8,128)(2,1)S(1)} async-done(((bf16[16,24,896]{2,1,0:T(8,128)(2,1)}), bf16[16,24,896]{2,1,0:T(8,128)(2,1)S(1)}, u32[]{:S(2)}, u32[]{:S(2)}) %all-to-all-start.3) | async-done | bytes 688160 | tf_op jit(solution)/shard_map/all_to_all | solution.py:457
  34.1 5.1 %all-to-all-start.2 = ((bf16[16,24,896]{2,1,0:T(8,128)(2,1)}), bf16[16,24,896]{2,1,0:T(8,128)(2,1)S(1)}, u32[]{:S(2)}, u32[]{:S(2)}) async-start(bf16[16,24,896]{2,1,0:T(8,128)(2,1)} %bitcast.20), calls=%async_computation.2 | async-start | bytes 1376256 | tf_op jit(solution)/shard_map/all_to_all | solution.py:457
  39.2 1.3 collective-permute-start.13
  40.5 1.5 collective-permute-start.14
  41.9 15.7 %all-to-all-done.2 = bf16[16,24,896]{2,1,0:T(8,128)(2,1)S(1)} async-done(((bf16[16,24,896]{2,1,0:T(8,128)(2,1)}), bf16[16,24,896]{2,1,0:T(8,128)(2,1)S(1)}, u32[]{:S(2)}, u32[]{:S(2)}) %all-to-all-start.2) | async-done | bytes 688160 | tf_op jit(solution)/shard_map/all_to_all | solution.py:457
  57.6 1.2 collective-permute-start.9
  58.8 1.5 collective-permute-start.10
  60.3 1.9 shard_map.122
  62.2 5.3 %all-to-all-start = ((bf16[16,24,896]{2,1,0:T(8,128)(2,1)}), bf16[16,24,896]{2,1,0:T(8,128)(2,1)S(1)}, u32[]{:S(2)}, u32[]{:S(2)}) async-start(bf16[16,24,896]{2,1,0:T(8,128)(2,1)} %bitcast.6), calls=%async_computation | async-start | bytes 1376256 | tf_op jit(solution)/shard_map/all_to_all | solution.py:457
  69.6 2.7 %collective-permute-start.16 = (bf16[192,896]{1,0:T(8,128)(2,1)S(1)}, bf16[192,896]{1,0:T(8,128)(2,1)S(1)}, u32[]{:S(2)}, u32[]{:S(2)}) collective-permute-start(bf16[192,896]{1,0:T(8,128)(2,1)S(1)} %slice.45), channel_id=1, source_target_pairs={{0,3},{1,0},{2,1},{3,2},{4,7},{5,4},{6,5},{7,6},{8,11},{9,8},{10,9... | collective-permute-start | bytes 1032200 | tf_op jit(solution)/shard_map/ppermute | solution.py:17
  75.0 2.7 %collective-permute-start.12 = (bf16[192,896]{1,0:T(8,128)(2,1)S(1)}, bf16[192,896]{1,0:T(8,128)(2,1)S(1)}, u32[]{:S(2)}, u32[]{:S(2)}) collective-permute-start(bf16[192,896]{1,0:T(8,128)(2,1)S(1)} %slice.43), channel_id=1, source_target_pairs={{0,3},{1,0},{2,1},{3,2},{4,7},{5,4},{6,5},{7,6},{8,11},{9,8},{10,9... | collective-permute-start | bytes 1032200 | tf_op jit(solution)/shard_map/ppermute | solution.py:17
  77.7 2.4 %collective-permute-done.15.refs_8_ = bf16[192,896]{1,0:T(8,128)(2,1)S(1)} collective-permute-done((bf16[192,896]{1,0:T(8,128)(2,1)S(1)}, bf16[192,896]{1,0:T(8,128)(2,1)S(1)}, u32[]{:S(2)}, u32[]{:S(2)}) %collective-permute-start.15) | collective-permute-done | bytes 344096 | tf_op jit(solution)/shard_map/ppermute | solution.py:17
  80.3 7.3 %collective-permute-done.11.refs_3_ = bf16[192,896]{1,0:T(8,128)(2,1)S(1)} collective-permute-done((bf16[192,896]{1,0:T(8,128)(2,1)S(1)}, bf16[192,896]{1,0:T(8,128)(2,1)S(1)}, u32[]{:S(2)}, u32[]{:S(2)}) %collective-permute-start.11) | collective-permute-done | bytes 344096 | tf_op jit(solution)/shard_map/ppermute | solution.py:17
  87.5 12.8 %shard_map.130 = (bf16[384,512]{1,0:T(8,128)(2,1)S(1)}, bf16[384,512]{1,0:T(8,128)(2,1)S(1)}, bf16[384,896]{1,0:T(8,128)(2,1)S(1)}) custom-call(s32[4]{0:T(128)S(1)} %and_select_fusion.rank_ref.order_ref, bf16[384,896]{1,0:T(8,128)(2,1)S(1)} %bitcast.48, bf16[384,896]{1,0:T(8,128)(2,1)} %collective-permute-done.9.refs_1_, ...), custom_call_target="tpu_custom_call" | custom-call | flops 4932501504 | bytes 12845056 | tf_op jit(solution)/shard_map/pallas_call | solution.py:354
  101.3 2.6 %collective-permute-start.17 = (bf16[192,896]{1,0:T(8,128)(2,1)}, bf16[192,896]{1,0:T(8,128)(2,1)}, u32[]{:S(2)}, u32[]{:S(2)}) collective-permute-start(bf16[192,896]{1,0:T(8,128)(2,1)} %get-tuple-element.33), channel_id=1, source_target_pairs={{0,3},{1,0},{2,1},{3,2},{4,7},{5,4},{6,5},{7,6},{8,11},{9,8},{10,9... | collective-permute-start | bytes 1032200 | tf_op jit(solution)/shard_map/ppermute | solution.py:17
  104.0 2.7 %collective-permute-start.1 = (bf16[384,896]{1,0:T(8,128)(2,1)S(1)}, bf16[384,896]{1,0:T(8,128)(2,1)S(1)}, u32[]{:S(2)}, u32[]{:S(2)}) collective-permute-start(bf16[384,896]{1,0:T(8,128)(2,1)S(1)} %bitcast.52), channel_id=1, source_target_pairs={{0,3},{1,0},{2,1},{3,2},{4,7},{5,4},{6,5},{7,6},{8,11},{9,8},{10,9... | collective-permute-start | bytes 2064392 | tf_op jit(solution)/shard_map/ppermute | solution.py:17
  106.7 2.0 copy-done
  108.7 2.0 copy-done.2
  111.8 3.9 %shard_map.131 = (bf16[384,896]{1,0:T(8,128)(2,1)S(1)}, bf16[384,896]{1,0:T(8,128)(2,1)S(1)}, bf16[384,896]{1,0:T(8,128)(2,1)S(1)}) custom-call(s32[4]{0:T(128)S(1)} %and_select_fusion.rank_ref.order_ref, bf16[384,512]{1,0:T(8,128)(2,1)S(1)} %get-tuple-element.24.d_gate_ref, bf16[384,512]{1,0:T(8,128)(2,1)S(1)} %copy-done.12, ...), custom_call_target="tpu_custom_call" | custom-call | flops 2113929216 | bytes 7569408 | tf_op jit(solution)/shard_map/pallas_call | solution.py:398
  115.6 1.3 shard_map.132
  116.9 1.5 collective-permute-start.19
  118.5 6.9 %collective-permute-done.refs_1_ = bf16[384,896]{1,0:T(8,128)(2,1)S(1)} collective-permute-done((bf16[384,896]{1,0:T(8,128)(2,1)S(1)}, bf16[384,896]{1,0:T(8,128)(2,1)S(1)}, u32[]{:S(2)}, u32[]{:S(2)}) %collective-permute-start) | collective-permute-done | bytes 688160 | tf_op jit(solution)/shard_map/ppermute | solution.py:17
  127.0 2.7 %collective-permute-start.3 = (bf16[192,896]{1,0:T(8,128)(2,1)}, bf16[192,896]{1,0:T(8,128)(2,1)}, u32[]{:S(2)}, u32[]{:S(2)}) collective-permute-start(bf16[192,896]{1,0:T(8,128)(2,1)} %slice.41), channel_id=1, source_target_pairs={{0,3},{1,0},{2,1},{3,2},{4,7},{5,4},{6,5},{7,6},{8,11},{9,8},{10,9... | collective-permute-start | bytes 1032200 | tf_op jit(solution)/shard_map/ppermute | solution.py:17
  129.7 7.3 %collective-permute-done.19.b_ref = bf16[384,896]{1,0:T(8,128)(2,1)S(1)} collective-permute-done((bf16[384,896]{1,0:T(8,128)(2,1)S(1)}, bf16[384,896]{1,0:T(8,128)(2,1)S(1)}, u32[]{:S(2)}, u32[]{:S(2)}) %collective-permute-start.19) | collective-permute-done | bytes 688160 | tf_op jit(solution)/shard_map/ppermute | solution.py:17
  137.0 3.1 %collective-permute-done.20.c_ref = bf16[384,896]{1,0:T(8,128)(2,1)S(1)} collective-permute-done((bf16[384,896]{1,0:T(8,128)(2,1)S(1)}, bf16[384,896]{1,0:T(8,128)(2,1)S(1)}, u32[]{:S(2)}, u32[]{:S(2)}) %collective-permute-start.20) | collective-permute-done | bytes 688160 | tf_op jit(solution)/shard_map/ppermute | solution.py:17
  140.2 1.1 shard_map.133
  141.3 9.3 %all-to-all-start.4 = ((bf16[16,24,896]{2,1,0:T(8,128)(2,1)}), bf16[16,24,896]{2,1,0:T(8,128)(2,1)S(1)}, u32[]{:S(2)}, u32[]{:S(2)}) async-start(bf16[16,24,896]{2,1,0:T(8,128)(2,1)} %bitcast.25), calls=%async_computation.4 | async-start | bytes 1376256 | tf_op jit(solution)/shard_map/all_to_all | solution.py:457
  150.6 2.0 copy-done.1
  152.7 2.0 copy-done.3
  155.8 7.5 %shard_map.123 = (bf16[384,512]{1,0:T(8,128)(2,1)S(1)}, bf16[384,896]{1,0:T(8,128)(2,1)S(1)}) custom-call(s32[4]{0:T(128)S(1)} %and_select_fusion.rank_ref.order_ref, bf16[384,896]{1,0:T(8,128)(2,1)S(1)} %bitcast.53, bf16[384,896]{1,0:T(8,128)(2,1)S(1)} %collective-permute-done.refs_1_, bf16[384,896]{1,0:T(8,128)(2,1)S(1)} %copy-done.7, ...), custom_call_target="tpu_custom_call" | custom-call | flops 3170893824 | bytes 8257536 | tf_op jit(solution)/shard_map/pallas_call | solution.py:246
  163.7 1.2 collective-permute-start.5
  164.9 2.8 %shard_map.124 = (bf16[384,896]{1,0:T(8,128)(2,1)S(1)}, bf16[384,896]{1,0:T(8,128)(2,1)S(1)}, bf16[384,896]{1,0:T(8,128)(2,1)S(1)}) custom-call(s32[4]{0:T(128)S(1)} %and_select_fusion.rank_ref.order_ref, bf16[384,512]{1,0:T(8,128)(2,1)S(1)} %get-tuple-element.17.hidden_ref, bf16[512,3584]{1,0:T(8,128)(2,1)S(1)} %bitcast.40), custom_call_target="tpu_custom_call" | custom-call | flops 1056964608 | bytes 4816896 | tf_op jit(solution)/shard_map/pallas_call | solution.py:283
  167.8 2.1 collective-permute-done.4.top_ref
  169.8 1.5 collective-permute-done.5.bottom_ref
  171.6 1.5 collective-permute-start.7
  173.1 10.8 %collective-permute-done.6.b_ref = bf16[384,896]{1,0:T(8,128)(2,1)S(1)} collective-permute-done((bf16[384,896]{1,0:T(8,128)(2,1)S(1)}, bf16[384,896]{1,0:T(8,128)(2,1)S(1)}, u32[]{:S(2)}, u32[]{:S(2)}) %collective-permute-start.6) | collective-permute-done | bytes 688160 | tf_op jit(solution)/shard_map/ppermute | solution.py:17
  183.9 1.3 collective-permute-done.7.c_ref
  185.2 1.1 shard_map.126
  186.3 7.4 %all-to-all-start.1 = ((bf16[16,24,896]{2,1,0:T(8,128)(2,1)}), bf16[16,24,896]{2,1,0:T(8,128)(2,1)S(1)}, u32[]{:S(2)}, u32[]{:S(2)}) async-start(bf16[16,24,896]{2,1,0:T(8,128)(2,1)} %bitcast.11), calls=%async_computation.1 | async-start | bytes 1376256 | tf_op jit(solution)/shard_map/all_to_all | solution.py:457
  194.3 8.9 %collective-permute-start.21 = (bf16[1,128,896]{2,1,0:T(8,128)(2,1)S(1)}, bf16[1,128,896]{2,1,0:T(8,128)(2,1)S(1)}, u32[]{:S(2)}, u32[]{:S(2)}) collective-permute-start(bf16[1,128,896]{2,1,0:T(8,128)(2,1)S(1)} %bitcast.58), channel_id=1, source_target_pairs={{0,192},{64,0},{128,64},{192,128},{1,193},{65,1},{129,65},{193,129... | collective-permute-start | bytes 688136 | tf_op jit(solution)/shard_map/ppermute | solution.py:17
  203.2 4.0 %all-to-all-done.1 = bf16[16,24,896]{2,1,0:T(8,128)(2,1)S(1)} async-done(((bf16[16,24,896]{2,1,0:T(8,128)(2,1)}), bf16[16,24,896]{2,1,0:T(8,128)(2,1)S(1)}, u32[]{:S(2)}, u32[]{:S(2)}) %all-to-all-start.1) | async-done | bytes 688160 | tf_op jit(solution)/shard_map/all_to_all | solution.py:457
  207.2 1.2 shard_map.127
  208.4 12.5 %collective-permute-start.8 = (bf16[1,128,896]{2,1,0:T(8,128)(2,1)S(1)}, bf16[1,128,896]{2,1,0:T(8,128)(2,1)S(1)}, u32[]{:S(2)}, u32[]{:S(2)}) collective-permute-start(bf16[1,128,896]{2,1,0:T(8,128)(2,1)S(1)} %bitcast.57), channel_id=1, source_target_pairs={{0,64},{64,128},{128,192},{192,0},{1,65},{65,129},{129,193},{193,1... | collective-permute-start | bytes 688136 | tf_op jit(solution)/shard_map/ppermute | solution.py:17
  220.9 3.0 %collective-permute-done.8 = bf16[1,128,896]{2,1,0:T(8,128)(2,1)S(1)} collective-permute-done((bf16[1,128,896]{2,1,0:T(8,128)(2,1)S(1)}, bf16[1,128,896]{2,1,0:T(8,128)(2,1)S(1)}, u32[]{:S(2)}, u32[]{:S(2)}) %collective-permute-start.8) | collective-permute-done | bytes 229408 | tf_op jit(solution)/shard_map/ppermute | solution.py:17
  (68 shorter events, 16.1 us)
Async XLA Ops:
  0.6 59.7 %copy-start.5 = (bf16[1,128,3584]{2,1,0:T(8,128)(2,1)S(1)}, bf16[1,128,3584]{2,1,0:T(8,128)(2,1)}, u32[]{:S(2)}) copy-start(bf16[1,128,3584]{2,1,0:T(8,128)(2,1)} %param.11) | copy-start | bytes 2752516
  1.4 1.2 copy-start.8
  2.6 0.7 copy-start.13
  3.2 57.1 %copy-start.16 = (s32[1,128,2]{1,2,0:T(2,128)S(1)}, s32[1,128,2]{1,2,0:T(2,128)}, u32[]{:S(2)}) copy-start(s32[1,128,2]{1,2,0:T(2,128)} %param.12) | copy-start | bytes 3076
  5.1 29.0 %all-to-all-start.3 = ((bf16[16,24,896]{2,1,0:T(8,128)(2,1)}), bf16[16,24,896]{2,1,0:T(8,128)(2,1)S(1)}, u32[]{:S(2)}, u32[]{:S(2)}) async-start(bf16[16,24,896]{2,1,0:T(8,128)(2,1)} %bitcast.23), calls=%async_computation.3 | async-start | bytes 1376256 | tf_op jit(solution)/shard_map/all_to_all | solution.py:457
  15.2 0.9 copy-start.9
  16.2 0.7 copy-start.14
  16.9 0.7 copy-start.18
  34.1 23.6 %all-to-all-start.2 = ((bf16[16,24,896]{2,1,0:T(8,128)(2,1)}), bf16[16,24,896]{2,1,0:T(8,128)(2,1)S(1)}, u32[]{:S(2)}, u32[]{:S(2)}) async-start(bf16[16,24,896]{2,1,0:T(8,128)(2,1)} %bitcast.20), calls=%async_computation.2 | async-start | bytes 1376256 | tf_op jit(solution)/shard_map/all_to_all | solution.py:457
  39.2 28.3 %collective-permute-start.13 = (bf16[384,896]{1,0:T(8,128)(2,1)S(1)}, bf16[384,896]{1,0:T(8,128)(2,1)}, u32[]{:S(2)}, u32[]{:S(2)}) collective-permute-start(bf16[384,896]{1,0:T(8,128)(2,1)S(1)} %bitcast.43), channel_id=1, source_target_pairs={{0,1},{1,2},{2,3},{3,0},{4,5},{5,6},{6,7},{7,4},{8,9},{9,10},{10,1... | collective-permute-start | bytes 2064392 | tf_op jit(solution)/shard_map/ppermute | solution.py:17
  40.5 28.1 %collective-permute-start.14 = (bf16[384,896]{1,0:T(8,128)(2,1)S(1)}, bf16[384,896]{1,0:T(8,128)(2,1)}, u32[]{:S(2)}, u32[]{:S(2)}) collective-permute-start(bf16[384,896]{1,0:T(8,128)(2,1)S(1)} %bitcast.44), channel_id=1, source_target_pairs={{0,3},{1,0},{2,1},{3,2},{4,7},{5,4},{6,5},{7,6},{8,11},{9,8},{10,9... | collective-permute-start | bytes 2064392 | tf_op jit(solution)/shard_map/ppermute | solution.py:17
  57.6 15.3 %collective-permute-start.9 = (bf16[384,896]{1,0:T(8,128)(2,1)S(1)}, bf16[384,896]{1,0:T(8,128)(2,1)}, u32[]{:S(2)}, u32[]{:S(2)}) collective-permute-start(bf16[384,896]{1,0:T(8,128)(2,1)S(1)} %bitcast.46), channel_id=1, source_target_pairs={{0,1},{1,2},{2,3},{3,0},{4,5},{5,6},{6,7},{7,4},{8,9},{9,10},{10,1... | collective-permute-start | bytes 2064392 | tf_op jit(solution)/shard_map/ppermute | solution.py:17
  58.8 15.1 %collective-permute-start.10 = (bf16[384,896]{1,0:T(8,128)(2,1)S(1)}, bf16[384,896]{1,0:T(8,128)(2,1)}, u32[]{:S(2)}, u32[]{:S(2)}) collective-permute-start(bf16[384,896]{1,0:T(8,128)(2,1)S(1)} %bitcast.47), channel_id=1, source_target_pairs={{0,3},{1,0},{2,1},{3,2},{4,7},{5,4},{6,5},{7,6},{8,11},{9,8},{10,9... | collective-permute-start | bytes 2064392 | tf_op jit(solution)/shard_map/ppermute | solution.py:17
  62.2 41.8 %all-to-all-start = ((bf16[16,24,896]{2,1,0:T(8,128)(2,1)}), bf16[16,24,896]{2,1,0:T(8,128)(2,1)S(1)}, u32[]{:S(2)}, u32[]{:S(2)}) async-start(bf16[16,24,896]{2,1,0:T(8,128)(2,1)} %bitcast.6), calls=%async_computation | async-start | bytes 1376256 | tf_op jit(solution)/shard_map/all_to_all | solution.py:457
  68.5 11.7 %collective-permute-start.15 = (bf16[192,896]{1,0:T(8,128)(2,1)S(1)}, bf16[192,896]{1,0:T(8,128)(2,1)S(1)}, u32[]{:S(2)}, u32[]{:S(2)}) collective-permute-start(bf16[192,896]{1,0:T(8,128)(2,1)S(1)} %slice.44), channel_id=1, source_target_pairs={{0,1},{1,2},{2,3},{3,0},{4,5},{5,6},{6,7},{7,4},{8,9},{9,10},{10,1... | collective-permute-start | bytes 1032200 | tf_op jit(solution)/shard_map/ppermute | solution.py:17
  69.6 10.7 %collective-permute-start.16 = (bf16[192,896]{1,0:T(8,128)(2,1)S(1)}, bf16[192,896]{1,0:T(8,128)(2,1)S(1)}, u32[]{:S(2)}, u32[]{:S(2)}) collective-permute-start(bf16[192,896]{1,0:T(8,128)(2,1)S(1)} %slice.45), channel_id=1, source_target_pairs={{0,3},{1,0},{2,1},{3,2},{4,7},{5,4},{6,5},{7,6},{8,11},{9,8},{10,9... | collective-permute-start | bytes 1032200 | tf_op jit(solution)/shard_map/ppermute | solution.py:17
  73.9 13.6 %collective-permute-start.11 = (bf16[192,896]{1,0:T(8,128)(2,1)S(1)}, bf16[192,896]{1,0:T(8,128)(2,1)S(1)}, u32[]{:S(2)}, u32[]{:S(2)}) collective-permute-start(bf16[192,896]{1,0:T(8,128)(2,1)S(1)} %slice.42), channel_id=1, source_target_pairs={{0,1},{1,2},{2,3},{3,0},{4,5},{5,6},{6,7},{7,4},{8,9},{9,10},{10,1... | collective-permute-start | bytes 1032200 | tf_op jit(solution)/shard_map/ppermute | solution.py:17
  75.0 12.5 %collective-permute-start.12 = (bf16[192,896]{1,0:T(8,128)(2,1)S(1)}, bf16[192,896]{1,0:T(8,128)(2,1)S(1)}, u32[]{:S(2)}, u32[]{:S(2)}) collective-permute-start(bf16[192,896]{1,0:T(8,128)(2,1)S(1)} %slice.43), channel_id=1, source_target_pairs={{0,3},{1,0},{2,1},{3,2},{4,7},{5,4},{6,5},{7,6},{8,11},{9,8},{10,9... | collective-permute-start | bytes 1032200 | tf_op jit(solution)/shard_map/ppermute | solution.py:17
  100.3 3.6 %copy-start.11 = (bf16[384,512]{1,0:T(8,128)(2,1)}, bf16[384,512]{1,0:T(8,128)(2,1)S(1)}, u32[]{:S(2)}) copy-start(bf16[384,512]{1,0:T(8,128)(2,1)S(1)} %get-tuple-element.25.d_up_ref) | copy-start | bytes 1179652
  101.3 14.3 %collective-permute-start.17 = (bf16[192,896]{1,0:T(8,128)(2,1)}, bf16[192,896]{1,0:T(8,128)(2,1)}, u32[]{:S(2)}, u32[]{:S(2)}) collective-permute-start(bf16[192,896]{1,0:T(8,128)(2,1)} %get-tuple-element.33), channel_id=1, source_target_pairs={{0,3},{1,0},{2,1},{3,2},{4,7},{5,4},{6,5},{7,6},{8,11},{9,8},{10,9... | collective-permute-start | bytes 1032200 | tf_op jit(solution)/shard_map/ppermute | solution.py:17
  103.9 11.7 %collective-permute-start.18 = (bf16[192,896]{1,0:T(8,128)(2,1)}, bf16[192,896]{1,0:T(8,128)(2,1)}, u32[]{:S(2)}, u32[]{:S(2)}) collective-permute-start(bf16[192,896]{1,0:T(8,128)(2,1)} %get-tuple-element.32), channel_id=1, source_target_pairs={{0,1},{1,2},{2,3},{3,0},{4,5},{5,6},{6,7},{7,4},{8,9},{9,10},{10,1... | collective-permute-start | bytes 1032200 | tf_op jit(solution)/shard_map/ppermute | solution.py:17
  103.9 21.5 %collective-permute-start = (bf16[384,896]{1,0:T(8,128)(2,1)S(1)}, bf16[384,896]{1,0:T(8,128)(2,1)S(1)}, u32[]{:S(2)}, u32[]{:S(2)}) collective-permute-start(bf16[384,896]{1,0:T(8,128)(2,1)S(1)} %bitcast.51), channel_id=1, source_target_pairs={{0,1},{1,2},{2,3},{3,0},{4,5},{5,6},{6,7},{7,4},{8,9},{9,10},{10,1... | collective-permute-start | bytes 2064392 | tf_op jit(solution)/shard_map/ppermute | solution.py:17
  104.0 22.2 %collective-permute-start.1 = (bf16[384,896]{1,0:T(8,128)(2,1)S(1)}, bf16[384,896]{1,0:T(8,128)(2,1)S(1)}, u32[]{:S(2)}, u32[]{:S(2)}) collective-permute-start(bf16[384,896]{1,0:T(8,128)(2,1)S(1)} %bitcast.52), channel_id=1, source_target_pairs={{0,3},{1,0},{2,1},{3,2},{4,7},{5,4},{6,5},{7,6},{8,11},{9,8},{10,9... | collective-permute-start | bytes 2064392 | tf_op jit(solution)/shard_map/ppermute | solution.py:17
  106.7 2.0 copy-start
  108.7 2.0 copy-start.2
  110.8 1.0 copy-start.12
  116.9 20.1 %collective-permute-start.19 = (bf16[384,896]{1,0:T(8,128)(2,1)S(1)}, bf16[384,896]{1,0:T(8,128)(2,1)S(1)}, u32[]{:S(2)}, u32[]{:S(2)}) collective-permute-start(bf16[384,896]{1,0:T(8,128)(2,1)S(1)} %get-tuple-element.30), channel_id=1, source_target_pairs={{0,3},{1,0},{2,1},{3,2},{4,7},{5,4},{6,5},{7,6},{8,11},{9,8},{10,9... | collective-permute-start | bytes 2064392 | tf_op jit(solution)/shard_map/ppermute | solution.py:17
  118.4 21.8 %collective-permute-start.20 = (bf16[384,896]{1,0:T(8,128)(2,1)S(1)}, bf16[384,896]{1,0:T(8,128)(2,1)S(1)}, u32[]{:S(2)}, u32[]{:S(2)}) collective-permute-start(bf16[384,896]{1,0:T(8,128)(2,1)S(1)} %get-tuple-element.31), channel_id=1, source_target_pairs={{0,1},{1,2},{2,3},{3,0},{4,5},{5,6},{6,7},{7,4},{8,9},{9,10},{10,1... | collective-permute-start | bytes 2064392 | tf_op jit(solution)/shard_map/ppermute | solution.py:17
  126.2 24.4 %collective-permute-start.2 = (bf16[192,896]{1,0:T(8,128)(2,1)}, bf16[192,896]{1,0:T(8,128)(2,1)S(1)}, u32[]{:S(2)}, u32[]{:S(2)}) collective-permute-start(bf16[192,896]{1,0:T(8,128)(2,1)} %slice.40), channel_id=1, source_target_pairs={{0,1},{1,2},{2,3},{3,0},{4,5},{5,6},{6,7},{7,4},{8,9},{9,10},{10,1... | collective-permute-start | bytes 1032200 | tf_op jit(solution)/shard_map/ppermute | solution.py:17
  126.2 15.1 %copy-start.6 = (bf16[384,896]{1,0:T(8,128)(2,1)}, bf16[384,896]{1,0:T(8,128)(2,1)S(1)}, u32[]{:S(2)}) copy-start(bf16[384,896]{1,0:T(8,128)(2,1)S(1)} %collective-permute-done.1.refs_2_) | copy-start | bytes 2064388
  127.0 23.6 %collective-permute-start.3 = (bf16[192,896]{1,0:T(8,128)(2,1)}, bf16[192,896]{1,0:T(8,128)(2,1)}, u32[]{:S(2)}, u32[]{:S(2)}) collective-permute-start(bf16[192,896]{1,0:T(8,128)(2,1)} %slice.41), channel_id=1, source_target_pairs={{0,3},{1,0},{2,1},{3,2},{4,7},{5,4},{6,5},{7,6},{8,11},{9,8},{10,9... | collective-permute-start | bytes 1032200 | tf_op jit(solution)/shard_map/ppermute | solution.py:17
  141.3 45.1 %all-to-all-start.4 = ((bf16[16,24,896]{2,1,0:T(8,128)(2,1)}), bf16[16,24,896]{2,1,0:T(8,128)(2,1)S(1)}, u32[]{:S(2)}, u32[]{:S(2)}) async-start(bf16[16,24,896]{2,1,0:T(8,128)(2,1)} %bitcast.25), calls=%async_computation.4 | async-start | bytes 1376256 | tf_op jit(solution)/shard_map/all_to_all | solution.py:457
  150.6 2.0 copy-start.1
  152.7 2.0 copy-start.3
  154.7 1.1 copy-start.7
  155.8 9.1 %copy-start.4 = (bf16[1,1,512,3584]{3,2,1,0:T(8,128)(2,1)S(1)}, bf16[1,1,512,3584]{3,2,1,0:T(8,128)(2,1)}, u32[]{:S(2)}) copy-start(bf16[1,1,512,3584]{3,2,1,0:T(8,128)(2,1)} %param.20) | copy-start | bytes 11010052
  163.4 6.5 %collective-permute-start.4 = (bf16[192,896]{1,0:T(8,128)(2,1)S(1)}, bf16[192,896]{1,0:T(8,128)(2,1)S(1)}, u32[]{:S(2)}, u32[]{:S(2)}) collective-permute-start(bf16[192,896]{1,0:T(8,128)(2,1)S(1)} %get-tuple-element.35), channel_id=1, source_target_pairs={{0,3},{1,0},{2,1},{3,2},{4,7},{5,4},{6,5},{7,6},{8,11},{9,8},{10,9... | collective-permute-start | bytes 1032200 | tf_op jit(solution)/shard_map/ppermute | solution.py:17
  163.7 7.6 %collective-permute-start.5 = (bf16[192,896]{1,0:T(8,128)(2,1)S(1)}, bf16[192,896]{1,0:T(8,128)(2,1)S(1)}, u32[]{:S(2)}, u32[]{:S(2)}) collective-permute-start(bf16[192,896]{1,0:T(8,128)(2,1)S(1)} %get-tuple-element.34), channel_id=1, source_target_pairs={{0,1},{1,2},{2,3},{3,0},{4,5},{5,6},{6,7},{7,4},{8,9},{9,10},{10,1... | collective-permute-start | bytes 1032200 | tf_op jit(solution)/shard_map/ppermute | solution.py:17
  167.7 26.0 %copy-start.10 = (bf16[1,128,896]{2,1,0:T(8,128)(2,1)S(1)}, bf16[1,128,896]{2,1,0:T(8,128)(2,1)}, u32[]{:S(2)}) copy-start(bf16[1,128,896]{2,1,0:T(8,128)(2,1)} %param.17) | copy-start | bytes 688132
  167.8 26.0 %copy-start.15 = (s32[1,128,2]{1,2,0:T(2,128)S(1)}, s32[1,128,2]{1,2,0:T(2,128)}, u32[]{:S(2)}) copy-start(s32[1,128,2]{1,2,0:T(2,128)} %param.15) | copy-start | bytes 3076
  171.3 35.9 %copy-start.17 = (f32[1,128,2]{1,2,0:T(2,128)S(1)}, f32[1,128,2]{1,2,0:T(2,128)}, u32[]{:S(2)}) copy-start(f32[1,128,2]{1,2,0:T(2,128)} %param.13) | copy-start | bytes 3076
  171.5 12.4 %collective-permute-start.6 = (bf16[384,896]{1,0:T(8,128)(2,1)S(1)}, bf16[384,896]{1,0:T(8,128)(2,1)S(1)}, u32[]{:S(2)}, u32[]{:S(2)}) collective-permute-start(bf16[384,896]{1,0:T(8,128)(2,1)S(1)} %get-tuple-element.22), channel_id=1, source_target_pairs={{0,3},{1,0},{2,1},{3,2},{4,7},{5,4},{6,5},{7,6},{8,11},{9,8},{10,9... | collective-permute-start | bytes 2064392 | tf_op jit(solution)/shard_map/ppermute | solution.py:17
  171.6 13.6 %collective-permute-start.7 = (bf16[384,896]{1,0:T(8,128)(2,1)S(1)}, bf16[384,896]{1,0:T(8,128)(2,1)S(1)}, u32[]{:S(2)}, u32[]{:S(2)}) collective-permute-start(bf16[384,896]{1,0:T(8,128)(2,1)S(1)} %get-tuple-element.23), channel_id=1, source_target_pairs={{0,1},{1,2},{2,3},{3,0},{4,5},{5,6},{6,7},{7,4},{8,9},{9,10},{10,1... | collective-permute-start | bytes 2064392 | tf_op jit(solution)/shard_map/ppermute | solution.py:17
  186.3 20.9 %all-to-all-start.1 = ((bf16[16,24,896]{2,1,0:T(8,128)(2,1)}), bf16[16,24,896]{2,1,0:T(8,128)(2,1)S(1)}, u32[]{:S(2)}, u32[]{:S(2)}) async-start(bf16[16,24,896]{2,1,0:T(8,128)(2,1)} %bitcast.11), calls=%async_computation.1 | async-start | bytes 1376256 | tf_op jit(solution)/shard_map/all_to_all | solution.py:457
  194.3 26.6 %collective-permute-start.21 = (bf16[1,128,896]{2,1,0:T(8,128)(2,1)S(1)}, bf16[1,128,896]{2,1,0:T(8,128)(2,1)S(1)}, u32[]{:S(2)}, u32[]{:S(2)}) collective-permute-start(bf16[1,128,896]{2,1,0:T(8,128)(2,1)S(1)} %bitcast.58), channel_id=1, source_target_pairs={{0,192},{64,0},{128,64},{192,128},{1,193},{65,1},{129,65},{193,129... | collective-permute-start | bytes 688136 | tf_op jit(solution)/shard_map/ppermute | solution.py:17
  208.4 15.5 %collective-permute-start.8 = (bf16[1,128,896]{2,1,0:T(8,128)(2,1)S(1)}, bf16[1,128,896]{2,1,0:T(8,128)(2,1)S(1)}, u32[]{:S(2)}, u32[]{:S(2)}) collective-permute-start(bf16[1,128,896]{2,1,0:T(8,128)(2,1)S(1)} %bitcast.57), channel_id=1, source_target_pairs={{0,64},{64,128},{128,192},{192,0},{1,65},{65,129},{129,193},{193,1... | collective-permute-start | bytes 688136 | tf_op jit(solution)/shard_map/ppermute | solution.py:17

commit v2 on v1

v2 whole, which is shorter than its diff:
```python
import functools

import jax
import jax.numpy as jnp
from jax import lax
from jax.experimental import pallas as pl
from jax.experimental.pallas import tpu as pltpu
from jax.sharding import PartitionSpec as P

F32 = jnp.float32
BF16 = jnp.bfloat16
MIB = 1024 * 1024


def shifted(array, axis, by):
    count = lax.axis_size(axis)
    return lax.ppermute(array, axis, [(i, (i + by) % count) for i in range(count)])


def dot(a, b):
    return jnp.dot(a, b, preferred_element_type=F32)


def dot_nt(a, b):
    return lax.dot_general(a, b, (((1,), (1,)), ((), ())), preferred_element_type=F32)


def params(mib):
    return pltpu.CompilerParams(vmem_limit_bytes=mib * MIB)


def cost(flops, nbytes):
    return pl.CostEstimate(flops=int(flops), bytes_accessed=int(nbytes), transcendentals=0)


def lasting(microseconds):
    return pl.CostEstimate(flops=int(1e9 * microseconds), bytes_accessed=0, transcendentals=0)


def whole(shape):
    return pl.BlockSpec(shape, lambda *_: (0,) * len(shape))


def targets(ids, experts, capacity):
    topk, rows = ids.shape
    expert_of = lax.broadcasted_iota(jnp.int32, (experts, rows), 0)
    earlier = (
        lax.broadcasted_iota(jnp.int32, (rows, rows), 0)
        < lax.broadcasted_iota(jnp.int32, (rows, rows), 1)
    ).astype(BF16)
    before = jnp.zeros((experts, 1), F32)
    found = []
    for k in range(topk):
        named = (expert_of == ids[k : k + 1]).astype(F32)
        place = dot(named.astype(BF16), earlier) + before
        place = jnp.sum(named * place, axis=0, keepdims=True)
        found.append(ids[k : k + 1] * capacity + place.astype(jnp.int32))
        before = before + jnp.sum(named, axis=1, keepdims=True)
    return found


def as_column(row):
    rows = row.shape[1]
    same = lax.broadcasted_iota(jnp.int32, (rows, rows), 0) == lax.broadcasted_iota(
        jnp.int32, (rows, rows), 1
    )
    return jnp.sum(jnp.where(same, row, jnp.zeros_like(row)), axis=1, keepdims=True)


def slot_hits(ids, experts, capacity):
    rows = ids.shape[1]
    slot = lax.broadcasted_iota(jnp.int32, (experts * capacity, rows), 0)
    return [slot == t for t in targets(ids, experts, capacity)]


def one_hot(hit):
    return jnp.where(hit, 1.0, 0.0).astype(BF16)


def pack_kernel(experts, capacity, ids_ref, source_ref, out_ref):
    hits = slot_hits(ids_ref[...], experts, capacity)
    chosen = one_hot(functools.reduce(jnp.logical_or, hits))
    out_ref[...] = dot(chosen, source_ref[...]).astype(BF16)


def pack(ids, source, experts, capacity):
    slots, width = experts * capacity, source.shape[1]
    return pl.pallas_call(
        functools.partial(pack_kernel, experts, capacity),
        out_shape=jax.ShapeDtypeStruct((slots, width), BF16),
        compiler_params=params(32),
        cost_estimate=cost(2 * slots * source.size, 4 * slots * width),
    )(ids, source)


def pack_pair_kernel(experts, capacity, order_ref, ids_ref, gates_ref, grad_ref, source_ref, out_ref):
    hits = slot_hits(ids_ref[...], experts, capacity)
    chosen = one_hot(functools.reduce(jnp.logical_or, hits))
    gate = sum(
        jnp.sum(jnp.where(hit, gates_ref[k : k + 1], 0.0), axis=1, keepdims=True)
        for k, hit in enumerate(hits)
    )
    quarter = grad_ref.shape[1]
    out_ref[:, :quarter] = (gate * dot(chosen, grad_ref[...])).astype(BF16)
    out_ref[:, quarter:] = dot(chosen, source_ref[...]).astype(BF16)


def pack_pair(order, ids, gates, grad, source, experts, capacity):
    rows, quarter = grad.shape
    slots = experts * capacity
    return pl.pallas_call(
        functools.partial(pack_pair_kernel, experts, capacity),
        grid_spec=pltpu.PrefetchScalarGridSpec(
            num_scalar_prefetch=1,
            grid=(1,),
            in_specs=[
                whole(ids.shape),
                whole(gates.shape),
                whole(grad.shape),
                pl.BlockSpec((rows, quarter), lambda i, order: (0, order[0])),
            ],
            out_specs=whole((slots, 2 * quarter)),
        ),
        out_shape=jax.ShapeDtypeStruct((slots, 2 * quarter), BF16),
        compiler_params=params(60),
        cost_estimate=cost(4 * slots * rows * quarter, 8 * slots * quarter),
    )(order, ids, gates, grad, source)


def token_hits(ids, experts, capacity):
    rows = ids.shape[1]
    slot = lax.broadcasted_iota(jnp.int32, (rows, experts * capacity), 1)
    return [slot == as_column(t) for t in targets(ids, experts, capacity)]


def combine_gated_kernel(experts, capacity, rank_ref, ids_ref, gates_ref, own_ref, back_ref, out_ref):
    total = own_ref[...].astype(F32)
    for k, hit in enumerate(token_hits(ids_ref[...], experts, capacity)):
        total += as_column(gates_ref[k : k + 1]) * dot(one_hot(hit), back_ref[...])
    out_ref[...] = total.astype(BF16)


def combine_kernel(experts, capacity, ids_ref, own_ref, back_ref, out_ref):
    hits = token_hits(ids_ref[...], experts, capacity)
    chosen = one_hot(functools.reduce(jnp.logical_or, hits))
    total = own_ref[...].astype(F32) + dot(chosen, back_ref[...])
    out_ref[...] = total.astype(BF16)


def combine_gated(rank, ids, gates, own, back, experts, capacity):
    rows = ids.shape[1]
    slots, quarter = back.shape
    return pl.pallas_call(
        functools.partial(combine_gated_kernel, experts, capacity),
        grid_spec=pltpu.PrefetchScalarGridSpec(
            num_scalar_prefetch=1,
            grid=(1,),
            in_specs=[
                whole(ids.shape),
                whole(gates.shape),
                pl.BlockSpec((rows, quarter), lambda i, order: (0, order[0])),
                whole(back.shape),
            ],
            out_specs=whole((rows, quarter)),
        ),
        out_shape=jax.ShapeDtypeStruct((rows, quarter), BF16),
        compiler_params=params(24),
        cost_estimate=cost(4 * slots * rows * quarter, 4 * slots * quarter),
    )(rank, ids, gates, own, back)


def combine(ids, own, back, experts, capacity):
    rows = ids.shape[1]
    slots, quarter = back.shape
    return pl.pallas_call(
        functools.partial(combine_kernel, experts, capacity),
        out_shape=jax.ShapeDtypeStruct((rows, quarter), BF16),
        compiler_params=params(24),
        cost_estimate=cost(2 * slots * rows * quarter, 4 * slots * quarter),
    )(ids, own, back)


def halves_kernel(top_ref, bottom_ref, top_out, bottom_out):
    top_out[...] = top_ref[...]
    bottom_out[...] = bottom_ref[...]


def halves(first, second):
    rows, width = first.shape
    half = (rows // 2, width)
    shape = jax.ShapeDtypeStruct(half, BF16)
    return pl.pallas_call(
        halves_kernel,
        grid=(1,),
        in_specs=[
            pl.BlockSpec(half, lambda i: (0, 0)),
            pl.BlockSpec(half, lambda i: (1, 0)),
        ],
        out_specs=[whole(half)] * 2,
        out_shape=[shape, shape],
        compiler_params=params(24),
        cost_estimate=cost(rows, 4 * rows * width),
    )(first, second)


def fixed(shape):
    return pl.BlockSpec(shape, lambda *_: (0,) * len(shape), pipeline_mode=pl.Buffered(1))


def accumulate(step, acc_ref, part):
    @pl.when(step == 0)
    def _():
        acc_ref[...] = part

    @pl.when(step > 0)
    def _():
        acc_ref[...] += part


def backward_early_kernel(order_ref, own, left, right, gate_ref, up_ref, down_ref, *refs):
    gate_acc, up_acc, back_acc, rows_ref = refs
    step = pl.program_id(0)
    for number, ref in enumerate((own, left, right)):

        @pl.when(step == number)
        def _():
            rows_ref[...] = ref[...]

    quarter = rows_ref.shape[1] // 2
    accumulate(step, back_acc, dot_nt(rows_ref[:, :quarter], down_ref[...]))
    accumulate(step, gate_acc, dot(rows_ref[:, quarter:], gate_ref[...]))
    accumulate(step, up_acc, dot(rows_ref[:, quarter:], up_ref[...]))


def backward_early(order, blocks, gate_mat, up_mat, down_mat):
    slots, pair = blocks[0].shape
    width, quarter = down_mat.shape[0], pair // 2
    weight = pl.BlockSpec((quarter, width), lambda i, order: (order[i], 0))
    return pl.pallas_call(
        backward_early_kernel,
        grid_spec=pltpu.PrefetchScalarGridSpec(
            num_scalar_prefetch=1,
            grid=(3,),
            in_specs=[fixed(b.shape) for b in blocks]
            + [weight, weight, pl.BlockSpec((width, quarter), lambda i, order: (0, order[i]))],
            out_specs=[whole((slots, width))] * 3,
            scratch_shapes=[pltpu.VMEM((slots, pair), BF16)],
        ),
        out_shape=[jax.ShapeDtypeStruct((slots, width), F32)] * 3,
        compiler_params=params(32),
        cost_estimate=cost(18 * slots * width * quarter, 18 * quarter * width),
    )(order, *blocks, gate_mat, up_mat, down_mat)


def split(value, top_out, bottom_out):
    half = top_out.shape[0]
    top_out[...] = value[:half].astype(BF16)
    bottom_out[...] = value[half:].astype(BF16)


def backward_late_kernel(order_ref, top, bottom, gate_in, up_in, back_in, gate_ref, up_ref, down_ref, *refs):
    d_gate_ref, d_up_ref, top_out, bottom_out, rows_ref = refs
    half = top.shape[0]
    quarter = rows_ref.shape[1] // 2
    rows_ref[:half] = top[...]
    rows_ref[half:] = bottom[...]
    gate_pre = gate_in[...] + dot(rows_ref[:, quarter:], gate_ref[...])
    up_pre = up_in[...] + dot(rows_ref[:, quarter:], up_ref[...])
    back = back_in[...] + dot_nt(rows_ref[:, :quarter], down_ref[...])
    squash = jax.nn.sigmoid(gate_pre)
    turned = back * squash
    d_gate = (turned * up_pre * (1.0 + gate_pre * (1.0 - squash))).astype(BF16)
    d_up = (turned * gate_pre).astype(BF16)
    d_gate_ref[...] = d_gate
    d_up_ref[...] = d_up
    split(dot_nt(d_gate, gate_ref[...]) + dot_nt(d_up, up_ref[...]), top_out, bottom_out)


def backward_late(order, far, accs, gate_mat, up_mat, down_mat):
    half, pair = far[0].shape
    quarter = pair // 2
    slots, width = accs[0].shape
    rows = pl.BlockSpec((quarter, width), lambda i, order: (order[3], 0))
    columns = pl.BlockSpec((width, quarter), lambda i, order: (0, order[3]))
    wide = jax.ShapeDtypeStruct((slots, width), BF16)
    part = jax.ShapeDtypeStruct((half, quarter), BF16)
    return pl.pallas_call(
        backward_late_kernel,
        grid_spec=pltpu.PrefetchScalarGridSpec(
            num_scalar_prefetch=1,
            grid=(1,),
            in_specs=[fixed(b.shape) for b in (*far, *accs)] + [rows, rows, columns],
            out_specs=[whole(wide.shape)] * 2 + [whole(part.shape)] * 2,
            scratch_shapes=[pltpu.VMEM((slots, pair), BF16)],
        ),
        out_shape=[wide, wide, part, part],
        compiler_params=params(32),
        cost_estimate=cost(10 * slots * width * quarter, 6 * quarter * width),
    )(order, *far, *accs, gate_mat, up_mat, down_mat)


def forward_hidden_kernel(order_ref, rows_ref, gate_ref, up_ref, down_ref, *refs):
    hidden_ref, top_out, bottom_out, gate_acc, up_acc = refs
    step = pl.program_id(0)
    accumulate(step, gate_acc, dot(rows_ref[...], gate_ref[...]))
    accumulate(step, up_acc, dot(rows_ref[...], up_ref[...]))

    @pl.when(step == pl.num_programs(0) - 1)
    def _():
        gate_pre = gate_acc[...]
        hidden = (gate_pre * jax.nn.sigmoid(gate_pre) * up_acc[...]).astype(BF16)
        hidden_ref[...] = hidden
        split(dot(hidden, down_ref[...]), top_out, bottom_out)


def forward_hidden(order, rows, gate_mat, up_mat, down_mat, groups):
    slots, quarter = rows.shape[0], rows.shape[1] // groups
    width = gate_mat.shape[1]
    weight = pl.BlockSpec((quarter, width), lambda i, order: (i, 0))
    wide = jax.ShapeDtypeStruct((slots, width), BF16)
    part = jax.ShapeDtypeStruct((slots // 2, quarter), BF16)
    return pl.pallas_call(
        forward_hidden_kernel,
        grid_spec=pltpu.PrefetchScalarGridSpec(
            num_scalar_prefetch=1,
            grid=(groups,),
            in_specs=[
                pl.BlockSpec((slots, quarter), lambda i, order: (0, i)),
                weight,
                weight,
                pl.BlockSpec((width, quarter), lambda i, order: (0, order[3])),
            ],
            out_specs=[whole(wide.shape)] + [whole(part.shape)] * 2,
            scratch_shapes=[pltpu.VMEM((slots, width), F32)] * 2,
        ),
        out_shape=[wide, part, part],
        compiler_params=params(60),
        cost_estimate=cost(18 * slots * width * quarter, 18 * quarter * width),
    )(order, rows, gate_mat, up_mat, down_mat)


def forward_rest_kernel(order_ref, hidden_ref, down_ref, top_ref, bottom_ref, left, right, own):
    step = pl.program_id(0)
    half = top_ref.shape[0]
    part = dot(hidden_ref[...], down_ref[...])

    @pl.when(step == 0)
    def _():
        left[:half] = (part[:half] + top_ref[...].astype(F32)).astype(BF16)
        left[half:] = part[half:].astype(BF16)

    @pl.when(step == 1)
    def _():
        right[:half] = part[:half].astype(BF16)
        right[half:] = (part[half:] + bottom_ref[...].astype(F32)).astype(BF16)

    @pl.when(step == 2)
    def _():
        own[...] = part.astype(BF16)


def forward_rest(order, hidden, down_mat, halves_in, hint):
    slots, width = hidden.shape
    half, quarter = halves_in[0].shape
    return pl.pallas_call(
        forward_rest_kernel,
        grid_spec=pltpu.PrefetchScalarGridSpec(
            num_scalar_prefetch=1,
            grid=(3,),
            in_specs=[
                whole((slots, width)),
                pl.BlockSpec((width, quarter), lambda i, order: (0, order[(i + 1) % 3])),
                whole((half, quarter)),
                whole((half, quarter)),
            ],
            out_specs=[whole((slots, quarter))] * 3,
        ),
        out_shape=[jax.ShapeDtypeStruct((slots, quarter), BF16)] * 3,
        compiler_params=params(32),
        cost_estimate=lasting(hint),
    )(order, hidden, down_mat, *halves_in)


def backward_rest_kernel(order_ref, d_gate_ref, d_up_ref, gate_ref, up_ref, *out_refs):
    step = pl.program_id(0)
    part = dot_nt(d_gate_ref[...], gate_ref[...]) + dot_nt(d_up_ref[...], up_ref[...])
    part = part.astype(BF16)
    for number, out_ref in enumerate(out_refs):

        @pl.when(step == number)
        def _():
            out_ref[...] = part


def backward_rest(order, d_gate, d_up, gate_mat, up_mat, quarter):
    slots, width = d_gate.shape
    weight = pl.BlockSpec((quarter, width), lambda i, order: (order[(i + 1) % 3], 0))
    return pl.pallas_call(
        backward_rest_kernel,
        grid_spec=pltpu.PrefetchScalarGridSpec(
            num_scalar_prefetch=1,
            grid=(3,),
            in_specs=[whole((slots, width)), whole((slots, width)), weight, weight],
            out_specs=[whole((slots, quarter))] * 3,
        ),
        out_shape=[jax.ShapeDtypeStruct((slots, quarter), BF16)] * 3,
        compiler_params=params(32),
        cost_estimate=cost(12 * slots * width * quarter, 6 * quarter * (2 * width + slots)),
    )(order, d_gate, d_up, gate_mat, up_mat)


def relay_add_kernel(left_ref, right_ref, top_ref, bottom_ref, left_out, right_out):
    half = top_ref.shape[0]
    left_out[:half] = (left_ref[:half].astype(F32) + top_ref[...].astype(F32)).astype(BF16)
    left_out[half:] = left_ref[half:]
    right_out[:half] = right_ref[:half]
    right_out[half:] = (right_ref[half:].astype(F32) + bottom_ref[...].astype(F32)).astype(BF16)


def relay_add(left, right, top, bottom):
    shape = jax.ShapeDtypeStruct(left.shape, BF16)
    return pl.pallas_call(
        relay_add_kernel,
        out_shape=[shape, shape],
        compiler_params=params(24),
        cost_estimate=lasting(1),
    )(left, right, top, bottom)


def sum_kernel(a_ref, b_ref, c_ref, *refs):
    total = a_ref[...].astype(F32) + b_ref[...].astype(F32) + c_ref[...].astype(F32)
    refs[-1][...] = total.astype(BF16)


def summed(a, b, c, hint, after=()):
    return pl.pallas_call(
        sum_kernel,
        grid=(1,),
        in_specs=[whole(a.shape)] * 3 + [pl.BlockSpec(memory_space=pl.ANY)] * len(after),
        out_specs=whole(a.shape),
        out_shape=jax.ShapeDtypeStruct(a.shape, BF16),
        compiler_params=params(24),
        cost_estimate=lasting(hint),
    )(a, b, c, *after)


def exchange(rows, experts):
    slots, width = rows.shape
    blocks = rows.reshape(experts, slots // experts, width)
    return lax.all_to_all(blocks, "expert", split_axis=0, concat_axis=0, tiled=True).reshape(
        slots, width
    )


def local(x_fwd, ids_fwd, gates_fwd, x_bwd, ids_bwd, gates_bwd, grad_in, w_gate, w_up, w_down):
    experts = lax.axis_size("expert")
    groups = lax.axis_size("dp")
    dp_rank = lax.axis_index("dp")
    rows_dev = x_fwd.shape[1]
    topk = ids_fwd.shape[2]
    capacity = rows_dev * topk * 3 // (2 * experts)
    quarter = x_fwd.shape[2] // groups
    order = (dp_rank + jnp.array([0, groups - 1, 1, 2], jnp.int32)) % groups
    gate_mat = w_gate[0, 0]
    up_mat = w_up[0, 0]
    down_mat = w_down[0, 0]
    fwd_ids, fwd_gates = ids_fwd[0].T, gates_fwd[0].T
    bwd_ids, bwd_gates = ids_bwd[0].T, gates_bwd[0].T

    bwd_rows = pack_pair(
        order, bwd_ids, bwd_gates, grad_in[0], x_bwd[0], experts, capacity
    )
    bwd_rows = exchange(bwd_rows, experts)
    fwd_rows = exchange(pack(fwd_ids, x_fwd[0], experts, capacity), experts)

    left, right = shifted(bwd_rows, "dp", 1), shifted(bwd_rows, "dp", -1)
    top, bottom = halves(left, right)
    far = shifted(top, "dp", 1), shifted(bottom, "dp", -1)
    accs = backward_early(order, (bwd_rows, left, right), gate_mat, up_mat, down_mat)
    d_gate, d_up, top, bottom = backward_late(order, far, accs, gate_mat, up_mat, down_mat)
    bwd_far = shifted(top, "dp", -1), shifted(bottom, "dp", 1)
    bwd_left, bwd_right, bwd_own = backward_rest(order, d_gate, d_up, gate_mat, up_mat, quarter)
    bwd_left, bwd_right = relay_add(bwd_left, bwd_right, *bwd_far)
    bwd_left, bwd_right = shifted(bwd_left, "dp", -1), shifted(bwd_right, "dp", 1)

    hidden, top, bottom = forward_hidden(order, fwd_rows, gate_mat, up_mat, down_mat, groups)
    fwd_far = shifted(top, "dp", -1), shifted(bottom, "dp", 1)
    bwd_back = exchange(summed(bwd_own, bwd_left, bwd_right, 20, (top,)), experts)

    fwd_left, fwd_right, fwd_own = forward_rest(order, hidden, down_mat, fwd_far, 40)
    fwd_left, fwd_right = shifted(fwd_left, "dp", -1), shifted(fwd_right, "dp", 1)
    fwd_back = exchange(summed(fwd_own, fwd_left, fwd_right, 1), experts)

    layer_grad = combine(bwd_ids, grad_in[0], bwd_back, experts, capacity)
    sent_backward = shifted(layer_grad[None], "pipe", -1)
    layer_out = combine_gated(order, fwd_ids, fwd_gates, x_fwd[0], fwd_back, experts, capacity)
    sent_forward = shifted(layer_out[None], "pipe", 1)
    return (sent_forward, sent_backward)


def solution(mesh):
    in_specs = (
        P("pipe", "expert", None),
        P("pipe", "expert", None),
        P("pipe", "expert", None),
        P("pipe", "expert", None),
        P("pipe", "expert", None),
        P("pipe", "expert", None),
        P("pipe", "expert", "dp"),
        P("pipe", "expert", None, "dp"),
        P("pipe", "expert", None, "dp"),
        P("pipe", "expert", "dp", None),
    )
    out_specs = (P("pipe", "expert", "dp"), P("pipe", "expert", "dp"))
    return jax.shard_map(local, mesh=mesh, in_specs=in_specs, out_specs=out_specs, check_vma=False)
```

time: 226 us -> 201 us (0.89)
  starting transfers between devices: 82.3 us -> 69.4 us
  local copies, waits for them, and re-layouts: 22.4 us -> 10.6 us
  waiting for transfers between devices: 81.3 us -> 78.5 us
  Pallas kernels: 37.5 us -> 40.2 us
    ppermute x22 -> x14, starting transfers between devices: 45.1 us -> 37.4 us  [shifted(): lax.ppermute(array, axis, [(i, (i + by) % count) for i in range(count)])]
    slice x8 -> x0, local copies, waits for them, and re-layouts: 6.65 us -> none  [the longest x3 2.84 us: gather_quarters(): far_bottom = shifted(right[half:], 'dp', -1)]
    all_to_all x5 -> x4, starting transfers between devices: 37.2 us -> 32 us  [exchange(): lax.all_to_all(blocks, 'expert', split_axis=0, concat_axis=0, tiled=True)]
    unnamed x40 -> x28, local copies, waits for them, and re-layouts: 15.8 us -> 10.6 us
    all_to_all x5 -> x4, waiting for transfers between devices: 34.9 us -> 31.1 us  [exchange(): lax.all_to_all(blocks, 'expert', split_axis=0, concat_axis=0, tiled=True)]
    pallas_call x1, Pallas kernels: 7.49 us -> 10.1 us  [forward_hidden(): pl.pallas_call(forward_hidden_kernel, grid_spec=pltpu.PrefetchScalarGridS...]
    ppermute x22 -> x14, waiting for transfers between devices: 46.5 us -> 47.3 us  [shifted(): lax.ppermute(array, axis, [(i, (i + by) % count) for i in range(count)])]
    pallas_call x6 -> x7, Pallas kernels: 20.1 us -> 19.6 us  [the longest x1 6.93 us: backward_early(): pl.pallas_call(backward_early_kernel, grid_spec=pltpu.PrefetchScalarGridS...]
  transfers between devices with their start and end apart: 27 -> 18, of which waited for: 15 -> 9; matrix products, arithmetic and copies ran while one was open for 3% -> 0% of each run, Pallas kernels for 16% -> 18%
where the time goes in v2:
time: 201 us
  waiting for transfers between devices  78.5 us (39%)
  starting transfers between devices  69.4 us (35%)
  Pallas kernels  40.2 us (20%)
  local copies, waits for them, and re-layouts  10.6 us (5%)
    ppermute x14, waiting for transfers between devices, shifted(): lax.ppermute(array, axis, [(i, (i + by) % count) for i in range(count)])  47.3 us
    ppermute x14, starting transfers between devices, shifted(): lax.ppermute(array, axis, [(i, (i + by) % count) for i in range(count)])  37.4 us
    all_to_all x4, starting transfers between devices, exchange(): lax.all_to_all(blocks, 'expert', split_axis=0, concat_axis=0, tiled=True)  32 us
    all_to_all x4, waiting for transfers between devices, exchange(): lax.all_to_all(blocks, 'expert', split_axis=0, concat_axis=0, tiled=True)  31.1 us
    unnamed x28, local copies, waits for them, and re-layouts  10.6 us
    pallas_call x1, Pallas kernels, forward_hidden(): pl.pallas_call(forward_hidden_kernel, grid_spec=pltpu.PrefetchScalarGridS...  10.1 us
    pallas_call x1, Pallas kernels, backward_early(): pl.pallas_call(backward_early_kernel, grid_spec=pltpu.PrefetchScalarGridS...  6.93 us
  transfers between devices with their start and end apart: 18, of which 9 were waited for; matrix products, arithmetic and copies ran while one was open for 0% of the time, Pallas kernels for 18%

profile of v2, /device:TPU:1, one launch (start us, length us, event | category | flops | bytes accessed | tf_op | source)
XLA Modules:
  0.0 200.7 jit_solution(15014268576614014580)
XLA Ops:
  0.7 1.3 and_select_fusion.order_ref.rank_ref
  1.9 3.5 %shard_map.127 = bf16[384,1792]{1,0:T(8,128)(2,1)} custom-call(s32[4]{0:T(128)} %and_select_fusion.order_ref.rank_ref, s32[2,128]{1,0:T(2,128)} %bitcast.51, f32[2,128]{1,0:T(2,128)} %bitcast.58, bf16[128,896]{1,0:T(8,128)(2,1)} %bitcast.47, bf16[128,3584]{1,0:T(8,128)(2,1)} %bitcast.57), custom_call_target="tpu_custom_call" | custom-call | flops 176160768 | bytes 2752512 | tf_op jit(solution)/shard_map/pallas_call | solution.py:111
  5.4 10.1 %all-to-all-start.2 = ((bf16[16,24,1792]{2,1,0:T(8,128)(2,1)}), bf16[16,24,1792]{2,1,0:T(8,128)(2,1)S(1)}, u32[]{:S(2)}, u32[]{:S(2)}) async-start(bf16[16,24,1792]{2,1,0:T(8,128)(2,1)} %bitcast.56), calls=%async_computation.2 | async-start | bytes 2752512 | tf_op jit(solution)/shard_map/all_to_all | solution.py:450
  15.6 2.5 %shard_map.122 = bf16[384,3584]{1,0:T(8,128)(2,1)} custom-call(s32[2,128]{1,0:T(2,128)S(1)} %bitcast.53, bf16[128,3584]{1,0:T(8,128)(2,1)S(1)} %bitcast.43), custom_call_target="tpu_custom_call" | custom-call | flops 352321536 | bytes 5505024 | tf_op jit(solution)/shard_map/pallas_call | solution.py:88
  18.1 28.8 %all-to-all-done.2 = bf16[16,24,1792]{2,1,0:T(8,128)(2,1)S(1)} async-done(((bf16[16,24,1792]{2,1,0:T(8,128)(2,1)}), bf16[16,24,1792]{2,1,0:T(8,128)(2,1)S(1)}, u32[]{:S(2)}, u32[]{:S(2)}) %all-to-all-start.2) | async-done | bytes 1376288 | tf_op jit(solution)/shard_map/all_to_all | solution.py:450
  46.9 7.4 %all-to-all-start = ((bf16[16,24,3584]{2,1,0:T(8,128)(2,1)}), bf16[16,24,3584]{2,1,0:T(8,128)(2,1)}, u32[]{:S(2)}, u32[]{:S(2)}) async-start(bf16[16,24,3584]{2,1,0:T(8,128)(2,1)} %bitcast.6), calls=%async_computation | async-start | bytes 5505024 | tf_op jit(solution)/shard_map/all_to_all | solution.py:450
  54.3 0.0 copy-start.6
  54.3 2.6 %collective-permute-start.6 = (bf16[384,1792]{1,0:T(8,128)(2,1)S(1)}, bf16[384,1792]{1,0:T(8,128)(2,1)S(1)}, u32[]{:S(2)}, u32[]{:S(2)}) collective-permute-start(bf16[384,1792]{1,0:T(8,128)(2,1)S(1)} %bitcast.40), channel_id=1, source_target_pairs={{0,3},{1,0},{2,1},{3,2},{4,7},{5,4},{6,5},{7,6},{8,11},{9,8},{10,9... | collective-permute-start | bytes 4128776 | tf_op jit(solution)/shard_map/ppermute | solution.py:17
  56.9 27.3 %collective-permute-done.6.bottom_ref.right = bf16[384,1792]{1,0:T(8,128)(2,1)S(1)} collective-permute-done((bf16[384,1792]{1,0:T(8,128)(2,1)S(1)}, bf16[384,1792]{1,0:T(8,128)(2,1)S(1)}, u32[]{:S(2)}, u32[]{:S(2)}) %collective-permute-start.6) | collective-permute-done | bytes 1376288 | tf_op jit(solution)/shard_map/ppermute | solution.py:17
  84.1 3.2 %collective-permute-done.5.top_ref.left = bf16[384,1792]{1,0:T(8,128)(2,1)S(1)} collective-permute-done((bf16[384,1792]{1,0:T(8,128)(2,1)S(1)}, bf16[384,1792]{1,0:T(8,128)(2,1)S(1)}, u32[]{:S(2)}, u32[]{:S(2)}) %collective-permute-start.5) | collective-permute-done | bytes 1376288 | tf_op jit(solution)/shard_map/ppermute | solution.py:17
  87.4 0.1 shard_map.128
  87.5 0.1 collective-permute-start.7
  87.6 2.7 %collective-permute-start.8 = (bf16[192,1792]{1,0:T(8,128)(2,1)S(1)}, bf16[192,1792]{1,0:T(8,128)(2,1)S(1)}, u32[]{:S(2)}, u32[]{:S(2)}) collective-permute-start(bf16[192,1792]{1,0:T(8,128)(2,1)S(1)} %get-tuple-element.29), channel_id=1, source_target_pairs={{0,3},{1,0},{2,1},{3,2},{4,7},{5,4},{6,5},{7,6},{8,11},{9,8},{10,9... | collective-permute-start | bytes 2064392 | tf_op jit(solution)/shard_map/ppermute | solution.py:17
  90.2 2.0 %copy-done = bf16[1,1,3584,512]{3,2,1,0:T(8,128)(2,1)S(1)} copy-done((bf16[1,1,3584,512]{3,2,1,0:T(8,128)(2,1)S(1)}, bf16[1,1,3584,512]{3,2,1,0:T(8,128)(2,1)}, u32[]{:S(2)}) %copy-start) | copy-done | bytes 3670040
  92.3 2.0 %copy-done.1 = bf16[1,1,3584,512]{3,2,1,0:T(8,128)(2,1)S(1)} copy-done((bf16[1,1,3584,512]{3,2,1,0:T(8,128)(2,1)S(1)}, bf16[1,1,3584,512]{3,2,1,0:T(8,128)(2,1)}, u32[]{:S(2)}) %copy-start.1) | copy-done | bytes 3670040
  94.3 2.0 %copy-done.2 = bf16[1,1,512,3584]{3,2,1,0:T(8,128)(2,1)S(1)} copy-done((bf16[1,1,512,3584]{3,2,1,0:T(8,128)(2,1)S(1)}, bf16[1,1,512,3584]{3,2,1,0:T(8,128)(2,1)}, u32[]{:S(2)}) %copy-start.2) | copy-done | bytes 3670040
  96.3 6.9 %shard_map.129 = (f32[384,512]{1,0:T(8,128)S(1)}, f32[384,512]{1,0:T(8,128)S(1)}, f32[384,512]{1,0:T(8,128)S(1)}) custom-call(s32[4]{0:T(128)S(1)} %copy-done.6, bf16[384,1792]{1,0:T(8,128)(2,1)S(1)} %bitcast.42, bf16[384,1792]{1,0:T(8,128)(2,1)S(1)} %collective-permute-done.5.top_ref.left, bf16[384,1792]{1,0:T(8,128)(2,1)S(1)} %collective-permute-done.6.bottom_ref.right, ...), custom_call_target="tpu_custom_call" | custom-call | flops 3170893824 | bytes 8257536 | tf_op jit(solution)/shard_map/pallas_call | solution.py:239
  103.3 3.1 %shard_map.130 = (bf16[384,512]{1,0:T(8,128)(2,1)S(1)}, bf16[384,512]{1,0:T(8,128)(2,1)S(1)}, bf16[192,896]{1,0:T(8,128)(2,1)S(1)}, bf16[192,896]{1,0:T(8,128)(2,1)S(1)}) custom-call(s32[4]{0:T(128)S(1)} %copy-done.6, bf16[192,1792]{1,0:T(8,128)(2,1)S(1)} %collective-permute-done.7.top, bf16[192,1792]{1,0:T(8,128)(2,1)S(1)} %collective-permute-done.8.bottom, ...), custom_call_target="tpu_custom_call" | custom-call | flops 1761607680 | bytes 2752512 | tf_op jit(solution)/shard_map/pallas_call | solution.py:287
  106.4 1.6 collective-permute-start.9
  108.1 3.9 %shard_map.131 = (bf16[384,896]{1,0:T(8,128)(2,1)S(1)}, bf16[384,896]{1,0:T(8,128)(2,1)S(1)}, bf16[384,896]{1,0:T(8,128)(2,1)S(1)}) custom-call(s32[4]{0:T(128)S(1)} %copy-done.6, bf16[384,512]{1,0:T(8,128)(2,1)S(1)} %get-tuple-element.33.d_gate_ref, bf16[384,512]{1,0:T(8,128)(2,1)S(1)} %get-tuple-element.34.d_up_ref, bf16[3584,512]{1,0:T(8,128)(2,1)S(1)} %bitcast.31, ...), custom_call_target="tpu_custom_call" | custom-call | flops 2113929216 | bytes 7569408 | tf_op jit(solution)/shard_map/pallas_call | solution.py:398
  111.9 1.1 collective-permute-done.9.top_ref
  113.0 2.8 %collective-permute-done.10.bottom_ref = bf16[192,896]{1,0:T(8,128)(2,1)S(1)} collective-permute-done((bf16[192,896]{1,0:T(8,128)(2,1)S(1)}, bf16[192,896]{1,0:T(8,128)(2,1)S(1)}, u32[]{:S(2)}, u32[]{:S(2)}) %collective-permute-start.10) | collective-permute-done | bytes 344096 | tf_op jit(solution)/shard_map/ppermute | solution.py:17
  115.8 1.0 shard_map.132
  116.7 1.5 collective-permute-start.12
  118.2 10.1 %shard_map.123 = (bf16[384,512]{1,0:T(8,128)(2,1)}, bf16[192,896]{1,0:T(8,128)(2,1)}, bf16[192,896]{1,0:T(8,128)(2,1)}) custom-call(s32[4]{0:T(128)} %and_select_fusion.order_ref.rank_ref, bf16[384,3584]{1,0:T(8,128)(2,1)} %bitcast.7.rows_ref, bf16[3584,512]{1,0:T(8,128)(2,1)} %bitcast.28, bf16[3584,512]{1,0:T(8,128)(2,1)} %bitcast.32, ...), custom_call_target="tpu_custom_call" | custom-call | flops 3170893824 | bytes 8257536 | tf_op jit(solution)/shard_map/pallas_call | solution.py:322
  128.3 0.1 collective-permute-start.1
  128.4 2.6 %collective-permute-start = (bf16[192,896]{1,0:T(8,128)(2,1)}, bf16[192,896]{1,0:T(8,128)(2,1)}, u32[]{:S(2)}, u32[]{:S(2)}) collective-permute-start(bf16[192,896]{1,0:T(8,128)(2,1)} %get-tuple-element.23.refs_0_), channel_id=1, source_target_pairs={{0,3},{1,0},{2,1},{3,2},{4,7},{5,4},{6,5},{7,6},{8,11},{9,8},{10,9... | collective-permute-start | bytes 1032200 | tf_op jit(solution)/shard_map/ppermute | solution.py:17
  131.0 1.0 copy-done.12
  132.0 2.3 %shard_map.133 = bf16[384,896]{1,0:T(8,128)(2,1)} custom-call(bf16[384,896]{1,0:T(8,128)(2,1)S(1)} %get-tuple-element.35.a_ref, bf16[384,896]{1,0:T(8,128)(2,1)S(1)} %collective-permute-done.11.b_ref, bf16[384,896]{1,0:T(8,128)(2,1)} %collective-permute-done.12.c_ref, bf16[192,896]{1,0:T(8,128)(2,1)S(1)} %copy-done.12), custom_call_target="tpu_custom_call" | custom-call | flops 20000000000 | tf_op jit(solution)/shard_map/pallas_call | solution.py:436
  134.3 6.9 %all-to-all-start.3 = ((bf16[16,24,896]{2,1,0:T(8,128)(2,1)}), bf16[16,24,896]{2,1,0:T(8,128)(2,1)S(1)}, u32[]{:S(2)}, u32[]{:S(2)}) async-start(bf16[16,24,896]{2,1,0:T(8,128)(2,1)} %bitcast.23), calls=%async_computation.3 | async-start | bytes 1376256 | tf_op jit(solution)/shard_map/all_to_all | solution.py:450
  141.3 0.0 copy-start.3
  141.3 2.0 %copy-done.3 = bf16[1,1,512,3584]{3,2,1,0:T(8,128)(2,1)S(1)} copy-done((bf16[1,1,512,3584]{3,2,1,0:T(8,128)(2,1)S(1)}, bf16[1,1,512,3584]{3,2,1,0:T(8,128)(2,1)}, u32[]{:S(2)}) %copy-start.3) | copy-done | bytes 3670040
  143.3 3.9 %shard_map.124 = (bf16[384,896]{1,0:T(8,128)(2,1)S(1)}, bf16[384,896]{1,0:T(8,128)(2,1)S(1)}, bf16[384,896]{1,0:T(8,128)(2,1)S(1)}) custom-call(s32[4]{0:T(128)S(1)} %copy-done.7, bf16[384,512]{1,0:T(8,128)(2,1)S(1)} %copy-done.11, bf16[512,3584]{1,0:T(8,128)(2,1)S(1)} %bitcast.39, bf16[192,896]{1,0:T(8,128)(2,1)} %collective-permute-done.top_ref, ...), custom_call_target="tpu_custom_call" | custom-call | flops 40000000000 | tf_op jit(solution)/shard_map/pallas_call | solution.py:365
  147.2 0.0 copy-start.8
  147.2 0.3 collective-permute-start.2
  147.5 1.3 collective-permute-start.3
  148.8 8.6 %collective-permute-done.2.b_ref = bf16[384,896]{1,0:T(8,128)(2,1)S(1)} collective-permute-done((bf16[384,896]{1,0:T(8,128)(2,1)S(1)}, bf16[384,896]{1,0:T(8,128)(2,1)S(1)}, u32[]{:S(2)}, u32[]{:S(2)}) %collective-permute-start.2) | collective-permute-done | bytes 688160 | tf_op jit(solution)/shard_map/ppermute | solution.py:17
  157.4 1.4 collective-permute-done.3.c_ref
  158.8 1.1 shard_map.125
  159.9 7.6 %all-to-all-start.1 = ((bf16[16,24,896]{2,1,0:T(8,128)(2,1)}), bf16[16,24,896]{2,1,0:T(8,128)(2,1)S(1)}, u32[]{:S(2)}, u32[]{:S(2)}) async-start(bf16[16,24,896]{2,1,0:T(8,128)(2,1)} %bitcast.11), calls=%async_computation.1 | async-start | bytes 1376256 | tf_op jit(solution)/shard_map/all_to_all | solution.py:450
  167.5 0.6 shard_map.134
  168.1 10.5 %collective-permute-start.13 = (bf16[1,128,896]{2,1,0:T(8,128)(2,1)S(1)}, bf16[1,128,896]{2,1,0:T(8,128)(2,1)S(1)}, u32[]{:S(2)}, u32[]{:S(2)}) collective-permute-start(bf16[1,128,896]{2,1,0:T(8,128)(2,1)S(1)} %bitcast.50), channel_id=1, source_target_pairs={{0,192},{64,0},{128,64},{192,128},{1,193},{65,1},{129,65},{193,129... | collective-permute-start | bytes 688136 | tf_op jit(solution)/shard_map/ppermute | solution.py:17
  178.6 2.3 %all-to-all-done.1 = bf16[16,24,896]{2,1,0:T(8,128)(2,1)S(1)} async-done(((bf16[16,24,896]{2,1,0:T(8,128)(2,1)}), bf16[16,24,896]{2,1,0:T(8,128)(2,1)S(1)}, u32[]{:S(2)}, u32[]{:S(2)}) %all-to-all-start.1) | async-done | bytes 688160 | tf_op jit(solution)/shard_map/all_to_all | solution.py:450
  180.9 1.2 shard_map.126
  182.2 14.2 %collective-permute-start.4 = (bf16[1,128,896]{2,1,0:T(8,128)(2,1)S(1)}, bf16[1,128,896]{2,1,0:T(8,128)(2,1)S(1)}, u32[]{:S(2)}, u32[]{:S(2)}) collective-permute-start(bf16[1,128,896]{2,1,0:T(8,128)(2,1)S(1)} %bitcast.49), channel_id=1, source_target_pairs={{0,64},{64,128},{128,192},{192,0},{1,65},{65,129},{129,193},{193,1... | collective-permute-start | bytes 688136 | tf_op jit(solution)/shard_map/ppermute | solution.py:17
  196.4 3.0 %collective-permute-done.4 = bf16[1,128,896]{2,1,0:T(8,128)(2,1)S(1)} collective-permute-done((bf16[1,128,896]{2,1,0:T(8,128)(2,1)S(1)}, bf16[1,128,896]{2,1,0:T(8,128)(2,1)S(1)}, u32[]{:S(2)}, u32[]{:S(2)}) %collective-permute-start.4) | collective-permute-done | bytes 229408 | tf_op jit(solution)/shard_map/ppermute | solution.py:17
  199.3 0.7 copy.15
  200.0 0.7 copy.16
  (30 shorter events, 0.1 us)
Async XLA Ops:
  0.6 15.0 %copy-start.9 = (s32[1,128,2]{1,2,0:T(2,128)S(1)}, s32[1,128,2]{1,2,0:T(2,128)}, u32[]{:S(2)}) copy-start(s32[1,128,2]{1,2,0:T(2,128)} %param.12) | copy-start | bytes 3076
  0.6 15.0 %copy-start.4 = (bf16[1,128,3584]{2,1,0:T(8,128)(2,1)S(1)}, bf16[1,128,3584]{2,1,0:T(8,128)(2,1)}, u32[]{:S(2)}) copy-start(bf16[1,128,3584]{2,1,0:T(8,128)(2,1)} %param.11) | copy-start | bytes 2752516
  5.4 41.5 %all-to-all-start.2 = ((bf16[16,24,1792]{2,1,0:T(8,128)(2,1)}), bf16[16,24,1792]{2,1,0:T(8,128)(2,1)S(1)}, u32[]{:S(2)}, u32[]{:S(2)}) async-start(bf16[16,24,1792]{2,1,0:T(8,128)(2,1)} %bitcast.56), calls=%async_computation.2 | async-start | bytes 2752512 | tf_op jit(solution)/shard_map/all_to_all | solution.py:450
  46.9 71.3 %all-to-all-start = ((bf16[16,24,3584]{2,1,0:T(8,128)(2,1)}), bf16[16,24,3584]{2,1,0:T(8,128)(2,1)}, u32[]{:S(2)}, u32[]{:S(2)}) async-start(bf16[16,24,3584]{2,1,0:T(8,128)(2,1)} %bitcast.6), calls=%async_computation | async-start | bytes 5505024 | tf_op jit(solution)/shard_map/all_to_all | solution.py:450
  54.3 35.9 %copy-start.6 = (s32[4]{0:T(128)S(1)}, s32[4]{0:T(128)}, u32[]{:S(2)}) copy-start(s32[4]{0:T(128)} %and_select_fusion.order_ref.rank_ref) | copy-start | bytes 52
  54.3 29.8 %collective-permute-start.6 = (bf16[384,1792]{1,0:T(8,128)(2,1)S(1)}, bf16[384,1792]{1,0:T(8,128)(2,1)S(1)}, u32[]{:S(2)}, u32[]{:S(2)}) collective-permute-start(bf16[384,1792]{1,0:T(8,128)(2,1)S(1)} %bitcast.40), channel_id=1, source_target_pairs={{0,3},{1,0},{2,1},{3,2},{4,7},{5,4},{6,5},{7,6},{8,11},{9,8},{10,9... | collective-permute-start | bytes 4128776 | tf_op jit(solution)/shard_map/ppermute | solution.py:17
  56.9 30.5 %collective-permute-start.5 = (bf16[384,1792]{1,0:T(8,128)(2,1)S(1)}, bf16[384,1792]{1,0:T(8,128)(2,1)S(1)}, u32[]{:S(2)}, u32[]{:S(2)}) collective-permute-start(bf16[384,1792]{1,0:T(8,128)(2,1)S(1)} %bitcast.41), channel_id=1, source_target_pairs={{0,1},{1,2},{2,3},{3,0},{4,5},{5,6},{6,7},{7,4},{8,9},{9,10},{10,1... | collective-permute-start | bytes 4128776 | tf_op jit(solution)/shard_map/ppermute | solution.py:17
  87.5 15.8 %collective-permute-start.7 = (bf16[192,1792]{1,0:T(8,128)(2,1)S(1)}, bf16[192,1792]{1,0:T(8,128)(2,1)S(1)}, u32[]{:S(2)}, u32[]{:S(2)}) collective-permute-start(bf16[192,1792]{1,0:T(8,128)(2,1)S(1)} %get-tuple-element.28), channel_id=1, source_target_pairs={{0,1},{1,2},{2,3},{3,0},{4,5},{5,6},{6,7},{7,4},{8,9},{9,10},{10,1... | collective-permute-start | bytes 2064392 | tf_op jit(solution)/shard_map/ppermute | solution.py:17
  87.6 15.7 %collective-permute-start.8 = (bf16[192,1792]{1,0:T(8,128)(2,1)S(1)}, bf16[192,1792]{1,0:T(8,128)(2,1)S(1)}, u32[]{:S(2)}, u32[]{:S(2)}) collective-permute-start(bf16[192,1792]{1,0:T(8,128)(2,1)S(1)} %get-tuple-element.29), channel_id=1, source_target_pairs={{0,3},{1,0},{2,1},{3,2},{4,7},{5,4},{6,5},{7,6},{8,11},{9,8},{10,9... | collective-permute-start | bytes 2064392 | tf_op jit(solution)/shard_map/ppermute | solution.py:17
  90.2 2.0 %copy-start = (bf16[1,1,3584,512]{3,2,1,0:T(8,128)(2,1)S(1)}, bf16[1,1,3584,512]{3,2,1,0:T(8,128)(2,1)}, u32[]{:S(2)}) copy-start(bf16[1,1,3584,512]{3,2,1,0:T(8,128)(2,1)} %param.18) | copy-start | bytes 11010052
  92.3 2.0 %copy-start.1 = (bf16[1,1,3584,512]{3,2,1,0:T(8,128)(2,1)S(1)}, bf16[1,1,3584,512]{3,2,1,0:T(8,128)(2,1)}, u32[]{:S(2)}) copy-start(bf16[1,1,3584,512]{3,2,1,0:T(8,128)(2,1)} %param.19) | copy-start | bytes 11010052
  94.3 2.0 %copy-start.2 = (bf16[1,1,512,3584]{3,2,1,0:T(8,128)(2,1)S(1)}, bf16[1,1,512,3584]{3,2,1,0:T(8,128)(2,1)}, u32[]{:S(2)}) copy-start(bf16[1,1,512,3584]{3,2,1,0:T(8,128)(2,1)} %param.20) | copy-start | bytes 11010052
  106.4 6.6 %collective-permute-start.9 = (bf16[192,896]{1,0:T(8,128)(2,1)S(1)}, bf16[192,896]{1,0:T(8,128)(2,1)S(1)}, u32[]{:S(2)}, u32[]{:S(2)}) collective-permute-start(bf16[192,896]{1,0:T(8,128)(2,1)S(1)} %get-tuple-element.38), channel_id=1, source_target_pairs={{0,3},{1,0},{2,1},{3,2},{4,7},{5,4},{6,5},{7,6},{8,11},{9,8},{10,9... | collective-permute-start | bytes 1032200 | tf_op jit(solution)/shard_map/ppermute | solution.py:17
  108.1 7.7 %collective-permute-start.10 = (bf16[192,896]{1,0:T(8,128)(2,1)S(1)}, bf16[192,896]{1,0:T(8,128)(2,1)S(1)}, u32[]{:S(2)}, u32[]{:S(2)}) collective-permute-start(bf16[192,896]{1,0:T(8,128)(2,1)S(1)} %get-tuple-element.39), channel_id=1, source_target_pairs={{0,1},{1,2},{2,3},{3,0},{4,5},{5,6},{6,7},{7,4},{8,9},{9,10},{10,1... | collective-permute-start | bytes 1032200 | tf_op jit(solution)/shard_map/ppermute | solution.py:17
  116.7 14.3 %collective-permute-start.11 = (bf16[384,896]{1,0:T(8,128)(2,1)}, bf16[384,896]{1,0:T(8,128)(2,1)S(1)}, u32[]{:S(2)}, u32[]{:S(2)}) collective-permute-start(bf16[384,896]{1,0:T(8,128)(2,1)} %get-tuple-element.40), channel_id=1, source_target_pairs={{0,3},{1,0},{2,1},{3,2},{4,7},{5,4},{6,5},{7,6},{8,11},{9,8},{10,9... | collective-permute-start | bytes 2064392 | tf_op jit(solution)/shard_map/ppermute | solution.py:17
  116.7 14.3 %collective-permute-start.12 = (bf16[384,896]{1,0:T(8,128)(2,1)S(1)}, bf16[384,896]{1,0:T(8,128)(2,1)}, u32[]{:S(2)}, u32[]{:S(2)}) collective-permute-start(bf16[384,896]{1,0:T(8,128)(2,1)S(1)} %get-tuple-element.41), channel_id=1, source_target_pairs={{0,1},{1,2},{2,3},{3,0},{4,5},{5,6},{6,7},{7,4},{8,9},{9,10},{10,1... | collective-permute-start | bytes 2064392 | tf_op jit(solution)/shard_map/ppermute | solution.py:17
  128.3 12.9 %collective-permute-start.1 = (bf16[192,896]{1,0:T(8,128)(2,1)}, bf16[192,896]{1,0:T(8,128)(2,1)}, u32[]{:S(2)}, u32[]{:S(2)}) collective-permute-start(bf16[192,896]{1,0:T(8,128)(2,1)} %get-tuple-element.24), channel_id=1, source_target_pairs={{0,1},{1,2},{2,3},{3,0},{4,5},{5,6},{6,7},{7,4},{8,9},{9,10},{10,1... | collective-permute-start | bytes 1032200 | tf_op jit(solution)/shard_map/ppermute | solution.py:17
  128.4 12.9 %collective-permute-start = (bf16[192,896]{1,0:T(8,128)(2,1)}, bf16[192,896]{1,0:T(8,128)(2,1)}, u32[]{:S(2)}, u32[]{:S(2)}) collective-permute-start(bf16[192,896]{1,0:T(8,128)(2,1)} %get-tuple-element.23.refs_0_), channel_id=1, source_target_pairs={{0,3},{1,0},{2,1},{3,2},{4,7},{5,4},{6,5},{7,6},{8,11},{9,8},{10,9... | collective-permute-start | bytes 1032200 | tf_op jit(solution)/shard_map/ppermute | solution.py:17
  131.0 1.0 copy-start.12
  132.0 9.2 %copy-start.7 = (s32[4]{0:T(128)S(1)}, s32[4]{0:T(128)}, u32[]{:S(2)}) copy-start(s32[4]{0:T(128)} %and_select_fusion.order_ref.rank_ref) | copy-start | bytes 52
  132.0 9.3 %copy-start.11 = (bf16[384,512]{1,0:T(8,128)(2,1)S(1)}, bf16[384,512]{1,0:T(8,128)(2,1)}, u32[]{:S(2)}) copy-start(bf16[384,512]{1,0:T(8,128)(2,1)} %get-tuple-element.22.hidden_ref) | copy-start | bytes 1179652
  134.3 25.6 %all-to-all-start.3 = ((bf16[16,24,896]{2,1,0:T(8,128)(2,1)}), bf16[16,24,896]{2,1,0:T(8,128)(2,1)S(1)}, u32[]{:S(2)}, u32[]{:S(2)}) async-start(bf16[16,24,896]{2,1,0:T(8,128)(2,1)} %bitcast.23), calls=%async_computation.3 | async-start | bytes 1376256 | tf_op jit(solution)/shard_map/all_to_all | solution.py:450
  141.3 2.0 %copy-start.3 = (bf16[1,1,512,3584]{3,2,1,0:T(8,128)(2,1)S(1)}, bf16[1,1,512,3584]{3,2,1,0:T(8,128)(2,1)}, u32[]{:S(2)}) copy-start(bf16[1,1,512,3584]{3,2,1,0:T(8,128)(2,1)} %param.20) | copy-start | bytes 11010052
  147.2 20.3 %copy-start.5 = (bf16[1,128,896]{2,1,0:T(8,128)(2,1)S(1)}, bf16[1,128,896]{2,1,0:T(8,128)(2,1)}, u32[]{:S(2)}) copy-start(bf16[1,128,896]{2,1,0:T(8,128)(2,1)} %param.17) | copy-start | bytes 688132
  147.2 20.3 %copy-start.8 = (s32[1,128,2]{1,2,0:T(2,128)S(1)}, s32[1,128,2]{1,2,0:T(2,128)}, u32[]{:S(2)}) copy-start(s32[1,128,2]{1,2,0:T(2,128)} %param.15) | copy-start | bytes 3076
  147.2 10.2 %collective-permute-start.2 = (bf16[384,896]{1,0:T(8,128)(2,1)S(1)}, bf16[384,896]{1,0:T(8,128)(2,1)S(1)}, u32[]{:S(2)}, u32[]{:S(2)}) collective-permute-start(bf16[384,896]{1,0:T(8,128)(2,1)S(1)} %get-tuple-element.26), channel_id=1, source_target_pairs={{0,3},{1,0},{2,1},{3,2},{4,7},{5,4},{6,5},{7,6},{8,11},{9,8},{10,9... | collective-permute-start | bytes 2064392 | tf_op jit(solution)/shard_map/ppermute | solution.py:17
  147.5 11.3 %collective-permute-start.3 = (bf16[384,896]{1,0:T(8,128)(2,1)S(1)}, bf16[384,896]{1,0:T(8,128)(2,1)S(1)}, u32[]{:S(2)}, u32[]{:S(2)}) collective-permute-start(bf16[384,896]{1,0:T(8,128)(2,1)S(1)} %get-tuple-element.27), channel_id=1, source_target_pairs={{0,1},{1,2},{2,3},{3,0},{4,5},{5,6},{6,7},{7,4},{8,9},{9,10},{10,1... | collective-permute-start | bytes 2064392 | tf_op jit(solution)/shard_map/ppermute | solution.py:17
  158.8 22.2 %copy-start.10 = (f32[1,128,2]{1,2,0:T(2,128)S(1)}, f32[1,128,2]{1,2,0:T(2,128)}, u32[]{:S(2)}) copy-start(f32[1,128,2]{1,2,0:T(2,128)} %param.13) | copy-start | bytes 3076
  159.9 21.0 %all-to-all-start.1 = ((bf16[16,24,896]{2,1,0:T(8,128)(2,1)}), bf16[16,24,896]{2,1,0:T(8,128)(2,1)S(1)}, u32[]{:S(2)}, u32[]{:S(2)}) async-start(bf16[16,24,896]{2,1,0:T(8,128)(2,1)} %bitcast.11), calls=%async_computation.1 | async-start | bytes 1376256 | tf_op jit(solution)/shard_map/all_to_all | solution.py:450
  168.1 28.3 %collective-permute-start.13 = (bf16[1,128,896]{2,1,0:T(8,128)(2,1)S(1)}, bf16[1,128,896]{2,1,0:T(8,128)(2,1)S(1)}, u32[]{:S(2)}, u32[]{:S(2)}) collective-permute-start(bf16[1,128,896]{2,1,0:T(8,128)(2,1)S(1)} %bitcast.50), channel_id=1, source_target_pairs={{0,192},{64,0},{128,64},{192,128},{1,193},{65,1},{129,65},{193,129... | collective-permute-start | bytes 688136 | tf_op jit(solution)/shard_map/ppermute | solution.py:17
  182.2 17.2 %collective-permute-start.4 = (bf16[1,128,896]{2,1,0:T(8,128)(2,1)S(1)}, bf16[1,128,896]{2,1,0:T(8,128)(2,1)S(1)}, u32[]{:S(2)}, u32[]{:S(2)}) collective-permute-start(bf16[1,128,896]{2,1,0:T(8,128)(2,1)S(1)} %bitcast.49), channel_id=1, source_target_pairs={{0,64},{64,128},{128,192},{192,0},{1,65},{65,129},{129,193},{193,1... | collective-permute-start | bytes 688136 | tf_op jit(solution)/shard_map/ppermute | solution.py:17

commit v3 on v2

--- a/solution.py
+++ b/solution.py
@@ -93,38 +93,40 @@
     )(ids, source)
 
 
-def pack_pair_kernel(experts, capacity, order_ref, ids_ref, gates_ref, grad_ref, source_ref, out_ref):
+def pack_pair_kernel(experts, capacity, ids_ref, gates_ref, grad_ref, source_hbm, out_ref, source, sem):
+    quarter = grad_ref.shape[1]
+    start = pl.multiple_of(lax.axis_index("dp") * quarter, 128)
+    copy = pltpu.make_async_copy(source_hbm.at[:, pl.ds(start, quarter)], source, sem)
+    copy.start()
     hits = slot_hits(ids_ref[...], experts, capacity)
     chosen = one_hot(functools.reduce(jnp.logical_or, hits))
     gate = sum(
         jnp.sum(jnp.where(hit, gates_ref[k : k + 1], 0.0), axis=1, keepdims=True)
         for k, hit in enumerate(hits)
     )
-    quarter = grad_ref.shape[1]
     out_ref[:, :quarter] = (gate * dot(chosen, grad_ref[...])).astype(BF16)
-    out_ref[:, quarter:] = dot(chosen, source_ref[...]).astype(BF16)
-
-
-def pack_pair(order, ids, gates, grad, source, experts, capacity):
+    copy.wait()
+    out_ref[:, quarter:] = dot(chosen, source[...]).astype(BF16)
+
+
+def pack_pair(ids, gates, grad, source, experts, capacity):
     rows, quarter = grad.shape
     slots = experts * capacity
     return pl.pallas_call(
         functools.partial(pack_pair_kernel, experts, capacity),
-        grid_spec=pltpu.PrefetchScalarGridSpec(
-            num_scalar_prefetch=1,
-            grid=(1,),
-            in_specs=[
-                whole(ids.shape),
-                whole(gates.shape),
-                whole(grad.shape),
-                pl.BlockSpec((rows, quarter), lambda i, order: (0, order[0])),
-            ],
-            out_specs=whole((slots, 2 * quarter)),
-        ),
+        grid=(1,),
+        in_specs=[
+            whole(ids.shape),
+            whole(gates.shape),
+            whole(grad.shape),
+            pl.BlockSpec(memory_space=pl.ANY),
+        ],
+        out_specs=whole((slots, 2 * quarter)),
         out_shape=jax.ShapeDtypeStruct((slots, 2 * quarter), BF16),
+        scratch_shapes=[pltpu.VMEM((rows, quarter), BF16), pltpu.SemaphoreType.DMA],
         compiler_params=params(60),
         cost_estimate=cost(4 * slots * rows * quarter, 8 * slots * quarter),
-    )(order, ids, gates, grad, source)
+    )(ids, gates, grad, source)
 
 
 def token_hits(ids, experts, capacity):
@@ -203,11 +205,32 @@
     )(first, second)
 
 
+def held_kernel(*refs):
+    del refs
+
+
+def held(arrays, after):
+    place = pl.BlockSpec(memory_space=pl.ANY)
+    return pl.pallas_call(
+        held_kernel,
+        in_specs=[place] * (len(arrays) + len(after)),
+        out_specs=[place] * len(arrays),
+        out_shape=[jax.ShapeDtypeStruct(a.shape, a.dtype) for a in arrays],
+        input_output_aliases={i: i for i in range(len(arrays))},
+        compiler_params=params(24),
+        cost_estimate=cost(1, 1),
+    )(*arrays, *after)
+
+
 def fixed(shape):
     return pl.BlockSpec(shape, lambda *_: (0,) * len(shape), pipeline_mode=pl.Buffered(1))
 
 
 def accumulate(step, acc_ref, part):
+    if isinstance(step, int):
+        acc_ref[...] = part if step == 0 else acc_ref[...] + part
+        return
+
     @pl.when(step == 0)
     def _():
         acc_ref[...] = part
@@ -248,7 +271,7 @@
         ),
         out_shape=[jax.ShapeDtypeStruct((slots, width), F32)] * 3,
         compiler_params=params(32),
-        cost_estimate=cost(18 * slots * width * quarter, 18 * quarter * width),
+        cost_estimate=lasting(30),
     )(order, *blocks, gate_mat, up_mat, down_mat)
 
 
@@ -299,39 +322,58 @@
     )(order, *far, *accs, gate_mat, up_mat, down_mat)
 
 
-def forward_hidden_kernel(order_ref, rows_ref, gate_ref, up_ref, down_ref, *refs):
-    hidden_ref, top_out, bottom_out, gate_acc, up_acc = refs
-    step = pl.program_id(0)
-    accumulate(step, gate_acc, dot(rows_ref[...], gate_ref[...]))
-    accumulate(step, up_acc, dot(rows_ref[...], up_ref[...]))
-
-    @pl.when(step == pl.num_programs(0) - 1)
-    def _():
-        gate_pre = gate_acc[...]
-        hidden = (gate_pre * jax.nn.sigmoid(gate_pre) * up_acc[...]).astype(BF16)
-        hidden_ref[...] = hidden
-        split(dot(hidden, down_ref[...]), top_out, bottom_out)
+def forward_hidden_kernel(groups, order_ref, rows_hbm, gate_hbm, up_hbm, down_hbm, *refs):
+    hidden_ref, top_out, bottom_out, rows, gates, ups, down, gate_acc, up_acc, sems = refs
+    quarter = rows.shape[2]
+    far = pl.multiple_of(order_ref[groups - 1] * quarter, 128)
+    copies = []
+    for i in range(groups):
+        block = pl.ds(i * quarter, quarter)
+        copies.append(
+            [
+                pltpu.make_async_copy(rows_hbm.at[:, block], rows.at[i], sems.at[0, i]),
+                pltpu.make_async_copy(gate_hbm.at[block], gates.at[i], sems.at[1, i]),
+                pltpu.make_async_copy(up_hbm.at[block], ups.at[i], sems.at[2, i]),
+            ]
+        )
+    last = pltpu.make_async_copy(down_hbm.at[:, pl.ds(far, quarter)], down, sems.at[3, 0])
+    for group in copies:
+        for copy in group:
+            copy.start()
+    last.start()
+    for i, group in enumerate(copies):
+        for copy in group:
+            copy.wait()
+        accumulate(i, gate_acc, dot(rows[i], gates[i]))
+        accumulate(i, up_acc, dot(rows[i], ups[i]))
+    gate_pre = gate_acc[...]
+    hidden = (gate_pre * jax.nn.sigmoid(gate_pre) * up_acc[...]).astype(BF16)
+    hidden_ref[...] = hidden
+    last.wait()
+    split(dot(hidden, down[...]), top_out, bottom_out)
 
 
 def forward_hidden(order, rows, gate_mat, up_mat, down_mat, groups):
     slots, quarter = rows.shape[0], rows.shape[1] // groups
     width = gate_mat.shape[1]
-    weight = pl.BlockSpec((quarter, width), lambda i, order: (i, 0))
     wide = jax.ShapeDtypeStruct((slots, width), BF16)
     part = jax.ShapeDtypeStruct((slots // 2, quarter), BF16)
     return pl.pallas_call(
-        forward_hidden_kernel,
+        functools.partial(forward_hidden_kernel, groups),
         grid_spec=pltpu.PrefetchScalarGridSpec(
             num_scalar_prefetch=1,
-            grid=(groups,),
-            in_specs=[
-                pl.BlockSpec((slots, quarter), lambda i, order: (0, i)),
-                weight,
-                weight,
-                pl.BlockSpec((width, quarter), lambda i, order: (0, order[3])),
+            grid=(1,),
+            in_specs=[pl.BlockSpec(memory_space=pl.ANY)] * 4,
+            out_specs=[whole(wide.shape)] + [whole(part.shape)] * 2,
+            scratch_shapes=[
+                pltpu.VMEM((groups, slots, quarter), BF16),
+                pltpu.VMEM((groups, quarter, width), BF16),
+                pltpu.VMEM((groups, quarter, width), BF16),
+                pltpu.VMEM((width, quarter), BF16),
+                pltpu.VMEM((slots, width), F32),
+                pltpu.VMEM((slots, width), F32),
+                pltpu.SemaphoreType.DMA((4, groups)),
             ],
-            out_specs=[whole(wide.shape)] + [whole(part.shape)] * 2,
-            scratch_shapes=[pltpu.VMEM((slots, width), F32)] * 2,
         ),
         out_shape=[wide, part, part],
         compiler_params=params(60),
@@ -467,11 +509,11 @@
     fwd_ids, fwd_gates = ids_fwd[0].T, gates_fwd[0].T
     bwd_ids, bwd_gates = ids_bwd[0].T, gates_bwd[0].T
 
-    bwd_rows = pack_pair(
-        order, bwd_ids, bwd_gates, grad_in[0], x_bwd[0], experts, capacity
-    )
+    bwd_rows = pack_pair(bwd_ids, bwd_gates, grad_in[0], x_bwd[0], experts, capacity)
     bwd_rows = exchange(bwd_rows, experts)
-    fwd_rows = exchange(pack(fwd_ids, x_fwd[0], experts, capacity), experts)
+    fwd_rows = pack(fwd_ids, x_fwd[0], experts, capacity)
+    (bwd_rows,) = held((bwd_rows,), (fwd_rows,))
+    fwd_rows = exchange(fwd_rows, experts)
 
     left, right = shifted(bwd_rows, "dp", 1), shifted(bwd_rows, "dp", -1)
     top, bottom = halves(left, right)

time: 201 us -> 198 us (0.985)
  starting transfers between devices: 69.4 us -> 65.8 us
    all_to_all x4, waiting for transfers between devices: 31.1 us -> 42.8 us  [exchange(): lax.all_to_all(blocks, 'expert', split_axis=0, concat_axis=0, tiled=True)]
    ppermute x14, waiting for transfers between devices: 47.3 us -> 36.2 us  [shifted(): lax.ppermute(array, axis, [(i, (i + by) % count) for i in range(count)])]
    pallas_call x1 -> x2, Pallas kernels: 10.1 us -> 7.42 us  [the longest x1 7.42 us: forward_hidden(): pl.pallas_call(functools.partial(forward_hidden_kernel, groups), grid_spe...]
    ppermute x14, starting transfers between devices: 37.4 us -> 35.3 us  [shifted(): lax.ppermute(array, axis, [(i, (i + by) % count) for i in range(count)])]
    unnamed x28 -> x30, local copies, waits for them, and re-layouts: 10.6 us -> 10.6 us
  transfers between devices with their start and end apart: 18 -> 18, of which waited for: 9 -> 10; matrix products, arithmetic and copies ran while one was open for 0% -> 0% of each run, Pallas kernels for 18% -> 19%
where the time goes in v3:
time: 198 us; the launch traced here: 197 us
  waiting for transfers between devices  79 us (40%)
  starting transfers between devices  65.8 us (33%)
  Pallas kernels  40.5 us (20%)
  local copies, waits for them, and re-layouts  10.6 us (5%)
    all_to_all x4, waiting for transfers between devices, exchange(): lax.all_to_all(blocks, 'expert', split_axis=0, concat_axis=0, tiled=True)  42.8 us
    ppermute x14, waiting for transfers between devices, shifted(): lax.ppermute(array, axis, [(i, (i + by) % count) for i in range(count)])  36.2 us
    ppermute x14, starting transfers between devices, shifted(): lax.ppermute(array, axis, [(i, (i + by) % count) for i in range(count)])  35.3 us
    all_to_all x4, starting transfers between devices, exchange(): lax.all_to_all(blocks, 'expert', split_axis=0, concat_axis=0, tiled=True)  30.6 us
    unnamed x30, local copies, waits for them, and re-layouts  10.6 us
    pallas_call x1, Pallas kernels, backward_early(): pl.pallas_call(backward_early_kernel, grid_spec=pltpu.PrefetchScalarGridS...  8.6 us
    pallas_call x1, Pallas kernels, forward_hidden(): pl.pallas_call(functools.partial(forward_hidden_kernel, groups), grid_spe...  7.42 us
  transfers between devices with their start and end apart: 18, of which 10 were waited for; matrix products, arithmetic and copies ran while one was open for 0% of the time, Pallas kernels for 19%

profile of v3, /device:TPU:1, one launch (start us, length us, event | category | flops | bytes accessed | tf_op | source)
XLA Modules:
  0.0 196.8 jit_solution(2716027939014855304)
XLA Ops:
  0.7 3.5 %shard_map.127 = bf16[384,1792]{1,0:T(8,128)(2,1)} custom-call(s32[2,128]{1,0:T(2,128)} %bitcast.49, f32[2,128]{1,0:T(2,128)} %bitcast.56, bf16[128,896]{1,0:T(8,128)(2,1)} %bitcast.45, bf16[128,3584]{1,0:T(8,128)(2,1)} %bitcast.55), custom_call_target="tpu_custom_call" | custom-call | flops 176160768 | bytes 2752512 | tf_op jit(solution)/shard_map/pallas_call | solution.py:115
  4.2 10.1 %all-to-all-start.2 = ((bf16[16,24,1792]{2,1,0:T(8,128)(2,1)}), bf16[16,24,1792]{2,1,0:T(8,128)(2,1)S(1)}, u32[]{:S(2)}, u32[]{:S(2)}) async-start(bf16[16,24,1792]{2,1,0:T(8,128)(2,1)} %bitcast.54), calls=%async_computation.2 | async-start | bytes 2752512 | tf_op jit(solution)/shard_map/all_to_all | solution.py:492
  14.3 2.6 %shard_map.122.refs_1_ = bf16[384,3584]{1,0:T(8,128)(2,1)} custom-call(s32[2,128]{1,0:T(2,128)S(1)} %bitcast.51, bf16[128,3584]{1,0:T(8,128)(2,1)S(1)} %bitcast.41), custom_call_target="tpu_custom_call" | custom-call | flops 352321536 | bytes 5505024 | tf_op jit(solution)/shard_map/pallas_call | solution.py:88
  16.9 28.8 %all-to-all-done.2 = bf16[16,24,1792]{2,1,0:T(8,128)(2,1)S(1)} async-done(((bf16[16,24,1792]{2,1,0:T(8,128)(2,1)}), bf16[16,24,1792]{2,1,0:T(8,128)(2,1)S(1)}, u32[]{:S(2)}, u32[]{:S(2)}) %all-to-all-start.2) | async-done | bytes 1376288 | tf_op jit(solution)/shard_map/all_to_all | solution.py:492
  45.7 2.5 %collective-permute-start.6 = (bf16[384,1792]{1,0:T(8,128)(2,1)S(1)}, bf16[384,1792]{1,0:T(8,128)(2,1)}, u32[]{:S(2)}, u32[]{:S(2)}) collective-permute-start(bf16[384,1792]{1,0:T(8,128)(2,1)S(1)} %shard_map.128.own), channel_id=1, source_target_pairs={{0,3},{1,0},{2,1},{3,2},{4,7},{5,4},{6,5},{7,6},{8,11},{9,8},{10,9... | collective-permute-start | bytes 4128776 | tf_op jit(solution)/shard_map/ppermute | solution.py:17
  48.1 7.5 %all-to-all-start = ((bf16[16,24,3584]{2,1,0:T(8,128)(2,1)}), bf16[16,24,3584]{2,1,0:T(8,128)(2,1)}, u32[]{:S(2)}, u32[]{:S(2)}) async-start(bf16[16,24,3584]{2,1,0:T(8,128)(2,1)} %bitcast.6), calls=%async_computation | async-start | bytes 5505024 | tf_op jit(solution)/shard_map/all_to_all | solution.py:492
  55.7 16.8 %collective-permute-done.6.bottom_ref.right = bf16[384,1792]{1,0:T(8,128)(2,1)} collective-permute-done((bf16[384,1792]{1,0:T(8,128)(2,1)S(1)}, bf16[384,1792]{1,0:T(8,128)(2,1)}, u32[]{:S(2)}, u32[]{:S(2)}) %collective-permute-start.6) | collective-permute-done | bytes 1376288 | tf_op jit(solution)/shard_map/ppermute | solution.py:17
  72.5 3.2 %collective-permute-done.5.top_ref.left = bf16[384,1792]{1,0:T(8,128)(2,1)} collective-permute-done((bf16[384,1792]{1,0:T(8,128)(2,1)S(1)}, bf16[384,1792]{1,0:T(8,128)(2,1)}, u32[]{:S(2)}, u32[]{:S(2)}) %collective-permute-start.5) | collective-permute-done | bytes 1376288 | tf_op jit(solution)/shard_map/ppermute | solution.py:17
  75.7 1.4 shard_map.129
  77.1 0.1 collective-permute-start.7
  77.2 2.7 %collective-permute-start.8 = (bf16[192,1792]{1,0:T(8,128)(2,1)S(1)}, bf16[192,1792]{1,0:T(8,128)(2,1)S(1)}, u32[]{:S(2)}, u32[]{:S(2)}) collective-permute-start(bf16[192,1792]{1,0:T(8,128)(2,1)S(1)} %get-tuple-element.29), channel_id=1, source_target_pairs={{0,3},{1,0},{2,1},{3,2},{4,7},{5,4},{6,5},{7,6},{8,11},{9,8},{10,9... | collective-permute-start | bytes 2064392 | tf_op jit(solution)/shard_map/ppermute | solution.py:17
  79.9 2.0 %copy-done = bf16[1,1,3584,512]{3,2,1,0:T(8,128)(2,1)S(1)} copy-done((bf16[1,1,3584,512]{3,2,1,0:T(8,128)(2,1)S(1)}, bf16[1,1,3584,512]{3,2,1,0:T(8,128)(2,1)}, u32[]{:S(2)}) %copy-start) | copy-done | bytes 3670040
  81.9 2.0 %copy-done.1 = bf16[1,1,3584,512]{3,2,1,0:T(8,128)(2,1)S(1)} copy-done((bf16[1,1,3584,512]{3,2,1,0:T(8,128)(2,1)S(1)}, bf16[1,1,3584,512]{3,2,1,0:T(8,128)(2,1)}, u32[]{:S(2)}) %copy-start.1) | copy-done | bytes 3670040
  83.9 2.0 %copy-done.2 = bf16[1,1,512,3584]{3,2,1,0:T(8,128)(2,1)S(1)} copy-done((bf16[1,1,512,3584]{3,2,1,0:T(8,128)(2,1)S(1)}, bf16[1,1,512,3584]{3,2,1,0:T(8,128)(2,1)}, u32[]{:S(2)}) %copy-start.2) | copy-done | bytes 3670040
  86.0 8.6 %shard_map.130 = (f32[384,512]{1,0:T(8,128)S(1)}, f32[384,512]{1,0:T(8,128)S(1)}, f32[384,512]{1,0:T(8,128)S(1)}) custom-call(s32[4]{0:T(128)S(1)} %and_select_fusion.order_ref.rank_ref, bf16[384,1792]{1,0:T(8,128)(2,1)S(1)} %shard_map.128.own, bf16[384,1792]{1,0:T(8,128)(2,1)} %collective-permute-done.5.top_ref.left, ...), custom_call_target="tpu_custom_call" | custom-call | flops 30000001024 | tf_op jit(solution)/shard_map/pallas_call | solution.py:262
  94.6 3.1 %shard_map.131 = (bf16[384,512]{1,0:T(8,128)(2,1)S(1)}, bf16[384,512]{1,0:T(8,128)(2,1)S(1)}, bf16[192,896]{1,0:T(8,128)(2,1)S(1)}, bf16[192,896]{1,0:T(8,128)(2,1)S(1)}) custom-call(s32[4]{0:T(128)S(1)} %and_select_fusion.order_ref.rank_ref, bf16[192,1792]{1,0:T(8,128)(2,1)S(1)} %collective-permute-done.7.top, ...), custom_call_target="tpu_custom_call" | custom-call | flops 1761607680 | bytes 2752512 | tf_op jit(solution)/shard_map/pallas_call | solution.py:310
  97.7 0.1 collective-permute-start.9
  97.8 1.5 collective-permute-start.10
  99.3 3.9 %shard_map.132 = (bf16[384,896]{1,0:T(8,128)(2,1)S(1)}, bf16[384,896]{1,0:T(8,128)(2,1)S(1)}, bf16[384,896]{1,0:T(8,128)(2,1)S(1)}) custom-call(s32[4]{0:T(128)S(1)} %and_select_fusion.order_ref.rank_ref, bf16[384,512]{1,0:T(8,128)(2,1)S(1)} %get-tuple-element.33.d_gate_ref, bf16[384,512]{1,0:T(8,128)(2,1)S(1)} %get-tuple-element.34.d_up_ref, ...), custom_call_target="tpu_custom_call" | custom-call | flops 2113929216 | bytes 7569408 | tf_op jit(solution)/shard_map/pallas_call | solution.py:440
  103.1 1.2 collective-permute-done.9.top_ref
  104.3 1.3 collective-permute-done.10.bottom_ref
  105.6 1.0 shard_map.133
  106.6 1.5 collective-permute-start.12
  108.0 10.5 %all-to-all-done = bf16[16,24,3584]{2,1,0:T(8,128)(2,1)} async-done(((bf16[16,24,3584]{2,1,0:T(8,128)(2,1)}), bf16[16,24,3584]{2,1,0:T(8,128)(2,1)}, u32[]{:S(2)}, u32[]{:S(2)}) %all-to-all-start) | async-done | bytes 2752544 | tf_op jit(solution)/shard_map/all_to_all | solution.py:492
  118.5 7.4 %shard_map.123 = (bf16[384,512]{1,0:T(8,128)(2,1)}, bf16[192,896]{1,0:T(8,128)(2,1)}, bf16[192,896]{1,0:T(8,128)(2,1)}) custom-call(s32[4]{0:T(128)} %copy-done.6, bf16[384,3584]{1,0:T(8,128)(2,1)} %bitcast.7.rows_hbm, bf16[3584,512]{1,0:T(8,128)(2,1)} %bitcast.28, bf16[3584,512]{1,0:T(8,128)(2,1)} %bitcast.32, bf16[512,3584]{1,0:T(8,128)(2,1)} %bitcast.36), custom_call_target="tpu_custom_call" | custom-call | flops 3170893824 | bytes 8257536 | tf_op jit(solution)/shard_map/pallas_call | solution.py:361
  125.9 0.5 collective-permute-start.1
  126.5 2.6 %collective-permute-start = (bf16[192,896]{1,0:T(8,128)(2,1)}, bf16[192,896]{1,0:T(8,128)(2,1)}, u32[]{:S(2)}, u32[]{:S(2)}) collective-permute-start(bf16[192,896]{1,0:T(8,128)(2,1)} %get-tuple-element.23.refs_0_), channel_id=1, source_target_pairs={{0,3},{1,0},{2,1},{3,2},{4,7},{5,4},{6,5},{7,6},{8,11},{9,8},{10,9... | collective-permute-start | bytes 1032200 | tf_op jit(solution)/shard_map/ppermute | solution.py:17
  129.0 1.0 copy-done.12
  130.0 2.3 %shard_map.134 = bf16[384,896]{1,0:T(8,128)(2,1)} custom-call(bf16[384,896]{1,0:T(8,128)(2,1)S(1)} %get-tuple-element.35.a_ref, bf16[384,896]{1,0:T(8,128)(2,1)S(1)} %collective-permute-done.11.b_ref, bf16[384,896]{1,0:T(8,128)(2,1)} %collective-permute-done.12.c_ref, bf16[192,896]{1,0:T(8,128)(2,1)S(1)} %copy-done.12), custom_call_target="tpu_custom_call" | custom-call | flops 20000000000 | tf_op jit(solution)/shard_map/pallas_call | solution.py:478
  132.3 5.6 %all-to-all-start.3 = ((bf16[16,24,896]{2,1,0:T(8,128)(2,1)}), bf16[16,24,896]{2,1,0:T(8,128)(2,1)S(1)}, u32[]{:S(2)}, u32[]{:S(2)}) async-start(bf16[16,24,896]{2,1,0:T(8,128)(2,1)} %bitcast.23), calls=%async_computation.3 | async-start | bytes 1376256 | tf_op jit(solution)/shard_map/all_to_all | solution.py:492
  137.9 0.0 copy-start.3
  137.9 2.0 %copy-done.3 = bf16[1,1,512,3584]{3,2,1,0:T(8,128)(2,1)S(1)} copy-done((bf16[1,1,512,3584]{3,2,1,0:T(8,128)(2,1)S(1)}, bf16[1,1,512,3584]{3,2,1,0:T(8,128)(2,1)}, u32[]{:S(2)}) %copy-start.3) | copy-done | bytes 3670040
  140.0 3.9 %shard_map.124 = (bf16[384,896]{1,0:T(8,128)(2,1)S(1)}, bf16[384,896]{1,0:T(8,128)(2,1)S(1)}, bf16[384,896]{1,0:T(8,128)(2,1)S(1)}) custom-call(s32[4]{0:T(128)S(1)} %copy-done.7, bf16[384,512]{1,0:T(8,128)(2,1)S(1)} %copy-done.11, bf16[512,3584]{1,0:T(8,128)(2,1)S(1)} %bitcast.39, bf16[192,896]{1,0:T(8,128)(2,1)} %collective-permute-done.top_ref, ...), custom_call_target="tpu_custom_call" | custom-call | flops 40000000000 | tf_op jit(solution)/shard_map/pallas_call | solution.py:407
  143.9 0.0 copy-start.5
  143.9 1.0 collective-permute-start.2
  144.9 0.5 collective-permute-start.3
  145.4 8.6 %collective-permute-done.2.b_ref = bf16[384,896]{1,0:T(8,128)(2,1)S(1)} collective-permute-done((bf16[384,896]{1,0:T(8,128)(2,1)S(1)}, bf16[384,896]{1,0:T(8,128)(2,1)S(1)}, u32[]{:S(2)}, u32[]{:S(2)}) %collective-permute-start.2) | collective-permute-done | bytes 688160 | tf_op jit(solution)/shard_map/ppermute | solution.py:17
  154.0 2.2 %collective-permute-done.3.c_ref = bf16[384,896]{1,0:T(8,128)(2,1)S(1)} collective-permute-done((bf16[384,896]{1,0:T(8,128)(2,1)S(1)}, bf16[384,896]{1,0:T(8,128)(2,1)S(1)}, u32[]{:S(2)}, u32[]{:S(2)}) %collective-permute-start.3) | collective-permute-done | bytes 688160 | tf_op jit(solution)/shard_map/ppermute | solution.py:17
  156.2 1.1 shard_map.125
  157.4 7.4 %all-to-all-start.1 = ((bf16[16,24,896]{2,1,0:T(8,128)(2,1)}), bf16[16,24,896]{2,1,0:T(8,128)(2,1)S(1)}, u32[]{:S(2)}, u32[]{:S(2)}) async-start(bf16[16,24,896]{2,1,0:T(8,128)(2,1)} %bitcast.11), calls=%async_computation.1 | async-start | bytes 1376256 | tf_op jit(solution)/shard_map/all_to_all | solution.py:492
  164.8 0.5 shard_map.135
  165.3 9.4 %collective-permute-start.13 = (bf16[1,128,896]{2,1,0:T(8,128)(2,1)S(1)}, bf16[1,128,896]{2,1,0:T(8,128)(2,1)S(1)}, u32[]{:S(2)}, u32[]{:S(2)}) collective-permute-start(bf16[1,128,896]{2,1,0:T(8,128)(2,1)S(1)} %bitcast.48), channel_id=1, source_target_pairs={{0,192},{64,0},{128,64},{192,128},{1,193},{65,1},{129,65},{193,129... | collective-permute-start | bytes 688136 | tf_op jit(solution)/shard_map/ppermute | solution.py:17
  174.7 3.5 %all-to-all-done.1 = bf16[16,24,896]{2,1,0:T(8,128)(2,1)S(1)} async-done(((bf16[16,24,896]{2,1,0:T(8,128)(2,1)}), bf16[16,24,896]{2,1,0:T(8,128)(2,1)S(1)}, u32[]{:S(2)}, u32[]{:S(2)}) %all-to-all-start.1) | async-done | bytes 688160 | tf_op jit(solution)/shard_map/all_to_all | solution.py:492
  178.2 1.2 shard_map.126
  179.4 13.0 %collective-permute-start.4 = (bf16[1,128,896]{2,1,0:T(8,128)(2,1)S(1)}, bf16[1,128,896]{2,1,0:T(8,128)(2,1)S(1)}, u32[]{:S(2)}, u32[]{:S(2)}) collective-permute-start(bf16[1,128,896]{2,1,0:T(8,128)(2,1)S(1)} %bitcast.47), channel_id=1, source_target_pairs={{0,64},{64,128},{128,192},{192,0},{1,65},{65,129},{129,193},{193,1... | collective-permute-start | bytes 688136 | tf_op jit(solution)/shard_map/ppermute | solution.py:17
  192.4 3.0 %collective-permute-done.4 = bf16[1,128,896]{2,1,0:T(8,128)(2,1)S(1)} collective-permute-done((bf16[1,128,896]{2,1,0:T(8,128)(2,1)S(1)}, bf16[1,128,896]{2,1,0:T(8,128)(2,1)S(1)}, u32[]{:S(2)}, u32[]{:S(2)}) %collective-permute-start.4) | collective-permute-done | bytes 229408 | tf_op jit(solution)/shard_map/ppermute | solution.py:17
  195.4 0.7 copy.17
  196.1 0.7 copy.18
  (33 shorter events, 0.1 us)
Async XLA Ops:
  0.6 13.7 %copy-start.9 = (s32[1,128,2]{1,2,0:T(2,128)S(1)}, s32[1,128,2]{1,2,0:T(2,128)}, u32[]{:S(2)}) copy-start(s32[1,128,2]{1,2,0:T(2,128)} %param.12) | copy-start | bytes 3076
  0.6 13.7 %copy-start.4 = (bf16[1,128,3584]{2,1,0:T(8,128)(2,1)S(1)}, bf16[1,128,3584]{2,1,0:T(8,128)(2,1)}, u32[]{:S(2)}) copy-start(bf16[1,128,3584]{2,1,0:T(8,128)(2,1)} %param.11) | copy-start | bytes 2752516
  4.2 41.5 %all-to-all-start.2 = ((bf16[16,24,1792]{2,1,0:T(8,128)(2,1)}), bf16[16,24,1792]{2,1,0:T(8,128)(2,1)S(1)}, u32[]{:S(2)}, u32[]{:S(2)}) async-start(bf16[16,24,1792]{2,1,0:T(8,128)(2,1)} %bitcast.54), calls=%async_computation.2 | async-start | bytes 2752512 | tf_op jit(solution)/shard_map/all_to_all | solution.py:492
  45.7 26.8 %collective-permute-start.6 = (bf16[384,1792]{1,0:T(8,128)(2,1)S(1)}, bf16[384,1792]{1,0:T(8,128)(2,1)}, u32[]{:S(2)}, u32[]{:S(2)}) collective-permute-start(bf16[384,1792]{1,0:T(8,128)(2,1)S(1)} %shard_map.128.own), channel_id=1, source_target_pairs={{0,3},{1,0},{2,1},{3,2},{4,7},{5,4},{6,5},{7,6},{8,11},{9,8},{10,9... | collective-permute-start | bytes 4128776 | tf_op jit(solution)/shard_map/ppermute | solution.py:17
  48.1 27.6 %collective-permute-start.5 = (bf16[384,1792]{1,0:T(8,128)(2,1)S(1)}, bf16[384,1792]{1,0:T(8,128)(2,1)}, u32[]{:S(2)}, u32[]{:S(2)}) collective-permute-start(bf16[384,1792]{1,0:T(8,128)(2,1)S(1)} %shard_map.128.own), channel_id=1, source_target_pairs={{0,1},{1,2},{2,3},{3,0},{4,5},{5,6},{6,7},{7,4},{8,9},{9,10},{10,1... | collective-permute-start | bytes 4128776 | tf_op jit(solution)/shard_map/ppermute | solution.py:17
  48.1 7.5 %copy-start.13 = (s32[4]{0:T(128)S(1)}, s32[4]{0:T(128)}, u32[]{:S(2)}) copy-start(s32[4]{0:T(128)} %constant.21.clone) | copy-start | bytes 52
  48.1 70.4 %all-to-all-start = ((bf16[16,24,3584]{2,1,0:T(8,128)(2,1)}), bf16[16,24,3584]{2,1,0:T(8,128)(2,1)}, u32[]{:S(2)}, u32[]{:S(2)}) async-start(bf16[16,24,3584]{2,1,0:T(8,128)(2,1)} %bitcast.6), calls=%async_computation | async-start | bytes 5505024 | tf_op jit(solution)/shard_map/all_to_all | solution.py:492
  55.7 43.6 %copy-start.6 = (s32[4]{0:T(128)}, s32[4]{0:T(128)S(1)}, u32[]{:S(2)}) copy-start(s32[4]{0:T(128)S(1)} %and_select_fusion.order_ref.rank_ref) | copy-start | bytes 52
  77.1 17.5 %collective-permute-start.7 = (bf16[192,1792]{1,0:T(8,128)(2,1)S(1)}, bf16[192,1792]{1,0:T(8,128)(2,1)S(1)}, u32[]{:S(2)}, u32[]{:S(2)}) collective-permute-start(bf16[192,1792]{1,0:T(8,128)(2,1)S(1)} %get-tuple-element.28), channel_id=1, source_target_pairs={{0,1},{1,2},{2,3},{3,0},{4,5},{5,6},{6,7},{7,4},{8,9},{9,10},{10,1... | collective-permute-start | bytes 2064392 | tf_op jit(solution)/shard_map/ppermute | solution.py:17
  77.2 17.4 %collective-permute-start.8 = (bf16[192,1792]{1,0:T(8,128)(2,1)S(1)}, bf16[192,1792]{1,0:T(8,128)(2,1)S(1)}, u32[]{:S(2)}, u32[]{:S(2)}) collective-permute-start(bf16[192,1792]{1,0:T(8,128)(2,1)S(1)} %get-tuple-element.29), channel_id=1, source_target_pairs={{0,3},{1,0},{2,1},{3,2},{4,7},{5,4},{6,5},{7,6},{8,11},{9,8},{10,9... | collective-permute-start | bytes 2064392 | tf_op jit(solution)/shard_map/ppermute | solution.py:17
  79.9 2.0 %copy-start = (bf16[1,1,3584,512]{3,2,1,0:T(8,128)(2,1)S(1)}, bf16[1,1,3584,512]{3,2,1,0:T(8,128)(2,1)}, u32[]{:S(2)}) copy-start(bf16[1,1,3584,512]{3,2,1,0:T(8,128)(2,1)} %param.18) | copy-start | bytes 11010052
  81.9 2.0 %copy-start.1 = (bf16[1,1,3584,512]{3,2,1,0:T(8,128)(2,1)S(1)}, bf16[1,1,3584,512]{3,2,1,0:T(8,128)(2,1)}, u32[]{:S(2)}) copy-start(bf16[1,1,3584,512]{3,2,1,0:T(8,128)(2,1)} %param.19) | copy-start | bytes 11010052
  83.9 2.0 %copy-start.2 = (bf16[1,1,512,3584]{3,2,1,0:T(8,128)(2,1)S(1)}, bf16[1,1,512,3584]{3,2,1,0:T(8,128)(2,1)}, u32[]{:S(2)}) copy-start(bf16[1,1,512,3584]{3,2,1,0:T(8,128)(2,1)} %param.20) | copy-start | bytes 11010052
  97.7 6.6 %collective-permute-start.9 = (bf16[192,896]{1,0:T(8,128)(2,1)S(1)}, bf16[192,896]{1,0:T(8,128)(2,1)S(1)}, u32[]{:S(2)}, u32[]{:S(2)}) collective-permute-start(bf16[192,896]{1,0:T(8,128)(2,1)S(1)} %get-tuple-element.38), channel_id=1, source_target_pairs={{0,3},{1,0},{2,1},{3,2},{4,7},{5,4},{6,5},{7,6},{8,11},{9,8},{10,9... | collective-permute-start | bytes 1032200 | tf_op jit(solution)/shard_map/ppermute | solution.py:17
  97.8 7.8 %collective-permute-start.10 = (bf16[192,896]{1,0:T(8,128)(2,1)S(1)}, bf16[192,896]{1,0:T(8,128)(2,1)S(1)}, u32[]{:S(2)}, u32[]{:S(2)}) collective-permute-start(bf16[192,896]{1,0:T(8,128)(2,1)S(1)} %get-tuple-element.39), channel_id=1, source_target_pairs={{0,1},{1,2},{2,3},{3,0},{4,5},{5,6},{6,7},{7,4},{8,9},{9,10},{10,1... | collective-permute-start | bytes 1032200 | tf_op jit(solution)/shard_map/ppermute | solution.py:17
  106.6 22.5 %collective-permute-start.11 = (bf16[384,896]{1,0:T(8,128)(2,1)}, bf16[384,896]{1,0:T(8,128)(2,1)S(1)}, u32[]{:S(2)}, u32[]{:S(2)}) collective-permute-start(bf16[384,896]{1,0:T(8,128)(2,1)} %get-tuple-element.40), channel_id=1, source_target_pairs={{0,3},{1,0},{2,1},{3,2},{4,7},{5,4},{6,5},{7,6},{8,11},{9,8},{10,9... | collective-permute-start | bytes 2064392 | tf_op jit(solution)/shard_map/ppermute | solution.py:17
  106.6 22.5 %collective-permute-start.12 = (bf16[384,896]{1,0:T(8,128)(2,1)S(1)}, bf16[384,896]{1,0:T(8,128)(2,1)}, u32[]{:S(2)}, u32[]{:S(2)}) collective-permute-start(bf16[384,896]{1,0:T(8,128)(2,1)S(1)} %get-tuple-element.41), channel_id=1, source_target_pairs={{0,1},{1,2},{2,3},{3,0},{4,5},{5,6},{6,7},{7,4},{8,9},{9,10},{10,1... | collective-permute-start | bytes 2064392 | tf_op jit(solution)/shard_map/ppermute | solution.py:17
  125.9 11.9 %collective-permute-start.1 = (bf16[192,896]{1,0:T(8,128)(2,1)}, bf16[192,896]{1,0:T(8,128)(2,1)}, u32[]{:S(2)}, u32[]{:S(2)}) collective-permute-start(bf16[192,896]{1,0:T(8,128)(2,1)} %get-tuple-element.24), channel_id=1, source_target_pairs={{0,1},{1,2},{2,3},{3,0},{4,5},{5,6},{6,7},{7,4},{8,9},{9,10},{10,1... | collective-permute-start | bytes 1032200 | tf_op jit(solution)/shard_map/ppermute | solution.py:17
  126.5 11.5 %collective-permute-start = (bf16[192,896]{1,0:T(8,128)(2,1)}, bf16[192,896]{1,0:T(8,128)(2,1)}, u32[]{:S(2)}, u32[]{:S(2)}) collective-permute-start(bf16[192,896]{1,0:T(8,128)(2,1)} %get-tuple-element.23.refs_0_), channel_id=1, source_target_pairs={{0,3},{1,0},{2,1},{3,2},{4,7},{5,4},{6,5},{7,6},{8,11},{9,8},{10,9... | collective-permute-start | bytes 1032200 | tf_op jit(solution)/shard_map/ppermute | solution.py:17
  129.0 1.0 copy-start.12
  130.0 7.9 %copy-start.7 = (s32[4]{0:T(128)S(1)}, s32[4]{0:T(128)}, u32[]{:S(2)}) copy-start(s32[4]{0:T(128)} %copy-done.6) | copy-start | bytes 52
  130.0 7.9 %copy-start.11 = (bf16[384,512]{1,0:T(8,128)(2,1)S(1)}, bf16[384,512]{1,0:T(8,128)(2,1)}, u32[]{:S(2)}) copy-start(bf16[384,512]{1,0:T(8,128)(2,1)} %get-tuple-element.22.hidden_ref) | copy-start | bytes 1179652
  132.3 25.0 %all-to-all-start.3 = ((bf16[16,24,896]{2,1,0:T(8,128)(2,1)}), bf16[16,24,896]{2,1,0:T(8,128)(2,1)S(1)}, u32[]{:S(2)}, u32[]{:S(2)}) async-start(bf16[16,24,896]{2,1,0:T(8,128)(2,1)} %bitcast.23), calls=%async_computation.3 | async-start | bytes 1376256 | tf_op jit(solution)/shard_map/all_to_all | solution.py:492
  137.9 2.0 %copy-start.3 = (bf16[1,1,512,3584]{3,2,1,0:T(8,128)(2,1)S(1)}, bf16[1,1,512,3584]{3,2,1,0:T(8,128)(2,1)}, u32[]{:S(2)}) copy-start(bf16[1,1,512,3584]{3,2,1,0:T(8,128)(2,1)} %param.20) | copy-start | bytes 11010052
  143.9 20.9 %copy-start.5 = (bf16[1,128,896]{2,1,0:T(8,128)(2,1)S(1)}, bf16[1,128,896]{2,1,0:T(8,128)(2,1)}, u32[]{:S(2)}) copy-start(bf16[1,128,896]{2,1,0:T(8,128)(2,1)} %param.17) | copy-start | bytes 688132
  143.9 20.9 %copy-start.8 = (s32[1,128,2]{1,2,0:T(2,128)S(1)}, s32[1,128,2]{1,2,0:T(2,128)}, u32[]{:S(2)}) copy-start(s32[1,128,2]{1,2,0:T(2,128)} %param.15) | copy-start | bytes 3076
  143.9 10.2 %collective-permute-start.2 = (bf16[384,896]{1,0:T(8,128)(2,1)S(1)}, bf16[384,896]{1,0:T(8,128)(2,1)S(1)}, u32[]{:S(2)}, u32[]{:S(2)}) collective-permute-start(bf16[384,896]{1,0:T(8,128)(2,1)S(1)} %get-tuple-element.26), channel_id=1, source_target_pairs={{0,3},{1,0},{2,1},{3,2},{4,7},{5,4},{6,5},{7,6},{8,11},{9,8},{10,9... | collective-permute-start | bytes 2064392 | tf_op jit(solution)/shard_map/ppermute | solution.py:17
  144.9 11.3 %collective-permute-start.3 = (bf16[384,896]{1,0:T(8,128)(2,1)S(1)}, bf16[384,896]{1,0:T(8,128)(2,1)S(1)}, u32[]{:S(2)}, u32[]{:S(2)}) collective-permute-start(bf16[384,896]{1,0:T(8,128)(2,1)S(1)} %get-tuple-element.27), channel_id=1, source_target_pairs={{0,1},{1,2},{2,3},{3,0},{4,5},{5,6},{6,7},{7,4},{8,9},{9,10},{10,1... | collective-permute-start | bytes 2064392 | tf_op jit(solution)/shard_map/ppermute | solution.py:17
  156.2 22.0 %copy-start.10 = (f32[1,128,2]{1,2,0:T(2,128)S(1)}, f32[1,128,2]{1,2,0:T(2,128)}, u32[]{:S(2)}) copy-start(f32[1,128,2]{1,2,0:T(2,128)} %param.13) | copy-start | bytes 3076
  157.4 20.8 %all-to-all-start.1 = ((bf16[16,24,896]{2,1,0:T(8,128)(2,1)}), bf16[16,24,896]{2,1,0:T(8,128)(2,1)S(1)}, u32[]{:S(2)}, u32[]{:S(2)}) async-start(bf16[16,24,896]{2,1,0:T(8,128)(2,1)} %bitcast.11), calls=%async_computation.1 | async-start | bytes 1376256 | tf_op jit(solution)/shard_map/all_to_all | solution.py:492
  165.3 27.1 %collective-permute-start.13 = (bf16[1,128,896]{2,1,0:T(8,128)(2,1)S(1)}, bf16[1,128,896]{2,1,0:T(8,128)(2,1)S(1)}, u32[]{:S(2)}, u32[]{:S(2)}) collective-permute-start(bf16[1,128,896]{2,1,0:T(8,128)(2,1)S(1)} %bitcast.48), channel_id=1, source_target_pairs={{0,192},{64,0},{128,64},{192,128},{1,193},{65,1},{129,65},{193,129... | collective-permute-start | bytes 688136 | tf_op jit(solution)/shard_map/ppermute | solution.py:17
  179.4 16.0 %collective-permute-start.4 = (bf16[1,128,896]{2,1,0:T(8,128)(2,1)S(1)}, bf16[1,128,896]{2,1,0:T(8,128)(2,1)S(1)}, u32[]{:S(2)}, u32[]{:S(2)}) collective-permute-start(bf16[1,128,896]{2,1,0:T(8,128)(2,1)S(1)} %bitcast.47), channel_id=1, source_target_pairs={{0,64},{64,128},{128,192},{192,0},{1,65},{65,129},{129,193},{193,1... | collective-permute-start | bytes 688136 | tf_op jit(solution)/shard_map/ppermute | solution.py:17

commit v4 on v3

--- a/solution.py
+++ b/solution.py
@@ -381,7 +381,7 @@
     )(order, rows, gate_mat, up_mat, down_mat)
 
 
-def forward_rest_kernel(order_ref, hidden_ref, down_ref, top_ref, bottom_ref, left, right, own):
+def forward_rest_kernel(order_ref, hidden_ref, down_ref, top_ref, bottom_ref, left, right):
     step = pl.program_id(0)
     half = top_ref.shape[0]
     part = dot(hidden_ref[...], down_ref[...])
@@ -396,10 +396,6 @@
         right[:half] = part[:half].astype(BF16)
         right[half:] = (part[half:] + bottom_ref[...].astype(F32)).astype(BF16)
 
-    @pl.when(step == 2)
-    def _():
-        own[...] = part.astype(BF16)
-
 
 def forward_rest(order, hidden, down_mat, halves_in, hint):
     slots, width = hidden.shape
@@ -408,19 +404,42 @@
         forward_rest_kernel,
         grid_spec=pltpu.PrefetchScalarGridSpec(
             num_scalar_prefetch=1,
-            grid=(3,),
+            grid=(2,),
             in_specs=[
                 whole((slots, width)),
-                pl.BlockSpec((width, quarter), lambda i, order: (0, order[(i + 1) % 3])),
+                pl.BlockSpec((width, quarter), lambda i, order: (0, order[i + 1])),
                 whole((half, quarter)),
                 whole((half, quarter)),
             ],
-            out_specs=[whole((slots, quarter))] * 3,
-        ),
-        out_shape=[jax.ShapeDtypeStruct((slots, quarter), BF16)] * 3,
-        compiler_params=params(32),
+            out_specs=[whole((slots, quarter))] * 2,
+        ),
+        out_shape=[jax.ShapeDtypeStruct((slots, quarter), BF16)] * 2,
+        compiler_params=params(60),
         cost_estimate=lasting(hint),
     )(order, hidden, down_mat, *halves_in)
+
+
+def forward_own_kernel(order_ref, hidden_ref, down_ref, out_ref):
+    out_ref[...] = dot(hidden_ref[...], down_ref[...]).astype(BF16)
+
+
+def forward_own(order, hidden, down_mat, quarter):
+    slots, width = hidden.shape
+    return pl.pallas_call(
+        forward_own_kernel,
+        grid_spec=pltpu.PrefetchScalarGridSpec(
+            num_scalar_prefetch=1,
+            grid=(1,),
+            in_specs=[
+                whole((slots, width)),
+                pl.BlockSpec((width, quarter), lambda i, order: (0, order[0])),
+            ],
+            out_specs=whole((slots, quarter)),
+        ),
+        out_shape=jax.ShapeDtypeStruct((slots, quarter), BF16),
+        compiler_params=params(32),
+        cost_estimate=cost(2 * slots * width * quarter, 2 * quarter * (width + slots)),
+    )(order, hidden, down_mat)
 
 
 def backward_rest_kernel(order_ref, d_gate_ref, d_up_ref, gate_ref, up_ref, *out_refs):
@@ -529,7 +548,8 @@
     fwd_far = shifted(top, "dp", -1), shifted(bottom, "dp", 1)
     bwd_back = exchange(summed(bwd_own, bwd_left, bwd_right, 20, (top,)), experts)
 
-    fwd_left, fwd_right, fwd_own = forward_rest(order, hidden, down_mat, fwd_far, 40)
+    fwd_left, fwd_right = forward_rest(order, hidden, down_mat, fwd_far, 40)
+    fwd_own = forward_own(order, hidden, down_mat, quarter)
     fwd_left, fwd_right = shifted(fwd_left, "dp", -1), shifted(fwd_right, "dp", 1)
     fwd_back = exchange(summed(fwd_own, fwd_left, fwd_right, 1), experts)
 

time: 198 us -> 195 us (0.985)
  starting transfers between devices: 65.8 us -> 61.6 us
  waiting for transfers between devices: 79 us -> 81.8 us
  local copies, waits for them, and re-layouts: 10.6 us -> 8.55 us
    ppermute x14, starting transfers between devices: 35.3 us -> 31.2 us  [shifted(): lax.ppermute(array, axis, [(i, (i + by) % count) for i in range(count)])]
    all_to_all x4, waiting for transfers between devices: 42.8 us -> 45.2 us  [exchange(): lax.all_to_all(blocks, 'expert', split_axis=0, concat_axis=0, tiled=True)]
    unnamed x30 -> x32, local copies, waits for them, and re-layouts: 10.6 us -> 8.55 us
where the time goes in v4:
time: 195 us; the launch traced here: 194 us
  waiting for transfers between devices  81.8 us (42%)
  starting transfers between devices  61.6 us (32%)
  Pallas kernels  41.4 us (21%)
  local copies, waits for them, and re-layouts  8.55 us (4%)
    all_to_all x4, waiting for transfers between devices, exchange(): lax.all_to_all(blocks, 'expert', split_axis=0, concat_axis=0, tiled=True)  45.2 us
    ppermute x14, waiting for transfers between devices, shifted(): lax.ppermute(array, axis, [(i, (i + by) % count) for i in range(count)])  36.6 us
    ppermute x14, starting transfers between devices, shifted(): lax.ppermute(array, axis, [(i, (i + by) % count) for i in range(count)])  31.2 us
    all_to_all x4, starting transfers between devices, exchange(): lax.all_to_all(blocks, 'expert', split_axis=0, concat_axis=0, tiled=True)  30.4 us
    unnamed x32, local copies, waits for them, and re-layouts  8.55 us
    pallas_call x1, Pallas kernels, backward_early(): pl.pallas_call(backward_early_kernel, grid_spec=pltpu.PrefetchScalarGridS...  8.16 us
    pallas_call x1, Pallas kernels, forward_hidden(): pl.pallas_call(functools.partial(forward_hidden_kernel, groups), grid_spe...  7.42 us
    pallas_call x1, Pallas kernels, forward_rest(): pl.pallas_call(forward_rest_kernel, grid_spec=pltpu.PrefetchScalarGridSpe...  5.11 us
  transfers between devices with their start and end apart: 18, of which 10 were waited for; matrix products, arithmetic and copies ran while one was open for 0% of the time, Pallas kernels for 19%

profile of v4, /device:TPU:1, one launch (start us, length us, event | category | flops | bytes accessed | tf_op | source)
XLA Modules:
  0.0 194.3 jit_solution(4290515950471640654)
XLA Ops:
  0.6 0.0 copy-start.4
  0.7 3.5 %shard_map.128 = bf16[384,1792]{1,0:T(8,128)(2,1)} custom-call(s32[2,128]{1,0:T(2,128)} %bitcast.49, f32[2,128]{1,0:T(2,128)} %bitcast.56, bf16[128,896]{1,0:T(8,128)(2,1)} %bitcast.45, bf16[128,3584]{1,0:T(8,128)(2,1)} %bitcast.55), custom_call_target="tpu_custom_call" | custom-call | flops 176160768 | bytes 2752512 | tf_op jit(solution)/shard_map/pallas_call | solution.py:115
  4.2 10.1 %all-to-all-start.2 = ((bf16[16,24,1792]{2,1,0:T(8,128)(2,1)}), bf16[16,24,1792]{2,1,0:T(8,128)(2,1)S(1)}, u32[]{:S(2)}, u32[]{:S(2)}) async-start(bf16[16,24,1792]{2,1,0:T(8,128)(2,1)} %bitcast.54), calls=%async_computation.2 | async-start | bytes 2752512 | tf_op jit(solution)/shard_map/all_to_all | solution.py:511
  14.3 2.5 %shard_map.122.refs_1_ = bf16[384,3584]{1,0:T(8,128)(2,1)} custom-call(s32[2,128]{1,0:T(2,128)S(1)} %bitcast.51, bf16[128,3584]{1,0:T(8,128)(2,1)S(1)} %bitcast.42), custom_call_target="tpu_custom_call" | custom-call | flops 352321536 | bytes 5505024 | tf_op jit(solution)/shard_map/pallas_call | solution.py:88
  16.9 28.8 %all-to-all-done.2 = bf16[16,24,1792]{2,1,0:T(8,128)(2,1)S(1)} async-done(((bf16[16,24,1792]{2,1,0:T(8,128)(2,1)}), bf16[16,24,1792]{2,1,0:T(8,128)(2,1)S(1)}, u32[]{:S(2)}, u32[]{:S(2)}) %all-to-all-start.2) | async-done | bytes 1376288 | tf_op jit(solution)/shard_map/all_to_all | solution.py:511
  45.6 2.5 %collective-permute-start.6 = (bf16[384,1792]{1,0:T(8,128)(2,1)S(1)}, bf16[384,1792]{1,0:T(8,128)(2,1)S(1)}, u32[]{:S(2)}, u32[]{:S(2)}) collective-permute-start(bf16[384,1792]{1,0:T(8,128)(2,1)S(1)} %shard_map.129.own), channel_id=1, source_target_pairs={{0,3},{1,0},{2,1},{3,2},{4,7},{5,4},{6,5},{7,6},{8,11},{9,8},{10,9... | collective-permute-start | bytes 4128776 | tf_op jit(solution)/shard_map/ppermute | solution.py:17
  48.1 7.5 %all-to-all-start = ((bf16[16,24,3584]{2,1,0:T(8,128)(2,1)}), bf16[16,24,3584]{2,1,0:T(8,128)(2,1)}, u32[]{:S(2)}, u32[]{:S(2)}) async-start(bf16[16,24,3584]{2,1,0:T(8,128)(2,1)} %bitcast.6), calls=%async_computation | async-start | bytes 5505024 | tf_op jit(solution)/shard_map/all_to_all | solution.py:511
  55.7 16.8 %collective-permute-done.6.bottom_ref.right = bf16[384,1792]{1,0:T(8,128)(2,1)S(1)} collective-permute-done((bf16[384,1792]{1,0:T(8,128)(2,1)S(1)}, bf16[384,1792]{1,0:T(8,128)(2,1)S(1)}, u32[]{:S(2)}, u32[]{:S(2)}) %collective-permute-start.6) | collective-permute-done | bytes 1376288 | tf_op jit(solution)/shard_map/ppermute | solution.py:17
  72.5 3.2 %collective-permute-done.5.top_ref.left = bf16[384,1792]{1,0:T(8,128)(2,1)} collective-permute-done((bf16[384,1792]{1,0:T(8,128)(2,1)S(1)}, bf16[384,1792]{1,0:T(8,128)(2,1)}, u32[]{:S(2)}, u32[]{:S(2)}) %collective-permute-start.5) | collective-permute-done | bytes 1376288 | tf_op jit(solution)/shard_map/ppermute | solution.py:17
  75.7 1.2 shard_map.130
  76.9 0.1 collective-permute-start.7
  77.0 2.7 %collective-permute-start.8 = (bf16[192,1792]{1,0:T(8,128)(2,1)S(1)}, bf16[192,1792]{1,0:T(8,128)(2,1)S(1)}, u32[]{:S(2)}, u32[]{:S(2)}) collective-permute-start(bf16[192,1792]{1,0:T(8,128)(2,1)S(1)} %get-tuple-element.27), channel_id=1, source_target_pairs={{0,3},{1,0},{2,1},{3,2},{4,7},{5,4},{6,5},{7,6},{8,11},{9,8},{10,9... | collective-permute-start | bytes 2064392 | tf_op jit(solution)/shard_map/ppermute | solution.py:17
  79.7 2.0 %copy-done = bf16[1,1,3584,512]{3,2,1,0:T(8,128)(2,1)S(1)} copy-done((bf16[1,1,3584,512]{3,2,1,0:T(8,128)(2,1)S(1)}, bf16[1,1,3584,512]{3,2,1,0:T(8,128)(2,1)}, u32[]{:S(2)}) %copy-start) | copy-done | bytes 3670040
  81.7 2.0 %copy-done.1 = bf16[1,1,3584,512]{3,2,1,0:T(8,128)(2,1)S(1)} copy-done((bf16[1,1,3584,512]{3,2,1,0:T(8,128)(2,1)S(1)}, bf16[1,1,3584,512]{3,2,1,0:T(8,128)(2,1)}, u32[]{:S(2)}) %copy-start.1) | copy-done | bytes 3670040
  83.7 2.0 %copy-done.2 = bf16[1,1,512,3584]{3,2,1,0:T(8,128)(2,1)S(1)} copy-done((bf16[1,1,512,3584]{3,2,1,0:T(8,128)(2,1)S(1)}, bf16[1,1,512,3584]{3,2,1,0:T(8,128)(2,1)}, u32[]{:S(2)}) %copy-start.2) | copy-done | bytes 3670040
  85.8 8.2 %shard_map.131 = (f32[384,512]{1,0:T(8,128)S(1)}, f32[384,512]{1,0:T(8,128)S(1)}, f32[384,512]{1,0:T(8,128)S(1)}) custom-call(s32[4]{0:T(128)S(1)} %and_select_fusion.order_ref.rank_ref, bf16[384,1792]{1,0:T(8,128)(2,1)S(1)} %shard_map.129.own, bf16[384,1792]{1,0:T(8,128)(2,1)} %collective-permute-done.5.top_ref.left, ...), custom_call_target="tpu_custom_call" | custom-call | flops 30000001024 | tf_op jit(solution)/shard_map/pallas_call | solution.py:262
  94.0 3.2 %shard_map.132 = (bf16[384,512]{1,0:T(8,128)(2,1)S(1)}, bf16[384,512]{1,0:T(8,128)(2,1)S(1)}, bf16[192,896]{1,0:T(8,128)(2,1)S(1)}, bf16[192,896]{1,0:T(8,128)(2,1)S(1)}) custom-call(s32[4]{0:T(128)S(1)} %and_select_fusion.order_ref.rank_ref, bf16[192,1792]{1,0:T(8,128)(2,1)S(1)} %collective-permute-done.7.top, ...), custom_call_target="tpu_custom_call" | custom-call | flops 1761607680 | bytes 2752512 | tf_op jit(solution)/shard_map/pallas_call | solution.py:310
  97.1 0.1 collective-permute-start.9
  97.2 1.5 collective-permute-start.10
  98.7 3.9 %shard_map.133 = (bf16[384,896]{1,0:T(8,128)(2,1)S(1)}, bf16[384,896]{1,0:T(8,128)(2,1)S(1)}, bf16[384,896]{1,0:T(8,128)(2,1)S(1)}) custom-call(s32[4]{0:T(128)S(1)} %and_select_fusion.order_ref.rank_ref, bf16[384,512]{1,0:T(8,128)(2,1)S(1)} %get-tuple-element.31.d_gate_ref, bf16[384,512]{1,0:T(8,128)(2,1)S(1)} %get-tuple-element.32.d_up_ref, ...), custom_call_target="tpu_custom_call" | custom-call | flops 2113929216 | bytes 7569408 | tf_op jit(solution)/shard_map/pallas_call | solution.py:459
  102.5 1.2 collective-permute-done.9.top_ref
  103.7 1.3 collective-permute-done.10.bottom_ref
  105.0 0.2 shard_map.134
  105.2 0.1 collective-permute-start.11
  105.3 1.5 collective-permute-start.12
  106.8 11.7 %all-to-all-done = bf16[16,24,3584]{2,1,0:T(8,128)(2,1)} async-done(((bf16[16,24,3584]{2,1,0:T(8,128)(2,1)}), bf16[16,24,3584]{2,1,0:T(8,128)(2,1)}, u32[]{:S(2)}, u32[]{:S(2)}) %all-to-all-start) | async-done | bytes 2752544 | tf_op jit(solution)/shard_map/all_to_all | solution.py:511
  118.5 7.4 %shard_map.123 = (bf16[384,512]{1,0:T(8,128)(2,1)}, bf16[192,896]{1,0:T(8,128)(2,1)}, bf16[192,896]{1,0:T(8,128)(2,1)}) custom-call(s32[4]{0:T(128)} %copy-done.8, bf16[384,3584]{1,0:T(8,128)(2,1)} %bitcast.7.rows_hbm, bf16[3584,512]{1,0:T(8,128)(2,1)} %bitcast.28, bf16[3584,512]{1,0:T(8,128)(2,1)} %bitcast.32, bf16[512,3584]{1,0:T(8,128)(2,1)} %bitcast.36), custom_call_target="tpu_custom_call" | custom-call | flops 3170893824 | bytes 8257536 | tf_op jit(solution)/shard_map/pallas_call | solution.py:361
  125.9 0.5 collective-permute-start.1
  126.5 2.6 %collective-permute-start = (bf16[192,896]{1,0:T(8,128)(2,1)}, bf16[192,896]{1,0:T(8,128)(2,1)}, u32[]{:S(2)}, u32[]{:S(2)}) collective-permute-start(bf16[192,896]{1,0:T(8,128)(2,1)} %get-tuple-element.22.refs_0_), channel_id=1, source_target_pairs={{0,3},{1,0},{2,1},{3,2},{4,7},{5,4},{6,5},{7,6},{8,11},{9,8},{10,9... | collective-permute-start | bytes 1032200 | tf_op jit(solution)/shard_map/ppermute | solution.py:17
  129.0 1.0 copy-done.13
  130.0 1.1 shard_map.135
  131.2 5.2 %all-to-all-start.3 = ((bf16[16,24,896]{2,1,0:T(8,128)(2,1)}), bf16[16,24,896]{2,1,0:T(8,128)(2,1)}, u32[]{:S(2)}, u32[]{:S(2)}) async-start(bf16[16,24,896]{2,1,0:T(8,128)(2,1)} %bitcast.23), calls=%async_computation.3 | async-start | bytes 1376256 | tf_op jit(solution)/shard_map/all_to_all | solution.py:511
  136.4 5.1 %shard_map.125 = (bf16[384,896]{1,0:T(8,128)(2,1)}, bf16[384,896]{1,0:T(8,128)(2,1)}) custom-call(s32[4]{0:T(128)} %copy-done.8, bf16[384,512]{1,0:T(8,128)(2,1)} %get-tuple-element.21.hidden_ref, bf16[512,3584]{1,0:T(8,128)(2,1)} %bitcast.37, bf16[192,896]{1,0:T(8,128)(2,1)} %collective-permute-done.top_ref, bf16[192,896]{1,0:T(8,128)(2,1)} %collective-permute-done.1.bottom_ref), custom_call_target="tpu_custom_call" | custom-call | flops 40000000000 | tf_op jit(solution)/shard_map/pallas_call | solution.py:403
  141.5 1.4 collective-permute-start.2
  142.9 0.1 collective-permute-start.3
  143.0 1.1 shard_map.124.a_ref
  144.2 8.0 %collective-permute-done.2.b_ref = bf16[384,896]{1,0:T(8,128)(2,1)S(1)} collective-permute-done((bf16[384,896]{1,0:T(8,128)(2,1)}, bf16[384,896]{1,0:T(8,128)(2,1)S(1)}, u32[]{:S(2)}, u32[]{:S(2)}) %collective-permute-start.2) | collective-permute-done | bytes 688160 | tf_op jit(solution)/shard_map/ppermute | solution.py:17
  152.2 3.1 %collective-permute-done.3.c_ref = bf16[384,896]{1,0:T(8,128)(2,1)S(1)} collective-permute-done((bf16[384,896]{1,0:T(8,128)(2,1)}, bf16[384,896]{1,0:T(8,128)(2,1)S(1)}, u32[]{:S(2)}, u32[]{:S(2)}) %collective-permute-start.3) | collective-permute-done | bytes 688160 | tf_op jit(solution)/shard_map/ppermute | solution.py:17
  155.3 1.1 shard_map.126
  156.4 7.5 %all-to-all-start.1 = ((bf16[16,24,896]{2,1,0:T(8,128)(2,1)}), bf16[16,24,896]{2,1,0:T(8,128)(2,1)S(1)}, u32[]{:S(2)}, u32[]{:S(2)}) async-start(bf16[16,24,896]{2,1,0:T(8,128)(2,1)} %bitcast.11), calls=%async_computation.1 | async-start | bytes 1376256 | tf_op jit(solution)/shard_map/all_to_all | solution.py:511
  164.0 1.6 shard_map.136
  165.6 7.2 %collective-permute-start.13 = (bf16[1,128,896]{2,1,0:T(8,128)(2,1)S(1)}, bf16[1,128,896]{2,1,0:T(8,128)(2,1)S(1)}, u32[]{:S(2)}, u32[]{:S(2)}) collective-permute-start(bf16[1,128,896]{2,1,0:T(8,128)(2,1)S(1)} %bitcast.48), channel_id=1, source_target_pairs={{0,192},{64,0},{128,64},{192,128},{1,193},{65,1},{129,65},{193,129... | collective-permute-start | bytes 688136 | tf_op jit(solution)/shard_map/ppermute | solution.py:17
  172.8 4.7 %all-to-all-done.1 = bf16[16,24,896]{2,1,0:T(8,128)(2,1)S(1)} async-done(((bf16[16,24,896]{2,1,0:T(8,128)(2,1)}), bf16[16,24,896]{2,1,0:T(8,128)(2,1)S(1)}, u32[]{:S(2)}, u32[]{:S(2)}) %all-to-all-start.1) | async-done | bytes 688160 | tf_op jit(solution)/shard_map/all_to_all | solution.py:511
  177.5 1.2 shard_map.127
  178.7 11.2 %collective-permute-start.4 = (bf16[1,128,896]{2,1,0:T(8,128)(2,1)S(1)}, bf16[1,128,896]{2,1,0:T(8,128)(2,1)S(1)}, u32[]{:S(2)}, u32[]{:S(2)}) collective-permute-start(bf16[1,128,896]{2,1,0:T(8,128)(2,1)S(1)} %bitcast.47), channel_id=1, source_target_pairs={{0,64},{64,128},{128,192},{192,0},{1,65},{65,129},{129,193},{193,1... | collective-permute-start | bytes 688136 | tf_op jit(solution)/shard_map/ppermute | solution.py:17
  189.9 3.0 %collective-permute-done.4 = bf16[1,128,896]{2,1,0:T(8,128)(2,1)S(1)} collective-permute-done((bf16[1,128,896]{2,1,0:T(8,128)(2,1)S(1)}, bf16[1,128,896]{2,1,0:T(8,128)(2,1)S(1)}, u32[]{:S(2)}, u32[]{:S(2)}) %collective-permute-start.4) | collective-permute-done | bytes 229408 | tf_op jit(solution)/shard_map/ppermute | solution.py:17
  192.9 0.7 copy.17
  193.6 0.7 copy.18
  (36 shorter events, 0.1 us)
Async XLA Ops:
  0.6 13.7 %copy-start.11 = (s32[1,128,2]{1,2,0:T(2,128)S(1)}, s32[1,128,2]{1,2,0:T(2,128)}, u32[]{:S(2)}) copy-start(s32[1,128,2]{1,2,0:T(2,128)} %param.12) | copy-start | bytes 3076
  0.6 13.7 %copy-start.4 = (bf16[1,128,3584]{2,1,0:T(8,128)(2,1)S(1)}, bf16[1,128,3584]{2,1,0:T(8,128)(2,1)}, u32[]{:S(2)}) copy-start(bf16[1,128,3584]{2,1,0:T(8,128)(2,1)} %param.11) | copy-start | bytes 2752516
  4.2 41.5 %all-to-all-start.2 = ((bf16[16,24,1792]{2,1,0:T(8,128)(2,1)}), bf16[16,24,1792]{2,1,0:T(8,128)(2,1)S(1)}, u32[]{:S(2)}, u32[]{:S(2)}) async-start(bf16[16,24,1792]{2,1,0:T(8,128)(2,1)} %bitcast.54), calls=%async_computation.2 | async-start | bytes 2752512 | tf_op jit(solution)/shard_map/all_to_all | solution.py:511
  45.6 26.8 %collective-permute-start.6 = (bf16[384,1792]{1,0:T(8,128)(2,1)S(1)}, bf16[384,1792]{1,0:T(8,128)(2,1)S(1)}, u32[]{:S(2)}, u32[]{:S(2)}) collective-permute-start(bf16[384,1792]{1,0:T(8,128)(2,1)S(1)} %shard_map.129.own), channel_id=1, source_target_pairs={{0,3},{1,0},{2,1},{3,2},{4,7},{5,4},{6,5},{7,6},{8,11},{9,8},{10,9... | collective-permute-start | bytes 4128776 | tf_op jit(solution)/shard_map/ppermute | solution.py:17
  48.1 27.6 %collective-permute-start.5 = (bf16[384,1792]{1,0:T(8,128)(2,1)S(1)}, bf16[384,1792]{1,0:T(8,128)(2,1)}, u32[]{:S(2)}, u32[]{:S(2)}) collective-permute-start(bf16[384,1792]{1,0:T(8,128)(2,1)S(1)} %shard_map.129.own), channel_id=1, source_target_pairs={{0,1},{1,2},{2,3},{3,0},{4,5},{5,6},{6,7},{7,4},{8,9},{9,10},{10,1... | collective-permute-start | bytes 4128776 | tf_op jit(solution)/shard_map/ppermute | solution.py:17
  48.1 7.5 %copy-start.14 = (s32[4]{0:T(128)S(1)}, s32[4]{0:T(128)}, u32[]{:S(2)}) copy-start(s32[4]{0:T(128)} %constant.21.clone) | copy-start | bytes 52
  48.1 70.4 %all-to-all-start = ((bf16[16,24,3584]{2,1,0:T(8,128)(2,1)}), bf16[16,24,3584]{2,1,0:T(8,128)(2,1)}, u32[]{:S(2)}, u32[]{:S(2)}) async-start(bf16[16,24,3584]{2,1,0:T(8,128)(2,1)} %bitcast.6), calls=%async_computation | async-start | bytes 5505024 | tf_op jit(solution)/shard_map/all_to_all | solution.py:511
  55.7 43.0 %copy-start.8 = (s32[4]{0:T(128)}, s32[4]{0:T(128)S(1)}, u32[]{:S(2)}) copy-start(s32[4]{0:T(128)S(1)} %and_select_fusion.order_ref.rank_ref) | copy-start | bytes 52
  76.9 17.0 %collective-permute-start.7 = (bf16[192,1792]{1,0:T(8,128)(2,1)S(1)}, bf16[192,1792]{1,0:T(8,128)(2,1)S(1)}, u32[]{:S(2)}, u32[]{:S(2)}) collective-permute-start(bf16[192,1792]{1,0:T(8,128)(2,1)S(1)} %get-tuple-element.26), channel_id=1, source_target_pairs={{0,1},{1,2},{2,3},{3,0},{4,5},{5,6},{6,7},{7,4},{8,9},{9,10},{10,1... | collective-permute-start | bytes 2064392 | tf_op jit(solution)/shard_map/ppermute | solution.py:17
  77.0 17.0 %collective-permute-start.8 = (bf16[192,1792]{1,0:T(8,128)(2,1)S(1)}, bf16[192,1792]{1,0:T(8,128)(2,1)S(1)}, u32[]{:S(2)}, u32[]{:S(2)}) collective-permute-start(bf16[192,1792]{1,0:T(8,128)(2,1)S(1)} %get-tuple-element.27), channel_id=1, source_target_pairs={{0,3},{1,0},{2,1},{3,2},{4,7},{5,4},{6,5},{7,6},{8,11},{9,8},{10,9... | collective-permute-start | bytes 2064392 | tf_op jit(solution)/shard_map/ppermute | solution.py:17
  79.6 2.0 %copy-start = (bf16[1,1,3584,512]{3,2,1,0:T(8,128)(2,1)S(1)}, bf16[1,1,3584,512]{3,2,1,0:T(8,128)(2,1)}, u32[]{:S(2)}) copy-start(bf16[1,1,3584,512]{3,2,1,0:T(8,128)(2,1)} %param.18) | copy-start | bytes 11010052
  81.7 2.0 %copy-start.1 = (bf16[1,1,3584,512]{3,2,1,0:T(8,128)(2,1)S(1)}, bf16[1,1,3584,512]{3,2,1,0:T(8,128)(2,1)}, u32[]{:S(2)}) copy-start(bf16[1,1,3584,512]{3,2,1,0:T(8,128)(2,1)} %param.19) | copy-start | bytes 11010052
  83.7 2.0 %copy-start.2 = (bf16[1,1,512,3584]{3,2,1,0:T(8,128)(2,1)S(1)}, bf16[1,1,512,3584]{3,2,1,0:T(8,128)(2,1)}, u32[]{:S(2)}) copy-start(bf16[1,1,512,3584]{3,2,1,0:T(8,128)(2,1)} %param.20) | copy-start | bytes 11010052
  97.1 6.6 %collective-permute-start.9 = (bf16[192,896]{1,0:T(8,128)(2,1)S(1)}, bf16[192,896]{1,0:T(8,128)(2,1)S(1)}, u32[]{:S(2)}, u32[]{:S(2)}) collective-permute-start(bf16[192,896]{1,0:T(8,128)(2,1)S(1)} %get-tuple-element.36), channel_id=1, source_target_pairs={{0,3},{1,0},{2,1},{3,2},{4,7},{5,4},{6,5},{7,6},{8,11},{9,8},{10,9... | collective-permute-start | bytes 1032200 | tf_op jit(solution)/shard_map/ppermute | solution.py:17
  97.2 7.8 %collective-permute-start.10 = (bf16[192,896]{1,0:T(8,128)(2,1)S(1)}, bf16[192,896]{1,0:T(8,128)(2,1)S(1)}, u32[]{:S(2)}, u32[]{:S(2)}) collective-permute-start(bf16[192,896]{1,0:T(8,128)(2,1)S(1)} %get-tuple-element.37), channel_id=1, source_target_pairs={{0,1},{1,2},{2,3},{3,0},{4,5},{5,6},{6,7},{7,4},{8,9},{9,10},{10,1... | collective-permute-start | bytes 1032200 | tf_op jit(solution)/shard_map/ppermute | solution.py:17
  105.2 23.8 %collective-permute-start.11 = (bf16[384,896]{1,0:T(8,128)(2,1)S(1)}, bf16[384,896]{1,0:T(8,128)(2,1)S(1)}, u32[]{:S(2)}, u32[]{:S(2)}) collective-permute-start(bf16[384,896]{1,0:T(8,128)(2,1)S(1)} %get-tuple-element.38), channel_id=1, source_target_pairs={{0,3},{1,0},{2,1},{3,2},{4,7},{5,4},{6,5},{7,6},{8,11},{9,8},{10,9... | collective-permute-start | bytes 2064392 | tf_op jit(solution)/shard_map/ppermute | solution.py:17
  105.3 23.7 %collective-permute-start.12 = (bf16[384,896]{1,0:T(8,128)(2,1)S(1)}, bf16[384,896]{1,0:T(8,128)(2,1)S(1)}, u32[]{:S(2)}, u32[]{:S(2)}) collective-permute-start(bf16[384,896]{1,0:T(8,128)(2,1)S(1)} %get-tuple-element.39), channel_id=1, source_target_pairs={{0,1},{1,2},{2,3},{3,0},{4,5},{5,6},{6,7},{7,4},{8,9},{9,10},{10,1... | collective-permute-start | bytes 2064392 | tf_op jit(solution)/shard_map/ppermute | solution.py:17
  125.9 10.4 %collective-permute-start.1 = (bf16[192,896]{1,0:T(8,128)(2,1)}, bf16[192,896]{1,0:T(8,128)(2,1)}, u32[]{:S(2)}, u32[]{:S(2)}) collective-permute-start(bf16[192,896]{1,0:T(8,128)(2,1)} %get-tuple-element.23), channel_id=1, source_target_pairs={{0,1},{1,2},{2,3},{3,0},{4,5},{5,6},{6,7},{7,4},{8,9},{9,10},{10,1... | collective-permute-start | bytes 1032200 | tf_op jit(solution)/shard_map/ppermute | solution.py:17
  126.5 9.9 %collective-permute-start = (bf16[192,896]{1,0:T(8,128)(2,1)}, bf16[192,896]{1,0:T(8,128)(2,1)}, u32[]{:S(2)}, u32[]{:S(2)}) collective-permute-start(bf16[192,896]{1,0:T(8,128)(2,1)} %get-tuple-element.22.refs_0_), channel_id=1, source_target_pairs={{0,3},{1,0},{2,1},{3,2},{4,7},{5,4},{6,5},{7,6},{8,11},{9,8},{10,9... | collective-permute-start | bytes 1032200 | tf_op jit(solution)/shard_map/ppermute | solution.py:17
  129.0 1.0 copy-start.13
  131.2 25.2 %all-to-all-start.3 = ((bf16[16,24,896]{2,1,0:T(8,128)(2,1)}), bf16[16,24,896]{2,1,0:T(8,128)(2,1)}, u32[]{:S(2)}, u32[]{:S(2)}) async-start(bf16[16,24,896]{2,1,0:T(8,128)(2,1)} %bitcast.23), calls=%async_computation.3 | async-start | bytes 1376256 | tf_op jit(solution)/shard_map/all_to_all | solution.py:511
  136.4 6.6 %copy-start.3 = (bf16[1,1,512,3584]{3,2,1,0:T(8,128)(2,1)S(1)}, bf16[1,1,512,3584]{3,2,1,0:T(8,128)(2,1)}, u32[]{:S(2)}) copy-start(bf16[1,1,512,3584]{3,2,1,0:T(8,128)(2,1)} %param.20) | copy-start | bytes 11010052
  136.4 6.6 %copy-start.7 = (bf16[384,512]{1,0:T(8,128)(2,1)S(1)}, bf16[384,512]{1,0:T(8,128)(2,1)}, u32[]{:S(2)}) copy-start(bf16[384,512]{1,0:T(8,128)(2,1)} %get-tuple-element.21.hidden_ref) | copy-start | bytes 1179652
  136.4 6.6 %copy-start.9 = (s32[4]{0:T(128)S(1)}, s32[4]{0:T(128)}, u32[]{:S(2)}) copy-start(s32[4]{0:T(128)} %copy-done.8) | copy-start | bytes 52
  141.5 10.6 %collective-permute-start.2 = (bf16[384,896]{1,0:T(8,128)(2,1)}, bf16[384,896]{1,0:T(8,128)(2,1)S(1)}, u32[]{:S(2)}, u32[]{:S(2)}) collective-permute-start(bf16[384,896]{1,0:T(8,128)(2,1)} %get-tuple-element.24), channel_id=1, source_target_pairs={{0,3},{1,0},{2,1},{3,2},{4,7},{5,4},{6,5},{7,6},{8,11},{9,8},{10,9... | collective-permute-start | bytes 2064392 | tf_op jit(solution)/shard_map/ppermute | solution.py:17
  142.9 12.4 %collective-permute-start.3 = (bf16[384,896]{1,0:T(8,128)(2,1)}, bf16[384,896]{1,0:T(8,128)(2,1)S(1)}, u32[]{:S(2)}, u32[]{:S(2)}) collective-permute-start(bf16[384,896]{1,0:T(8,128)(2,1)} %get-tuple-element.25), channel_id=1, source_target_pairs={{0,1},{1,2},{2,3},{3,0},{4,5},{5,6},{6,7},{7,4},{8,9},{9,10},{10,1... | collective-permute-start | bytes 2064392 | tf_op jit(solution)/shard_map/ppermute | solution.py:17
  144.1 19.8 %copy-start.6 = (bf16[1,128,896]{2,1,0:T(8,128)(2,1)S(1)}, bf16[1,128,896]{2,1,0:T(8,128)(2,1)}, u32[]{:S(2)}) copy-start(bf16[1,128,896]{2,1,0:T(8,128)(2,1)} %param.17) | copy-start | bytes 688132
  144.1 19.8 %copy-start.10 = (s32[1,128,2]{1,2,0:T(2,128)S(1)}, s32[1,128,2]{1,2,0:T(2,128)}, u32[]{:S(2)}) copy-start(s32[1,128,2]{1,2,0:T(2,128)} %param.15) | copy-start | bytes 3076
  144.2 33.4 %copy-start.5 = (bf16[1,128,3584]{2,1,0:T(8,128)(2,1)S(1)}, bf16[1,128,3584]{2,1,0:T(8,128)(2,1)}, u32[]{:S(2)}) copy-start(bf16[1,128,3584]{2,1,0:T(8,128)(2,1)} %param.11) | copy-start | bytes 2752516
  144.2 33.4 %copy-start.12 = (f32[1,128,2]{1,2,0:T(2,128)S(1)}, f32[1,128,2]{1,2,0:T(2,128)}, u32[]{:S(2)}) copy-start(f32[1,128,2]{1,2,0:T(2,128)} %param.13) | copy-start | bytes 3076
  156.4 21.1 %all-to-all-start.1 = ((bf16[16,24,896]{2,1,0:T(8,128)(2,1)}), bf16[16,24,896]{2,1,0:T(8,128)(2,1)S(1)}, u32[]{:S(2)}, u32[]{:S(2)}) async-start(bf16[16,24,896]{2,1,0:T(8,128)(2,1)} %bitcast.11), calls=%async_computation.1 | async-start | bytes 1376256 | tf_op jit(solution)/shard_map/all_to_all | solution.py:511
  165.6 24.3 %collective-permute-start.13 = (bf16[1,128,896]{2,1,0:T(8,128)(2,1)S(1)}, bf16[1,128,896]{2,1,0:T(8,128)(2,1)S(1)}, u32[]{:S(2)}, u32[]{:S(2)}) collective-permute-start(bf16[1,128,896]{2,1,0:T(8,128)(2,1)S(1)} %bitcast.48), channel_id=1, source_target_pairs={{0,192},{64,0},{128,64},{192,128},{1,193},{65,1},{129,65},{193,129... | collective-permute-start | bytes 688136 | tf_op jit(solution)/shard_map/ppermute | solution.py:17
  178.7 14.2 %collective-permute-start.4 = (bf16[1,128,896]{2,1,0:T(8,128)(2,1)S(1)}, bf16[1,128,896]{2,1,0:T(8,128)(2,1)S(1)}, u32[]{:S(2)}, u32[]{:S(2)}) collective-permute-start(bf16[1,128,896]{2,1,0:T(8,128)(2,1)S(1)} %bitcast.47), channel_id=1, source_target_pairs={{0,64},{64,128},{128,192},{192,0},{1,65},{65,129},{129,193},{193,1... | collective-permute-start | bytes 688136 | tf_op jit(solution)/shard_map/ppermute | solution.py:17

commit v5 on v4

--- a/solution.py
+++ b/solution.py
@@ -381,42 +381,68 @@
     )(order, rows, gate_mat, up_mat, down_mat)
 
 
-def forward_rest_kernel(order_ref, hidden_ref, down_ref, top_ref, bottom_ref, left, right):
-    step = pl.program_id(0)
-    half = top_ref.shape[0]
-    part = dot(hidden_ref[...], down_ref[...])
-
-    @pl.when(step == 0)
-    def _():
-        left[:half] = (part[:half] + top_ref[...].astype(F32)).astype(BF16)
-        left[half:] = part[half:].astype(BF16)
-
-    @pl.when(step == 1)
-    def _():
-        right[:half] = part[:half].astype(BF16)
-        right[half:] = (part[half:] + bottom_ref[...].astype(F32)).astype(BF16)
-
-
-def forward_rest(order, hidden, down_mat, halves_in, hint):
+def forward_rest_kernel(order_ref, hidden_hbm, down_hbm, top_hbm, bottom_hbm, *refs):
+    outs_hbm, (hidden, downs, far, outs, in_sems, out_sems) = refs[:2], refs[2:]
+    quarter, half = outs.shape[2], far.shape[1]
+
+    def block(i):
+        start = pl.multiple_of(order_ref[i + 1] * quarter, 128)
+        return down_hbm.at[:, pl.ds(start, quarter)]
+
+    first = pltpu.make_async_copy(hidden_hbm, hidden, in_sems.at[0])
+    weights = [pltpu.make_async_copy(block(i), downs.at[i], in_sems.at[1 + i]) for i in range(2)]
+    sides = [
+        pltpu.make_async_copy(ref, far.at[i], in_sems.at[3 + i])
+        for i, ref in enumerate((top_hbm, bottom_hbm))
+    ]
+    sent = [
+        pltpu.make_async_copy(outs.at[i], ref, out_sems.at[i]) for i, ref in enumerate(outs_hbm)
+    ]
+    first.start()
+    weights[0].start()
+    sides[0].start()
+    weights[1].start()
+    sides[1].start()
+    first.wait()
+    for i in range(2):
+        weights[i].wait()
+        part = dot(hidden[...], downs[i])
+        sides[i].wait()
+        if i == 0:
+            outs[0, :half] = (part[:half] + far[0].astype(F32)).astype(BF16)
+            outs[0, half:] = part[half:].astype(BF16)
+        else:
+            outs[1, :half] = part[:half].astype(BF16)
+            outs[1, half:] = (part[half:] + far[1].astype(F32)).astype(BF16)
+        sent[i].start()
+    for copy in sent:
+        copy.wait()
+
+
+def forward_rest(order, hidden, down_mat, relayed, hint):
     slots, width = hidden.shape
-    half, quarter = halves_in[0].shape
+    half, quarter = relayed[0].shape
+    place = pl.BlockSpec(memory_space=pl.ANY)
     return pl.pallas_call(
         forward_rest_kernel,
         grid_spec=pltpu.PrefetchScalarGridSpec(
             num_scalar_prefetch=1,
-            grid=(2,),
-            in_specs=[
-                whole((slots, width)),
-                pl.BlockSpec((width, quarter), lambda i, order: (0, order[i + 1])),
-                whole((half, quarter)),
-                whole((half, quarter)),
+            grid=(1,),
+            in_specs=[place] * 4,
+            out_specs=[place] * 2,
+            scratch_shapes=[
+                pltpu.VMEM((slots, width), BF16),
+                pltpu.VMEM((2, width, quarter), BF16),
+                pltpu.VMEM((2, half, quarter), BF16),
+                pltpu.VMEM((2, slots, quarter), BF16),
+                pltpu.SemaphoreType.DMA((5,)),
+                pltpu.SemaphoreType.DMA((2,)),
             ],
-            out_specs=[whole((slots, quarter))] * 2,
         ),
         out_shape=[jax.ShapeDtypeStruct((slots, quarter), BF16)] * 2,
         compiler_params=params(60),
         cost_estimate=lasting(hint),
-    )(order, hidden, down_mat, *halves_in)
+    )(order, hidden, down_mat, *relayed)
 
 
 def forward_own_kernel(order_ref, hidden_ref, down_ref, out_ref):

time: 195 us -> 195 us (level)
  no operation moved by 1% of the time
where the time goes in v5:
time: 195 us; the launch traced here: 194 us
  waiting for transfers between devices  81.5 us (42%)
  starting transfers between devices  61.8 us (32%)
  Pallas kernels  41 us (21%)
  local copies, waits for them, and re-layouts  8.55 us (4%)
    all_to_all x4, waiting for transfers between devices, exchange(): lax.all_to_all(blocks, 'expert', split_axis=0, concat_axis=0, tiled=True)  45 us
    ppermute x14, waiting for transfers between devices, shifted(): lax.ppermute(array, axis, [(i, (i + by) % count) for i in range(count)])  36.5 us
    ppermute x14, starting transfers between devices, shifted(): lax.ppermute(array, axis, [(i, (i + by) % count) for i in range(count)])  31.5 us
    all_to_all x4, starting transfers between devices, exchange(): lax.all_to_all(blocks, 'expert', split_axis=0, concat_axis=0, tiled=True)  30.3 us
    unnamed x32, local copies, waits for them, and re-layouts  8.55 us
    pallas_call x1, Pallas kernels, backward_early(): pl.pallas_call(backward_early_kernel, grid_spec=pltpu.PrefetchScalarGridS...  8.16 us
    pallas_call x1, Pallas kernels, forward_hidden(): pl.pallas_call(functools.partial(forward_hidden_kernel, groups), grid_spe...  7.42 us
    pallas_call x1, Pallas kernels, forward_rest(): pl.pallas_call(forward_rest_kernel, grid_spec=pltpu.PrefetchScalarGridSpe...  4.73 us
  transfers between devices with their start and end apart: 18, of which 10 were waited for; matrix products, arithmetic and copies ran while one was open for 0% of the time, Pallas kernels for 19%

profile of v5, /device:TPU:1, one launch (start us, length us, event | category | flops | bytes accessed | tf_op | source)
XLA Modules:
  0.0 193.9 jit_solution(6547959238273795256)
XLA Ops:
  0.6 0.0 copy-start.4
  0.7 3.5 %shard_map.128 = bf16[384,1792]{1,0:T(8,128)(2,1)} custom-call(s32[2,128]{1,0:T(2,128)} %bitcast.49, f32[2,128]{1,0:T(2,128)} %bitcast.56, bf16[128,896]{1,0:T(8,128)(2,1)} %bitcast.45, bf16[128,3584]{1,0:T(8,128)(2,1)} %bitcast.55), custom_call_target="tpu_custom_call" | custom-call | flops 176160768 | bytes 2752512 | tf_op jit(solution)/shard_map/pallas_call | solution.py:115
  4.2 10.1 %all-to-all-start.2 = ((bf16[16,24,1792]{2,1,0:T(8,128)(2,1)}), bf16[16,24,1792]{2,1,0:T(8,128)(2,1)S(1)}, u32[]{:S(2)}, u32[]{:S(2)}) async-start(bf16[16,24,1792]{2,1,0:T(8,128)(2,1)} %bitcast.54), calls=%async_computation.2 | async-start | bytes 2752512 | tf_op jit(solution)/shard_map/all_to_all | solution.py:537
  14.3 2.5 %shard_map.122.refs_1_ = bf16[384,3584]{1,0:T(8,128)(2,1)} custom-call(s32[2,128]{1,0:T(2,128)S(1)} %bitcast.51, bf16[128,3584]{1,0:T(8,128)(2,1)S(1)} %bitcast.42), custom_call_target="tpu_custom_call" | custom-call | flops 352321536 | bytes 5505024 | tf_op jit(solution)/shard_map/pallas_call | solution.py:88
  16.9 28.8 %all-to-all-done.2 = bf16[16,24,1792]{2,1,0:T(8,128)(2,1)S(1)} async-done(((bf16[16,24,1792]{2,1,0:T(8,128)(2,1)}), bf16[16,24,1792]{2,1,0:T(8,128)(2,1)S(1)}, u32[]{:S(2)}, u32[]{:S(2)}) %all-to-all-start.2) | async-done | bytes 1376288 | tf_op jit(solution)/shard_map/all_to_all | solution.py:537
  45.6 2.5 %collective-permute-start.6 = (bf16[384,1792]{1,0:T(8,128)(2,1)S(1)}, bf16[384,1792]{1,0:T(8,128)(2,1)S(1)}, u32[]{:S(2)}, u32[]{:S(2)}) collective-permute-start(bf16[384,1792]{1,0:T(8,128)(2,1)S(1)} %shard_map.129.own), channel_id=1, source_target_pairs={{0,3},{1,0},{2,1},{3,2},{4,7},{5,4},{6,5},{7,6},{8,11},{9,8},{10,9... | collective-permute-start | bytes 4128776 | tf_op jit(solution)/shard_map/ppermute | solution.py:17
  48.1 7.5 %all-to-all-start = ((bf16[16,24,3584]{2,1,0:T(8,128)(2,1)}), bf16[16,24,3584]{2,1,0:T(8,128)(2,1)}, u32[]{:S(2)}, u32[]{:S(2)}) async-start(bf16[16,24,3584]{2,1,0:T(8,128)(2,1)} %bitcast.6), calls=%async_computation | async-start | bytes 5505024 | tf_op jit(solution)/shard_map/all_to_all | solution.py:537
  55.7 16.8 %collective-permute-done.6.bottom_ref.right = bf16[384,1792]{1,0:T(8,128)(2,1)S(1)} collective-permute-done((bf16[384,1792]{1,0:T(8,128)(2,1)S(1)}, bf16[384,1792]{1,0:T(8,128)(2,1)S(1)}, u32[]{:S(2)}, u32[]{:S(2)}) %collective-permute-start.6) | collective-permute-done | bytes 1376288 | tf_op jit(solution)/shard_map/ppermute | solution.py:17
  72.5 3.2 %collective-permute-done.5.top_ref.left = bf16[384,1792]{1,0:T(8,128)(2,1)} collective-permute-done((bf16[384,1792]{1,0:T(8,128)(2,1)S(1)}, bf16[384,1792]{1,0:T(8,128)(2,1)}, u32[]{:S(2)}, u32[]{:S(2)}) %collective-permute-start.5) | collective-permute-done | bytes 1376288 | tf_op jit(solution)/shard_map/ppermute | solution.py:17
  75.7 1.2 shard_map.130
  76.9 0.1 collective-permute-start.7
  77.0 2.7 %collective-permute-start.8 = (bf16[192,1792]{1,0:T(8,128)(2,1)S(1)}, bf16[192,1792]{1,0:T(8,128)(2,1)S(1)}, u32[]{:S(2)}, u32[]{:S(2)}) collective-permute-start(bf16[192,1792]{1,0:T(8,128)(2,1)S(1)} %get-tuple-element.27), channel_id=1, source_target_pairs={{0,3},{1,0},{2,1},{3,2},{4,7},{5,4},{6,5},{7,6},{8,11},{9,8},{10,9... | collective-permute-start | bytes 2064392 | tf_op jit(solution)/shard_map/ppermute | solution.py:17
  79.7 2.0 %copy-done = bf16[1,1,3584,512]{3,2,1,0:T(8,128)(2,1)S(1)} copy-done((bf16[1,1,3584,512]{3,2,1,0:T(8,128)(2,1)S(1)}, bf16[1,1,3584,512]{3,2,1,0:T(8,128)(2,1)}, u32[]{:S(2)}) %copy-start) | copy-done | bytes 3670040
  81.7 2.0 %copy-done.1 = bf16[1,1,3584,512]{3,2,1,0:T(8,128)(2,1)S(1)} copy-done((bf16[1,1,3584,512]{3,2,1,0:T(8,128)(2,1)S(1)}, bf16[1,1,3584,512]{3,2,1,0:T(8,128)(2,1)}, u32[]{:S(2)}) %copy-start.1) | copy-done | bytes 3670040
  83.7 2.0 %copy-done.2 = bf16[1,1,512,3584]{3,2,1,0:T(8,128)(2,1)S(1)} copy-done((bf16[1,1,512,3584]{3,2,1,0:T(8,128)(2,1)S(1)}, bf16[1,1,512,3584]{3,2,1,0:T(8,128)(2,1)}, u32[]{:S(2)}) %copy-start.2) | copy-done | bytes 3670040
  85.8 8.2 %shard_map.131 = (f32[384,512]{1,0:T(8,128)S(1)}, f32[384,512]{1,0:T(8,128)S(1)}, f32[384,512]{1,0:T(8,128)S(1)}) custom-call(s32[4]{0:T(128)S(1)} %and_select_fusion.order_ref.rank_ref, bf16[384,1792]{1,0:T(8,128)(2,1)S(1)} %shard_map.129.own, bf16[384,1792]{1,0:T(8,128)(2,1)} %collective-permute-done.5.top_ref.left, ...), custom_call_target="tpu_custom_call" | custom-call | flops 30000001024 | tf_op jit(solution)/shard_map/pallas_call | solution.py:262
  94.0 3.2 %shard_map.132 = (bf16[384,512]{1,0:T(8,128)(2,1)S(1)}, bf16[384,512]{1,0:T(8,128)(2,1)S(1)}, bf16[192,896]{1,0:T(8,128)(2,1)S(1)}, bf16[192,896]{1,0:T(8,128)(2,1)S(1)}) custom-call(s32[4]{0:T(128)S(1)} %and_select_fusion.order_ref.rank_ref, bf16[192,1792]{1,0:T(8,128)(2,1)S(1)} %collective-permute-done.7.top, ...), custom_call_target="tpu_custom_call" | custom-call | flops 1761607680 | bytes 2752512 | tf_op jit(solution)/shard_map/pallas_call | solution.py:310
  97.1 0.1 collective-permute-start.9
  97.2 1.5 collective-permute-start.10
  98.7 3.9 %shard_map.133 = (bf16[384,896]{1,0:T(8,128)(2,1)S(1)}, bf16[384,896]{1,0:T(8,128)(2,1)S(1)}, bf16[384,896]{1,0:T(8,128)(2,1)S(1)}) custom-call(s32[4]{0:T(128)S(1)} %and_select_fusion.order_ref.rank_ref, bf16[384,512]{1,0:T(8,128)(2,1)S(1)} %get-tuple-element.31.d_gate_ref, bf16[384,512]{1,0:T(8,128)(2,1)S(1)} %get-tuple-element.32.d_up_ref, ...), custom_call_target="tpu_custom_call" | custom-call | flops 2113929216 | bytes 7569408 | tf_op jit(solution)/shard_map/pallas_call | solution.py:485
  102.5 1.2 collective-permute-done.9.top_ref
  103.7 1.3 collective-permute-done.10.bottom_ref
  105.0 0.2 shard_map.134
  105.2 0.1 collective-permute-start.11
  105.3 1.5 collective-permute-start.12
  106.8 11.7 %all-to-all-done = bf16[16,24,3584]{2,1,0:T(8,128)(2,1)} async-done(((bf16[16,24,3584]{2,1,0:T(8,128)(2,1)}), bf16[16,24,3584]{2,1,0:T(8,128)(2,1)}, u32[]{:S(2)}, u32[]{:S(2)}) %all-to-all-start) | async-done | bytes 2752544 | tf_op jit(solution)/shard_map/all_to_all | solution.py:537
  118.5 7.4 %shard_map.123 = (bf16[384,512]{1,0:T(8,128)(2,1)}, bf16[192,896]{1,0:T(8,128)(2,1)}, bf16[192,896]{1,0:T(8,128)(2,1)}) custom-call(s32[4]{0:T(128)} %copy-done.8, bf16[384,3584]{1,0:T(8,128)(2,1)} %bitcast.7.rows_hbm, bf16[3584,512]{1,0:T(8,128)(2,1)} %bitcast.28, bf16[3584,512]{1,0:T(8,128)(2,1)} %bitcast.32, bf16[512,3584]{1,0:T(8,128)(2,1)} %bitcast.36), custom_call_target="tpu_custom_call" | custom-call | flops 3170893824 | bytes 8257536 | tf_op jit(solution)/shard_map/pallas_call | solution.py:361
  125.9 0.5 collective-permute-start.1
  126.5 2.6 %collective-permute-start = (bf16[192,896]{1,0:T(8,128)(2,1)}, bf16[192,896]{1,0:T(8,128)(2,1)}, u32[]{:S(2)}, u32[]{:S(2)}) collective-permute-start(bf16[192,896]{1,0:T(8,128)(2,1)} %get-tuple-element.22.refs_0_), channel_id=1, source_target_pairs={{0,3},{1,0},{2,1},{3,2},{4,7},{5,4},{6,5},{7,6},{8,11},{9,8},{10,9... | collective-permute-start | bytes 1032200 | tf_op jit(solution)/shard_map/ppermute | solution.py:17
  129.0 1.0 copy-done.13
  130.0 1.1 shard_map.135
  131.2 5.2 %all-to-all-start.3 = ((bf16[16,24,896]{2,1,0:T(8,128)(2,1)}), bf16[16,24,896]{2,1,0:T(8,128)(2,1)}, u32[]{:S(2)}, u32[]{:S(2)}) async-start(bf16[16,24,896]{2,1,0:T(8,128)(2,1)} %bitcast.23), calls=%async_computation.3 | async-start | bytes 1376256 | tf_op jit(solution)/shard_map/all_to_all | solution.py:537
  136.4 4.7 %shard_map.125 = (bf16[384,896]{1,0:T(8,128)(2,1)}, bf16[384,896]{1,0:T(8,128)(2,1)}) custom-call(s32[4]{0:T(128)} %copy-done.8, bf16[384,512]{1,0:T(8,128)(2,1)} %get-tuple-element.21.hidden_ref.hidden_hbm, bf16[512,3584]{1,0:T(8,128)(2,1)} %bitcast.37, bf16[192,896]{1,0:T(8,128)(2,1)} %collective-permute-done.top_hbm, ...), custom_call_target="tpu_custom_call" | custom-call | flops 40000000000 | tf_op jit(solution)/shard_map/pallas_call | solution.py:426
  141.1 1.5 collective-permute-start.2
  142.6 0.1 collective-permute-start.3
  142.7 1.1 shard_map.124.a_ref
  143.9 8.0 %collective-permute-done.2.b_ref = bf16[384,896]{1,0:T(8,128)(2,1)S(1)} collective-permute-done((bf16[384,896]{1,0:T(8,128)(2,1)}, bf16[384,896]{1,0:T(8,128)(2,1)S(1)}, u32[]{:S(2)}, u32[]{:S(2)}) %collective-permute-start.2) | collective-permute-done | bytes 688160 | tf_op jit(solution)/shard_map/ppermute | solution.py:17
  151.9 3.0 %collective-permute-done.3.c_ref = bf16[384,896]{1,0:T(8,128)(2,1)S(1)} collective-permute-done((bf16[384,896]{1,0:T(8,128)(2,1)}, bf16[384,896]{1,0:T(8,128)(2,1)S(1)}, u32[]{:S(2)}, u32[]{:S(2)}) %collective-permute-start.3) | collective-permute-done | bytes 688160 | tf_op jit(solution)/shard_map/ppermute | solution.py:17
  154.9 1.1 shard_map.126
  156.0 7.5 %all-to-all-start.1 = ((bf16[16,24,896]{2,1,0:T(8,128)(2,1)}), bf16[16,24,896]{2,1,0:T(8,128)(2,1)S(1)}, u32[]{:S(2)}, u32[]{:S(2)}) async-start(bf16[16,24,896]{2,1,0:T(8,128)(2,1)} %bitcast.11), calls=%async_computation.1 | async-start | bytes 1376256 | tf_op jit(solution)/shard_map/all_to_all | solution.py:537
  163.5 1.6 shard_map.136
  165.2 7.4 %collective-permute-start.13 = (bf16[1,128,896]{2,1,0:T(8,128)(2,1)S(1)}, bf16[1,128,896]{2,1,0:T(8,128)(2,1)S(1)}, u32[]{:S(2)}, u32[]{:S(2)}) collective-permute-start(bf16[1,128,896]{2,1,0:T(8,128)(2,1)S(1)} %bitcast.48), channel_id=1, source_target_pairs={{0,192},{64,0},{128,64},{192,128},{1,193},{65,1},{129,65},{193,129... | collective-permute-start | bytes 688136 | tf_op jit(solution)/shard_map/ppermute | solution.py:17
  172.5 4.5 %all-to-all-done.1 = bf16[16,24,896]{2,1,0:T(8,128)(2,1)S(1)} async-done(((bf16[16,24,896]{2,1,0:T(8,128)(2,1)}), bf16[16,24,896]{2,1,0:T(8,128)(2,1)S(1)}, u32[]{:S(2)}, u32[]{:S(2)}) %all-to-all-start.1) | async-done | bytes 688160 | tf_op jit(solution)/shard_map/all_to_all | solution.py:537
  177.1 1.2 shard_map.127
  178.3 11.2 %collective-permute-start.4 = (bf16[1,128,896]{2,1,0:T(8,128)(2,1)S(1)}, bf16[1,128,896]{2,1,0:T(8,128)(2,1)S(1)}, u32[]{:S(2)}, u32[]{:S(2)}) collective-permute-start(bf16[1,128,896]{2,1,0:T(8,128)(2,1)S(1)} %bitcast.47), channel_id=1, source_target_pairs={{0,64},{64,128},{128,192},{192,0},{1,65},{65,129},{129,193},{193,1... | collective-permute-start | bytes 688136 | tf_op jit(solution)/shard_map/ppermute | solution.py:17
  189.5 3.0 %collective-permute-done.4 = bf16[1,128,896]{2,1,0:T(8,128)(2,1)S(1)} collective-permute-done((bf16[1,128,896]{2,1,0:T(8,128)(2,1)S(1)}, bf16[1,128,896]{2,1,0:T(8,128)(2,1)S(1)}, u32[]{:S(2)}, u32[]{:S(2)}) %collective-permute-start.4) | collective-permute-done | bytes 229408 | tf_op jit(solution)/shard_map/ppermute | solution.py:17
  192.5 0.7 copy.17
  193.2 0.7 copy.18
  (36 shorter events, 0.1 us)
Async XLA Ops:
  0.6 13.7 %copy-start.11 = (s32[1,128,2]{1,2,0:T(2,128)S(1)}, s32[1,128,2]{1,2,0:T(2,128)}, u32[]{:S(2)}) copy-start(s32[1,128,2]{1,2,0:T(2,128)} %param.12) | copy-start | bytes 3076
  0.6 13.7 %copy-start.4 = (bf16[1,128,3584]{2,1,0:T(8,128)(2,1)S(1)}, bf16[1,128,3584]{2,1,0:T(8,128)(2,1)}, u32[]{:S(2)}) copy-start(bf16[1,128,3584]{2,1,0:T(8,128)(2,1)} %param.11) | copy-start | bytes 2752516
  4.2 41.5 %all-to-all-start.2 = ((bf16[16,24,1792]{2,1,0:T(8,128)(2,1)}), bf16[16,24,1792]{2,1,0:T(8,128)(2,1)S(1)}, u32[]{:S(2)}, u32[]{:S(2)}) async-start(bf16[16,24,1792]{2,1,0:T(8,128)(2,1)} %bitcast.54), calls=%async_computation.2 | async-start | bytes 2752512 | tf_op jit(solution)/shard_map/all_to_all | solution.py:537
  45.6 26.8 %collective-permute-start.6 = (bf16[384,1792]{1,0:T(8,128)(2,1)S(1)}, bf16[384,1792]{1,0:T(8,128)(2,1)S(1)}, u32[]{:S(2)}, u32[]{:S(2)}) collective-permute-start(bf16[384,1792]{1,0:T(8,128)(2,1)S(1)} %shard_map.129.own), channel_id=1, source_target_pairs={{0,3},{1,0},{2,1},{3,2},{4,7},{5,4},{6,5},{7,6},{8,11},{9,8},{10,9... | collective-permute-start | bytes 4128776 | tf_op jit(solution)/shard_map/ppermute | solution.py:17
  48.1 27.6 %collective-permute-start.5 = (bf16[384,1792]{1,0:T(8,128)(2,1)S(1)}, bf16[384,1792]{1,0:T(8,128)(2,1)}, u32[]{:S(2)}, u32[]{:S(2)}) collective-permute-start(bf16[384,1792]{1,0:T(8,128)(2,1)S(1)} %shard_map.129.own), channel_id=1, source_target_pairs={{0,1},{1,2},{2,3},{3,0},{4,5},{5,6},{6,7},{7,4},{8,9},{9,10},{10,1... | collective-permute-start | bytes 4128776 | tf_op jit(solution)/shard_map/ppermute | solution.py:17
  48.1 7.5 %copy-start.14 = (s32[4]{0:T(128)S(1)}, s32[4]{0:T(128)}, u32[]{:S(2)}) copy-start(s32[4]{0:T(128)} %constant.21.clone) | copy-start | bytes 52
  48.1 70.4 %all-to-all-start = ((bf16[16,24,3584]{2,1,0:T(8,128)(2,1)}), bf16[16,24,3584]{2,1,0:T(8,128)(2,1)}, u32[]{:S(2)}, u32[]{:S(2)}) async-start(bf16[16,24,3584]{2,1,0:T(8,128)(2,1)} %bitcast.6), calls=%async_computation | async-start | bytes 5505024 | tf_op jit(solution)/shard_map/all_to_all | solution.py:537
  55.7 43.0 %copy-start.8 = (s32[4]{0:T(128)}, s32[4]{0:T(128)S(1)}, u32[]{:S(2)}) copy-start(s32[4]{0:T(128)S(1)} %and_select_fusion.order_ref.rank_ref) | copy-start | bytes 52
  76.9 17.0 %collective-permute-start.7 = (bf16[192,1792]{1,0:T(8,128)(2,1)S(1)}, bf16[192,1792]{1,0:T(8,128)(2,1)S(1)}, u32[]{:S(2)}, u32[]{:S(2)}) collective-permute-start(bf16[192,1792]{1,0:T(8,128)(2,1)S(1)} %get-tuple-element.26), channel_id=1, source_target_pairs={{0,1},{1,2},{2,3},{3,0},{4,5},{5,6},{6,7},{7,4},{8,9},{9,10},{10,1... | collective-permute-start | bytes 2064392 | tf_op jit(solution)/shard_map/ppermute | solution.py:17
  77.0 17.0 %collective-permute-start.8 = (bf16[192,1792]{1,0:T(8,128)(2,1)S(1)}, bf16[192,1792]{1,0:T(8,128)(2,1)S(1)}, u32[]{:S(2)}, u32[]{:S(2)}) collective-permute-start(bf16[192,1792]{1,0:T(8,128)(2,1)S(1)} %get-tuple-element.27), channel_id=1, source_target_pairs={{0,3},{1,0},{2,1},{3,2},{4,7},{5,4},{6,5},{7,6},{8,11},{9,8},{10,9... | collective-permute-start | bytes 2064392 | tf_op jit(solution)/shard_map/ppermute | solution.py:17
  79.6 2.0 %copy-start = (bf16[1,1,3584,512]{3,2,1,0:T(8,128)(2,1)S(1)}, bf16[1,1,3584,512]{3,2,1,0:T(8,128)(2,1)}, u32[]{:S(2)}) copy-start(bf16[1,1,3584,512]{3,2,1,0:T(8,128)(2,1)} %param.18) | copy-start | bytes 11010052
  81.7 2.0 %copy-start.1 = (bf16[1,1,3584,512]{3,2,1,0:T(8,128)(2,1)S(1)}, bf16[1,1,3584,512]{3,2,1,0:T(8,128)(2,1)}, u32[]{:S(2)}) copy-start(bf16[1,1,3584,512]{3,2,1,0:T(8,128)(2,1)} %param.19) | copy-start | bytes 11010052
  83.7 2.0 %copy-start.2 = (bf16[1,1,512,3584]{3,2,1,0:T(8,128)(2,1)S(1)}, bf16[1,1,512,3584]{3,2,1,0:T(8,128)(2,1)}, u32[]{:S(2)}) copy-start(bf16[1,1,512,3584]{3,2,1,0:T(8,128)(2,1)} %param.20) | copy-start | bytes 11010052
  97.1 6.6 %collective-permute-start.9 = (bf16[192,896]{1,0:T(8,128)(2,1)S(1)}, bf16[192,896]{1,0:T(8,128)(2,1)S(1)}, u32[]{:S(2)}, u32[]{:S(2)}) collective-permute-start(bf16[192,896]{1,0:T(8,128)(2,1)S(1)} %get-tuple-element.36), channel_id=1, source_target_pairs={{0,3},{1,0},{2,1},{3,2},{4,7},{5,4},{6,5},{7,6},{8,11},{9,8},{10,9... | collective-permute-start | bytes 1032200 | tf_op jit(solution)/shard_map/ppermute | solution.py:17
  97.2 7.8 %collective-permute-start.10 = (bf16[192,896]{1,0:T(8,128)(2,1)S(1)}, bf16[192,896]{1,0:T(8,128)(2,1)S(1)}, u32[]{:S(2)}, u32[]{:S(2)}) collective-permute-start(bf16[192,896]{1,0:T(8,128)(2,1)S(1)} %get-tuple-element.37), channel_id=1, source_target_pairs={{0,1},{1,2},{2,3},{3,0},{4,5},{5,6},{6,7},{7,4},{8,9},{9,10},{10,1... | collective-permute-start | bytes 1032200 | tf_op jit(solution)/shard_map/ppermute | solution.py:17
  105.2 23.8 %collective-permute-start.11 = (bf16[384,896]{1,0:T(8,128)(2,1)S(1)}, bf16[384,896]{1,0:T(8,128)(2,1)S(1)}, u32[]{:S(2)}, u32[]{:S(2)}) collective-permute-start(bf16[384,896]{1,0:T(8,128)(2,1)S(1)} %get-tuple-element.38), channel_id=1, source_target_pairs={{0,3},{1,0},{2,1},{3,2},{4,7},{5,4},{6,5},{7,6},{8,11},{9,8},{10,9... | collective-permute-start | bytes 2064392 | tf_op jit(solution)/shard_map/ppermute | solution.py:17
  105.3 23.7 %collective-permute-start.12 = (bf16[384,896]{1,0:T(8,128)(2,1)S(1)}, bf16[384,896]{1,0:T(8,128)(2,1)S(1)}, u32[]{:S(2)}, u32[]{:S(2)}) collective-permute-start(bf16[384,896]{1,0:T(8,128)(2,1)S(1)} %get-tuple-element.39), channel_id=1, source_target_pairs={{0,1},{1,2},{2,3},{3,0},{4,5},{5,6},{6,7},{7,4},{8,9},{9,10},{10,1... | collective-permute-start | bytes 2064392 | tf_op jit(solution)/shard_map/ppermute | solution.py:17
  125.9 10.4 %collective-permute-start.1 = (bf16[192,896]{1,0:T(8,128)(2,1)}, bf16[192,896]{1,0:T(8,128)(2,1)}, u32[]{:S(2)}, u32[]{:S(2)}) collective-permute-start(bf16[192,896]{1,0:T(8,128)(2,1)} %get-tuple-element.23), channel_id=1, source_target_pairs={{0,1},{1,2},{2,3},{3,0},{4,5},{5,6},{6,7},{7,4},{8,9},{9,10},{10,1... | collective-permute-start | bytes 1032200 | tf_op jit(solution)/shard_map/ppermute | solution.py:17
  126.5 9.9 %collective-permute-start = (bf16[192,896]{1,0:T(8,128)(2,1)}, bf16[192,896]{1,0:T(8,128)(2,1)}, u32[]{:S(2)}, u32[]{:S(2)}) collective-permute-start(bf16[192,896]{1,0:T(8,128)(2,1)} %get-tuple-element.22.refs_0_), channel_id=1, source_target_pairs={{0,3},{1,0},{2,1},{3,2},{4,7},{5,4},{6,5},{7,6},{8,11},{9,8},{10,9... | collective-permute-start | bytes 1032200 | tf_op jit(solution)/shard_map/ppermute | solution.py:17
  129.0 1.0 copy-start.13
  131.2 24.9 %all-to-all-start.3 = ((bf16[16,24,896]{2,1,0:T(8,128)(2,1)}), bf16[16,24,896]{2,1,0:T(8,128)(2,1)}, u32[]{:S(2)}, u32[]{:S(2)}) async-start(bf16[16,24,896]{2,1,0:T(8,128)(2,1)} %bitcast.23), calls=%async_computation.3 | async-start | bytes 1376256 | tf_op jit(solution)/shard_map/all_to_all | solution.py:537
  136.4 6.3 %copy-start.3 = (bf16[1,1,512,3584]{3,2,1,0:T(8,128)(2,1)S(1)}, bf16[1,1,512,3584]{3,2,1,0:T(8,128)(2,1)}, u32[]{:S(2)}) copy-start(bf16[1,1,512,3584]{3,2,1,0:T(8,128)(2,1)} %param.20) | copy-start | bytes 11010052
  136.4 6.3 %copy-start.7 = (bf16[384,512]{1,0:T(8,128)(2,1)S(1)}, bf16[384,512]{1,0:T(8,128)(2,1)}, u32[]{:S(2)}) copy-start(bf16[384,512]{1,0:T(8,128)(2,1)} %get-tuple-element.21.hidden_ref.hidden_hbm) | copy-start | bytes 1179652
  136.4 6.3 %copy-start.9 = (s32[4]{0:T(128)S(1)}, s32[4]{0:T(128)}, u32[]{:S(2)}) copy-start(s32[4]{0:T(128)} %copy-done.8) | copy-start | bytes 52
  141.1 10.7 %collective-permute-start.2 = (bf16[384,896]{1,0:T(8,128)(2,1)}, bf16[384,896]{1,0:T(8,128)(2,1)S(1)}, u32[]{:S(2)}, u32[]{:S(2)}) collective-permute-start(bf16[384,896]{1,0:T(8,128)(2,1)} %get-tuple-element.24), channel_id=1, source_target_pairs={{0,3},{1,0},{2,1},{3,2},{4,7},{5,4},{6,5},{7,6},{8,11},{9,8},{10,9... | collective-permute-start | bytes 2064392 | tf_op jit(solution)/shard_map/ppermute | solution.py:17
  142.6 12.3 %collective-permute-start.3 = (bf16[384,896]{1,0:T(8,128)(2,1)}, bf16[384,896]{1,0:T(8,128)(2,1)S(1)}, u32[]{:S(2)}, u32[]{:S(2)}) collective-permute-start(bf16[384,896]{1,0:T(8,128)(2,1)} %get-tuple-element.25), channel_id=1, source_target_pairs={{0,1},{1,2},{2,3},{3,0},{4,5},{5,6},{6,7},{7,4},{8,9},{9,10},{10,1... | collective-permute-start | bytes 2064392 | tf_op jit(solution)/shard_map/ppermute | solution.py:17
  143.8 19.7 %copy-start.6 = (bf16[1,128,896]{2,1,0:T(8,128)(2,1)S(1)}, bf16[1,128,896]{2,1,0:T(8,128)(2,1)}, u32[]{:S(2)}) copy-start(bf16[1,128,896]{2,1,0:T(8,128)(2,1)} %param.17) | copy-start | bytes 688132
  143.8 19.7 %copy-start.10 = (s32[1,128,2]{1,2,0:T(2,128)S(1)}, s32[1,128,2]{1,2,0:T(2,128)}, u32[]{:S(2)}) copy-start(s32[1,128,2]{1,2,0:T(2,128)} %param.15) | copy-start | bytes 3076
  143.9 33.2 %copy-start.5 = (bf16[1,128,3584]{2,1,0:T(8,128)(2,1)S(1)}, bf16[1,128,3584]{2,1,0:T(8,128)(2,1)}, u32[]{:S(2)}) copy-start(bf16[1,128,3584]{2,1,0:T(8,128)(2,1)} %param.11) | copy-start | bytes 2752516
  143.9 33.2 %copy-start.12 = (f32[1,128,2]{1,2,0:T(2,128)S(1)}, f32[1,128,2]{1,2,0:T(2,128)}, u32[]{:S(2)}) copy-start(f32[1,128,2]{1,2,0:T(2,128)} %param.13) | copy-start | bytes 3076
  156.0 21.0 %all-to-all-start.1 = ((bf16[16,24,896]{2,1,0:T(8,128)(2,1)}), bf16[16,24,896]{2,1,0:T(8,128)(2,1)S(1)}, u32[]{:S(2)}, u32[]{:S(2)}) async-start(bf16[16,24,896]{2,1,0:T(8,128)(2,1)} %bitcast.11), calls=%async_computation.1 | async-start | bytes 1376256 | tf_op jit(solution)/shard_map/all_to_all | solution.py:537
  165.2 24.3 %collective-permute-start.13 = (bf16[1,128,896]{2,1,0:T(8,128)(2,1)S(1)}, bf16[1,128,896]{2,1,0:T(8,128)(2,1)S(1)}, u32[]{:S(2)}, u32[]{:S(2)}) collective-permute-start(bf16[1,128,896]{2,1,0:T(8,128)(2,1)S(1)} %bitcast.48), channel_id=1, source_target_pairs={{0,192},{64,0},{128,64},{192,128},{1,193},{65,1},{129,65},{193,129... | collective-permute-start | bytes 688136 | tf_op jit(solution)/shard_map/ppermute | solution.py:17
  178.3 14.2 %collective-permute-start.4 = (bf16[1,128,896]{2,1,0:T(8,128)(2,1)S(1)}, bf16[1,128,896]{2,1,0:T(8,128)(2,1)S(1)}, u32[]{:S(2)}, u32[]{:S(2)}) collective-permute-start(bf16[1,128,896]{2,1,0:T(8,128)(2,1)S(1)} %bitcast.47), channel_id=1, source_target_pairs={{0,64},{64,128},{128,192},{192,0},{1,65},{65,129},{129,193},{193,1... | collective-permute-start | bytes 688136 | tf_op jit(solution)/shard_map/ppermute | solution.py:17
